TPU v7x, 128 devices: a whole 4x4x4 slice. The times are simulated.
128 devices in a mesh: rows: 16 (over z, y), samp: 8 (over x, core).
Axes of the slice: x: 4, y: 4, z: 4, core: 2. Of those that a mesh axis runs over, the one named last changes fastest.
Arguments:
- temp_slab: bfloat16 [128, 65536], P('samp', 'rows'), may hold values from -6 to 6
- stream_slab: bfloat16 [128, 65536], P('samp', 'rows'), may hold values from -6 to 6
- probe: bfloat16 [512, 65536], P(None, 'rows'), may hold values from -6 to 6
Outputs:
- basis: bfloat16 [512, 65536], P(None, 'rows')
- back_image: float32 [512, 65536], P('samp', 'rows')
All inputs are finite; a program needn't handle non-finite values.
Results may differ from a plain program's by a relative error of at most 0.0049.
Values may be sent and summed in bfloat16 or wider, within the bound.
No kernel may reach another device: no remote copies, remote signals or barrier semaphores. Data moves between devices by JAX's collectives and lax.ppermute only.
A program may use at most 64 MiB of HBM per device.

v0:
```python
import jax
import jax.numpy as jnp
from jax import lax
from jax.sharding import PartitionSpec as P


def inner_rows(left, right):
    return lax.dot_general(
        left, right, (((1,), (1,)), ((), ())), preferred_element_type=jnp.float32
    )


def inner_samples(left, right):
    return lax.dot_general(
        left, right, (((0,), (0,)), ((), ())), preferred_element_type=jnp.float32
    )


def shards(temp_slab, stream_slab, probe):
    local_rows = temp_slab.shape[1]
    total_rows = local_rows * lax.axis_size("rows")
    groups = lax.axis_size("samp")
    samples = temp_slab.shape[0] * groups
    projected = lax.psum(inner_rows(stream_slab, probe), "rows").astype(jnp.bfloat16)
    image = lax.psum(inner_samples(projected, temp_slab), "samp") / (samples - 1.0)
    power = lax.psum(jnp.sum(image * image, axis=1), "rows")
    basis = (image * lax.rsqrt(power / total_rows + 1e-06)[:, None]).astype(jnp.bfloat16)
    scale_back = 1.0 / ((samples - 1.0) * jnp.sqrt(jnp.float32(total_rows)))
    weights = lax.psum(inner_rows(temp_slab, basis), "rows").astype(jnp.bfloat16)
    back_image = (
        lax.psum_scatter(
            inner_samples(weights, stream_slab), "samp", scatter_dimension=0, tiled=True
        )
        * scale_back
    )
    return (basis, back_image)


def solution(mesh):
    return jax.shard_map(
        shards,
        mesh=mesh,
        in_specs=(P("samp", "rows"), P("samp", "rows"), P(None, "rows")),
        out_specs=(P(None, "rows"), P("samp", "rows")),
        check_vma=False,
    )
```

profile of v0, /device:TPU:1, one launch (start us, length us, event | category | flops | bytes accessed | tf_op | source)
XLA Modules:
  0.0 378.1 jit_solution(7391117618999646826)
XLA Ops:
  7.2 0.0 copy-start
  7.2 0.0 all-reduce.2.cloned.1.call-start
  7.2 3.5 fusion.4
  10.7 62.5 %psum.28 = bf16[16,512]{1,0:T(8,128)(2,1)S(1)} all-reduce(f32[16,512]{1,0:T(8,128)S(1)} %fusion.4), channel_id=1, replica_groups=mesh['rows'=16,'samp'=8] {'rows'}, use_global_device_ids=true, to_apply=%region_0.0 | all-reduce | flops 8192 | bytes 49152 | tf_op jit(solution)/shard_map/psum | solution.py:24
  73.2 0.0 copy-done
  73.2 4.5 %fusion.6 = f32[512,4096]{1,0:T(8,128)} fusion(bf16[16,512]{1,0:T(8,128)(2,1)S(1)} %psum.28, bf16[16,4096]{1,0:T(8,128)(2,1)S(1)} %copy-done), kind=kOutput, calls=%fused_computation.11 | convolution fusion | flops 67108864 | bytes 8536064 | tf_op jit(solution)/shard_map/dot_general | solution.py:14
  77.7 0.0 all-reduce.2.cloned.1.call-update
  77.7 0.0 reduce-scatter.2.cloned.1.call-start
  77.8 114.1 %all-reduce.2.cloned.1.call-done = f32[512,4096]{1,0:T(8,128)} async-done(((f32[512,4096]{1,0:T(8,128)}), f32[512,4096]{1,0:T(8,128)}) %all-reduce.2.cloned.1.call-update) | async-done | bytes 8388624 | tf_op jit(solution)/shard_map/psum | solution.py:25
  191.9 4.3 %multiply_reduce_fusion = f32[512]{0:T(512)S(1)} fusion(f32[512,4096]{1,0:T(8,128)} %all-reduce.2.cloned.1.call-done), kind=kLoop, calls=%fused_computation.1 | loop fusion | flops 6290944 | bytes 8390656 | tf_op jit(solution)/shard_map/reduce_sum | solution.py:26
  196.2 33.4 %psum.30 = f32[512]{0:T(512)S(1)} all-reduce(f32[512]{0:T(512)S(1)} %multiply_reduce_fusion), channel_id=1, replica_groups=mesh['rows'=16,'samp'=8] {'rows'}, use_global_device_ids=true, to_apply=%region_3.0 | all-reduce | flops 512 | bytes 4096 | tf_op jit(solution)/shard_map/psum | solution.py:26
  229.6 0.0 copy-start.2
  229.6 4.6 %multiply_convert_fusion = bf16[512,4096]{1,0:T(8,128)(2,1)S(1)} fusion(f32[512,4096]{1,0:T(8,128)} %all-reduce.2.cloned.1.call-done, f32[512]{0:T(512)S(1)} %rsqrt_multiply_fusion), kind=kLoop, calls=%fused_computation | loop fusion | flops 4194304 | bytes 12584960 | tf_op jit(solution)/shard_map/convert_element_type | solution.py:27
  234.2 0.0 copy-start.1
  234.2 2.0 copy-done.1
  236.2 1.2 convolution_bitcast_fusion
  237.5 57.9 %psum.31 = bf16[16,512]{0,1:T(8,128)(2,1)S(1)} all-reduce(f32[16,512]{0,1:T(8,128)S(1)} %convolution_bitcast_fusion), channel_id=1, replica_groups=mesh['rows'=16,'samp'=8] {'rows'}, use_global_device_ids=true, to_apply=%region_4.0 | all-reduce | flops 8192 | bytes 49152 | tf_op jit(solution)/shard_map/psum | solution.py:29
  295.3 0.0 copy-done.2
  295.3 4.4 %fusion.5 = f32[512,4096]{1,0:T(8,128)} fusion(bf16[16,512]{0,1:T(8,128)(2,1)S(1)} %psum.31, bf16[16,4096]{1,0:T(8,128)(2,1)S(1)} %copy-done.2), kind=kOutput, calls=%fused_computation.10 | convolution fusion | flops 67108864 | bytes 8536064 | tf_op jit(solution)/shard_map/dot_general | solution.py:14
  299.8 0.0 reduce-scatter.2.cloned.1.call-update
  299.8 69.2 %reduce-scatter.2.cloned.1.call-done = f32[64,4096]{1,0:T(8,128)} async-done(((f32[512,4096]{1,0:T(8,128)}), f32[64,4096]{1,0:T(8,128)}) %reduce-scatter.2.cloned.1.call-update) | async-done | bytes 1048592 | tf_op jit(solution)/shard_map/reduce_scatter | solution.py:31
  369.0 2.3 broadcast_multiply_fusion
  (1 shorter events, 0.0 us)
Async XLA Ops:
  7.2 66.1 %copy-start = (bf16[16,4096]{1,0:T(8,128)(2,1)S(1)}, bf16[16,4096]{1,0:T(8,128)(2,1)}, u32[]{:S(2)}) copy-start(bf16[16,4096]{1,0:T(8,128)(2,1)} %param.3) | copy-start | bytes 393220
  7.2 184.8 %all-reduce.2.cloned.1.call-start = ((), (), s32[]{:S(2)}) async-start(), calls=%async_computation.1 | async-start | bytes 16777216 | tf_op jit(solution)/shard_map/psum | solution.py:25
  77.7 291.2 %reduce-scatter.2.cloned.1.call-start = ((), (), s32[]{:S(2)}) async-start(), calls=%async_computation.2 | async-start | bytes 9437184 | tf_op jit(solution)/shard_map/reduce_scatter | solution.py:31
  229.6 65.7 %copy-start.2 = (bf16[16,4096]{1,0:T(8,128)(2,1)S(1)}, bf16[16,4096]{1,0:T(8,128)(2,1)}, u32[]{:S(2)}) copy-start(bf16[16,4096]{1,0:T(8,128)(2,1)} %param.4) | copy-start | bytes 393220
  234.2 2.0 copy-start.1
Sparse Core Ops, SparseCore 0:
  77.9 114.0 all-reduce.1
  299.9 69.0 reduce-scatter.1
where the time goes:
time: 378 us
  waiting for transfers between devices  183 us (48%)
  blocking collectives  154 us (41%)
  between operations  14.1 us (4%)
  matrix products  13.6 us (4%)
  other arithmetic  11.2 us (3%)
    psum x1, waiting for transfers between devices, shards(): lax.psum(inner_samples(projected, temp_slab), 'samp') / (samples - 1.0)  114 us
    reduce_scatter x1, waiting for transfers between devices, shards(): lax.psum_scatter(inner_samples(weights, stream_slab), 'samp', scatter_dim...  69.2 us
    psum x1, blocking collectives, shards(): lax.psum(inner_rows(stream_slab, probe), 'rows').astype(jnp.bfloat16)  62.5 us
    psum x1, blocking collectives, shards(): lax.psum(inner_rows(temp_slab, basis), 'rows').astype(jnp.bfloat16)  57.9 us
    psum x1, blocking collectives, shards(): power = lax.psum(jnp.sum(image * image, axis=1), 'rows')  33.4 us
    dot_general x2, matrix products, inner_samples(): lax.dot_general(left, right, (((0,), (0,)), ((), ())), preferred_element_...  8.93 us
  transfers between devices with their start and end apart: 2, of which 2 were waited for; matrix products, arithmetic and copies ran while one was open for 0% of the time, Pallas kernels for 0%

commit v1 on v0

v1 whole, which is shorter than its diff:
```python
import functools

import jax
import jax.numpy as jnp
from jax import lax
from jax.experimental import pallas as pl
from jax.experimental.pallas import tpu as pltpu
from jax.sharding import PartitionSpec as P

F32 = jnp.float32
BF16 = jnp.bfloat16
CORES = 2
HALF_WORK = 1 << 33


def dot(left, right, dims):
    return lax.dot_general(left, right, (dims, ((), ())), preferred_element_type=F32)


def split3(value):
    high = value.astype(BF16)
    rest = value - high.astype(F32)
    mid = rest.astype(BF16)
    return high, mid, (rest - mid.astype(F32)).astype(BF16)


def params(mebibytes):
    return pltpu.CompilerParams(vmem_limit_bytes=mebibytes << 20)


def whole(count):
    return [pl.BlockSpec(memory_space=pltpu.VMEM)] * count


def cost(flops, traffic):
    return pl.CostEstimate(flops=flops, bytes_accessed=traffic, transcendentals=0)


def permute(value, source):
    return lax.ppermute(value, "samp", [(source(n), n) for n in range(lax.axis_size("samp"))])


def chip_step(value, step):
    groups = lax.axis_size("samp")
    return permute(value, lambda n: (n + step * CORES) % groups)


def sibling(value):
    return permute(value, lambda n: n ^ 1)


def around(value, stride, axis="rows"):
    size, span = lax.axis_size(axis), 4 * stride
    steps = [
        [(n // span * span + (n + step * stride) % span, n) for n in range(size)] for step in (1, 3, 2)
    ]
    first, last, opposite = [lax.ppermute(value, axis, pairs) for pairs in steps]
    return [value, first, opposite, last]


def rows_at(place, height):
    return pl.ds(pl.multiple_of(place * height, height), height)


def gram_kernel(part_ref, own_ref, next_ref, half_ref, sibling_ref, message_ref, temp):
    height, columns = part_ref.shape
    chips = temp.shape[0] // height
    span = half_ref.shape[1]
    chip = lax.axis_index("samp") // CORES
    opposite = rows_at(lax.rem(chip + 2, chips), height)
    temp[rows_at(chip, height), :] = own_ref[...]
    temp[rows_at(lax.rem(chip + 1, chips), height), :] = next_ref[...]
    temp[opposite, :] = jnp.zeros(own_ref.shape, BF16)
    temp[opposite, rows_at(chip // 2, span)] = half_ref[...]
    temp[rows_at(lax.rem(chip + 3, chips), height), :] = jnp.zeros(own_ref.shape, BF16)
    mine = jnp.concatenate([own_ref[...], sibling_ref[...]], axis=0)
    gram = dot(mine, temp[...], ((1,), (1,)))
    place = lax.broadcasted_iota(jnp.int32, gram.shape, 1) // height
    gram = jnp.where(place == chip, 0.5 * gram, gram)
    gram = jnp.concatenate([gram[:height], gram[height:]], axis=1)
    message_ref[:, :columns] = part_ref[...]
    message_ref[:, columns:] = gram


def half_kernel(temp_ref, out_ref):
    span = out_ref.shape[1]
    out_ref[...] = temp_ref[:, rows_at(1 - lax.axis_index("samp") // CORES // 2, span)]


def part_kernel(stream_ref, probe_ref, part_ref):
    part_ref[...] = dot(stream_ref[...], probe_ref[...], ((1,), (1,)))


def chip_kernel(temp_ref, temp_sibling_ref, stream_ref, stream_sibling_ref, _, out_ref):
    height = temp_ref.shape[0]
    core = lax.rem(lax.axis_index("samp"), CORES)
    for base, (own, other) in enumerate(((temp_ref, temp_sibling_ref), (stream_ref, stream_sibling_ref))):
        out_ref[rows_at(CORES * base + core, height), :] = own[...]
        out_ref[rows_at(CORES * base + 1 - core, height), :] = other[...]


def copy_kernel(value_ref, _, out_ref):
    out_ref[...] = value_ref[...]


def relay_kernel(both_ref, _, out_ref):
    core = lax.rem(lax.axis_index("samp"), CORES)
    out_ref[...] = both_ref[rows_at(core, out_ref.shape[0]), :]


def order_kernel(chip_ref, beside_ref, beside_sibling_ref, across_ref, across_sibling_ref, out_ref):
    own = lax.axis_index("samp")
    chip, core = own // CORES, lax.rem(own, CORES)
    height = chip_ref.shape[0] // (2 * CORES)
    chips = out_ref.shape[0] // chip_ref.shape[0]

    def put(ref, step, bases):
        place = lax.rem(chip + step, chips)
        for n in range(ref.shape[0] // height):
            base = bases * CORES + n
            out_ref[rows_at(base * chips + place, height), :] = ref[n * height : (n + 1) * height]

    put(chip_ref, 0, 0)
    put(beside_ref, chips - 1 - core * (chips - 2), 0)
    put(beside_sibling_ref, 1 + core * (chips - 2), 0)
    put(across_ref, 2, core)
    put(across_sibling_ref, 2, 1 - core)


def add_kernel(a_ref, b_ref, c_ref, d_ref, out_ref):
    out_ref[...] = (a_ref[...] + b_ref[...]) + (c_ref[...] + d_ref[...])


def sum_kernel(columns, a_ref, b_ref, c_ref, d_ref, message_ref):
    total = (a_ref[...] + b_ref[...]) + (c_ref[...] + d_ref[...])
    pieces = [total[:, :columns].astype(BF16), *split3(total[:, columns:])]
    pieces = jnp.concatenate(pieces, axis=1)
    message_ref[...] = pieces


def collect_kernel(*refs):
    *blocks, out_ref = refs
    height = blocks[0].shape[0]
    chip = lax.axis_index("samp") // CORES
    for step, block in enumerate(blocks):
        out_ref[rows_at(lax.rem(chip + step, len(blocks)), height), :] = block[...]


def output_kernel(columns, scales, *refs):
    near_ref, far_ref, slabs_ref, basis_ref, back_ref, left, gain, weights, message, basis, back, done = refs
    half = near_ref.shape[0]
    samples = CORES * half
    image_scale, back_scale, total_rows = scales
    own = lax.axis_index("samp")
    core = lax.rem(own, CORES)
    message[rows_at(core, half), :] = near_ref[...]
    message[rows_at(1 - core, half), :] = far_ref[...]
    turned = message[:, :columns].astype(F32).T
    left[...] = turned.astype(BF16)
    products = sum(
        message[:, columns + n * samples : columns + (n + 1) * samples].astype(F32) for n in range(3)
    )
    first = lax.broadcasted_iota(jnp.int32, (half, samples), 1) < half
    top = jnp.where(first, products[:half], products[half:])
    bottom = jnp.where(first, products[half:], products[:half])
    bottom = jnp.concatenate([bottom[:, half:], bottom[:, :half]], axis=1)
    gram = jnp.concatenate([top, bottom], axis=0)
    product = sum(dot(left[...], piece, ((1,), (0,))) for piece in split3(gram + gram.T))
    power = jnp.maximum(jnp.sum(product * turned, axis=1, keepdims=True), 0.0)
    power = power * (image_scale * image_scale)
    gain[...] = jnp.broadcast_to(
        image_scale * lax.rsqrt(power / total_rows + 1e-06), gain.shape
    )
    weights[...] = product * gain[...]

    chunks = done.shape[0] - 1
    height = columns // chunks
    copies = []
    for n in range(chunks):
        here = pl.ds(n * height, height)
        image = dot(left[here, :], slabs_ref[:samples, :], ((1,), (0,)))
        scale = jnp.concatenate([gain[here, :]] * (image.shape[1] // samples), axis=1)
        basis[here, :] = (image * scale).astype(BF16)
        copies.append(pltpu.make_async_copy(basis.at[here], basis_ref.at[here], done.at[n]))
        copies[-1].start()
    chosen = weights[rows_at(own, back.shape[0]), :].astype(BF16)
    back[...] = dot(chosen, slabs_ref[samples:, :], ((1,), (0,))) * back_scale
    copies.append(pltpu.make_async_copy(back, back_ref, done.at[chunks]))
    copies[-1].start()
    for copy in copies:
        copy.wait()


def shards(temp_slab, stream_slab, probe):
    height, local_rows = temp_slab.shape
    columns = probe.shape[0]
    groups = lax.axis_size("samp")
    row_groups = lax.axis_size("rows")
    total_rows = local_rows * row_groups
    samples = height * groups
    half = samples // CORES
    wide = columns + samples
    shape = jax.ShapeDtypeStruct

    def call(kernel, name, operands, outs, scratch=(), work=0):
        outs = [shape(*out) for out in outs]
        traffic = sum(value.size * value.dtype.itemsize for value in [*operands, *outs])
        return pl.pallas_call(
            kernel,
            out_shape=tuple(outs),
            in_specs=whole(len(operands)),
            out_specs=tuple(whole(len(outs))),
            scratch_shapes=[pltpu.VMEM(*one) for one in scratch],
            compiler_params=params(16),
            cost_estimate=cost(work, traffic),
            name=name,
        )(*operands)

    packed = columns + 3 * samples
    span = local_rows // 2
    chips = groups // CORES

    (temp_half,) = call(half_kernel, "half", [temp_slab], [((height, span), BF16)], work=HALF_WORK)
    temp_half = chip_step(temp_half, 2)
    temp_next = chip_step(temp_slab, 1)
    temp_sibling = sibling(temp_slab)
    stream_sibling = sibling(stream_slab)
    (part,) = call(
        part_kernel, "part", [stream_slab, probe], [((height, columns), F32)], work=2 * height * columns * local_rows
    )
    (message,) = call(
        gram_kernel,
        "gram",
        [part, temp_slab, temp_next, temp_half, temp_sibling],
        [((height, wide), F32)],
        [((half, local_rows), BF16)],
        4 * height * half * local_rows,
    )
    (chip,) = call(
        chip_kernel,
        "chip",
        [temp_slab, temp_sibling, stream_slab, stream_sibling, message],
        [((4 * height, local_rows), BF16)],
    )
    beside = permute(chip, lambda n: (n - CORES if n % CORES == 0 else n + CORES) % groups)
    (message,) = call(add_kernel, "add", around(message, 1), [((height, wide), F32)])
    (across,) = call(relay_kernel, "relay", [beside, message], [((2 * height, local_rows), BF16)])
    across = permute(across, lambda n: (n - CORES if n % CORES == 0 else n + CORES) % groups)
    beside_sibling = sibling(beside)
    (message,) = call(
        functools.partial(sum_kernel, columns), "total", around(message, 4), [((height, packed), BF16)]
    )
    (later,) = call(copy_kernel, "later", [across, message], [((2 * height, local_rows), BF16)])
    across_sibling = sibling(later)
    (slabs,) = call(
        order_kernel,
        "order",
        [chip, beside, beside_sibling, across, across_sibling],
        [((2 * samples, local_rows), BF16)],
    )
    (message,) = call(collect_kernel, "collect", around(message, CORES, "samp"), [((half, packed), BF16)])
    message_other = sibling(message)

    scales = (
        1.0 / (samples - 1.0),
        1.0 / ((samples - 1.0) * float(total_rows) ** 0.5),
        float(total_rows),
    )
    mine = columns // groups
    chunks = 4
    outs = (shape((columns, local_rows), BF16), shape((mine, local_rows), F32))
    basis, back_image = pl.pallas_call(
        functools.partial(output_kernel, columns, scales),
        out_shape=outs,
        in_specs=whole(3),
        out_specs=tuple([pl.BlockSpec(memory_space=pl.ANY)] * 2),
        scratch_shapes=[
            pltpu.VMEM((columns, samples), BF16),
            pltpu.VMEM((columns, samples), F32),
            pltpu.VMEM((columns, samples), F32),
            pltpu.VMEM((samples, packed), BF16),
            *[pltpu.VMEM(out.shape, out.dtype) for out in outs],
            pltpu.SemaphoreType.DMA((chunks + 1,)),
        ],
        compiler_params=params(40),
        cost_estimate=cost(2 * (columns + mine) * samples * local_rows, 7 << 20),
        name="outputs",
    )(message, message_other, slabs)
    return (basis, back_image)


def solution(mesh):
    return jax.shard_map(
        shards,
        mesh=mesh,
        in_specs=(P("samp", "rows"), P("samp", "rows"), P(None, "rows")),
        out_specs=(P(None, "rows"), P("samp", "rows")),
        check_vma=False,
    )
```

time: 378 us -> 45.8 us (0.12)
  waiting for transfers between devices: 183 us -> 10.7 us
  blocking collectives: 154 us -> 0 us
  starting transfers between devices: 0.08 us -> 28.2 us
  matrix products: 13.6 us -> 0 us
  between operations: 14.1 us -> 0.73 us
  other arithmetic: 11.2 us -> 0 us
  Pallas kernels: 0 us -> 5.09 us
    psum x3 -> x0, blocking collectives: 154 us -> none  [the longest x1 62.5 us: shards(): lax.psum(inner_rows(stream_slab, probe), 'rows').astype(jnp.bfloat16)]
    psum x1 -> x0, waiting for transfers between devices: 114 us -> none  [shards(): lax.psum(inner_samples(projected, temp_slab), 'samp') / (samples - 1.0)]
    reduce_scatter x1 -> x0, waiting for transfers between devices: 69.2 us -> none  [shards(): lax.psum_scatter(inner_samples(weights, stream_slab), 'samp', scatter_dim...]
    ppermute x0 -> x18, starting transfers between devices: none -> 28.2 us  [the longest x9 15.1 us: around(): lax.ppermute(value, axis, pairs)]
    dot_general x4 -> x0, matrix products: 13.6 us -> none  [the longest x2 8.93 us: inner_samples(): lax.dot_general(left, right, (((0,), (0,)), ((), ())), preferred_element_...]
    ppermute x0 -> x18, waiting for transfers between devices: none -> 10.7 us  [the longest x9 6.58 us: around(): lax.ppermute(value, axis, pairs)]
    pallas_call x0 -> x11, Pallas kernels: none -> 5.09 us  [the longest x1 3.21 us: shards(): pl.pallas_call(functools.partial(output_kernel, columns, scales), out_sha...]
    convert_element_type x1 -> x0, other arithmetic: 4.61 us -> none  [shards(): (image * lax.rsqrt(power / total_rows + 1e-06)[:, None]).astype(jnp.bfloa...]
  transfers between devices with their start and end apart: 2 -> 18, of which waited for: 2 -> 8; matrix products, arithmetic and copies ran while one was open for 0% -> 0% of each run, Pallas kernels for 0% -> 4%
where the time goes in v1:
time: 45.8 us; the launch traced here: 45.7 us
  starting transfers between devices  28.2 us (62%)
  waiting for transfers between devices  10.7 us (23%)
  Pallas kernels  5.09 us (11%)
  local copies, waits for them, and re-layouts  0.92 us (2%)
  between operations  0.73 us (2%)
    ppermute x9, starting transfers between devices, around(): lax.ppermute(value, axis, pairs)  15.1 us
    ppermute x9, starting transfers between devices, permute(): lax.ppermute(value, 'samp', [(source(n), n) for n in range(lax.axis_size(...  13.1 us
    ppermute x9, waiting for transfers between devices, around(): lax.ppermute(value, axis, pairs)  6.58 us
    ppermute x9, waiting for transfers between devices, permute(): lax.ppermute(value, 'samp', [(source(n), n) for n in range(lax.axis_size(...  4.16 us
    pallas_call x1, Pallas kernels, shards(): pl.pallas_call(functools.partial(output_kernel, columns, scales), out_sha...  3.21 us
    pallas_call x10, Pallas kernels, call(): pl.pallas_call(kernel, out_shape=tuple(outs), in_specs=whole(len(operands...  1.88 us
  transfers between devices with their start and end apart: 18, of which 8 were waited for; matrix products, arithmetic and copies ran while one was open for 0% of the time, Pallas kernels for 4%

profile of v1, /device:TPU:1, one launch (start us, length us, event | category | flops | bytes accessed | tf_op | source)
XLA Modules:
  0.0 45.7 jit_solution(17381084295575046721)
XLA Ops:
  0.6 0.0 copy-start.1
  0.6 0.0 copy-start
  0.6 1.5 %collective-permute-start.2 = (bf16[16,4096]{1,0:T(8,128)(2,1)}, bf16[16,4096]{1,0:T(8,128)(2,1)S(1)}, u32[]{:S(2)}, u32[]{:S(2)}) collective-permute-start(bf16[16,4096]{1,0:T(8,128)(2,1)} %temp_ref.3), channel_id=1, source_target_pairs={{1,0},{0,1},{3,2},{2,3},{5,4},{4,5},{7,6},{6,7},{9,8},{8,9},{11,10... | collective-permute-start | bytes 393224 | tf_op jit(solution)/shard_map/ppermute | solution.py:40
  2.2 2.6 %collective-permute-start = (bf16[16,4096]{1,0:T(8,128)(2,1)}, bf16[16,4096]{1,0:T(8,128)(2,1)S(1)}, u32[]{:S(2)}, u32[]{:S(2)}) collective-permute-start(bf16[16,4096]{1,0:T(8,128)(2,1)} %temp_ref.3), channel_id=1, source_target_pairs={{2,0},{3,1},{4,2},{5,3},{6,4},{7,5},{0,6},{1,7},{10,8},{11,9},{12,... | collective-permute-start | bytes 393224 | tf_op jit(solution)/shard_map/ppermute | solution.py:40
  4.7 0.3 collective-permute-start.13
  5.1 0.9 %copy-done.2 = bf16[16,4096]{1,0:T(8,128)(2,1)S(1)} copy-done((bf16[16,4096]{1,0:T(8,128)(2,1)S(1)}, bf16[16,4096]{1,0:T(8,128)(2,1)}, u32[]{:S(2)}) %copy-start.2) | copy-done | bytes 131096
  6.0 0.0 copy-start.3
  6.0 0.6 %collective-permute-start.1 = (bf16[16,2048]{1,0:T(8,128)(2,1)S(1)}, bf16[16,2048]{1,0:T(8,128)(2,1)S(1)}, u32[]{:S(2)}, u32[]{:S(2)}) collective-permute-start(bf16[16,2048]{1,0:T(8,128)(2,1)S(1)} %half.1), channel_id=1, source_target_pairs={{4,0},{5,1},{6,2},{7,3},{0,4},{1,5},{2,6},{3,7},{12,8},{13,9},{14,... | collective-permute-start | bytes 196616 | tf_op jit(solution)/shard_map/ppermute | solution.py:40
  6.6 0.0 copy-done.1
  6.6 0.0 copy-done
  6.6 1.2 %part.1.part_ref = f32[16,512]{1,0:T(8,128)S(1)} custom-call(bf16[16,4096]{1,0:T(8,128)(2,1)S(1)} %copy-done.1, bf16[512,4096]{1,0:T(8,128)(2,1)S(1)} %copy-done), custom_call_target="tpu_custom_call" | custom-call | flops 67108864 | bytes 4358144 | tf_op jit(solution)/shard_map/part/pallas_call | solution.py:208
  7.8 3.3 %collective-permute-done.1.half_ref = bf16[16,2048]{1,0:T(8,128)(2,1)S(1)} collective-permute-done((bf16[16,2048]{1,0:T(8,128)(2,1)S(1)}, bf16[16,2048]{1,0:T(8,128)(2,1)S(1)}, u32[]{:S(2)}, u32[]{:S(2)}) %collective-permute-start.1) | collective-permute-done | bytes 65568 | tf_op jit(solution)/shard_map/ppermute | solution.py:40
  11.1 0.0 collective-permute-done.2.sibling_ref.temp_sibling_ref
  11.1 0.0 collective-permute-done.next_ref
  11.1 0.0 copy-done.3
  11.1 0.4 gram.1.a_ref._
  11.5 0.0 collective-permute-done.13.stream_sibling_ref
  11.5 0.1 chip.1.chip_ref
  11.6 1.5 %collective-permute-start.14 = (bf16[64,4096]{1,0:T(8,128)(2,1)S(1)}, bf16[64,4096]{1,0:T(8,128)(2,1)S(1)}, u32[]{:S(2)}, u32[]{:S(2)}) collective-permute-start(bf16[64,4096]{1,0:T(8,128)(2,1)S(1)} %chip.1.chip_ref), channel_id=1, source_target_pairs={{6,0},{3,1},{0,2},{5,3},{2,4},{7,5},{4,6},{1,7},{14,8},{11,9},{8,1... | collective-permute-start | bytes 1572872 | tf_op jit(solution)/shard_map/ppermute | solution.py:40
  13.1 1.3 %collective-permute-start.5 = (f32[16,640]{1,0:T(8,128)S(1)}, f32[16,640]{1,0:T(8,128)S(1)}, u32[]{:S(2)}, u32[]{:S(2)}) collective-permute-start(f32[16,640]{1,0:T(8,128)S(1)} %gram.1.a_ref._), channel_id=1, source_target_pairs={{24,0},{0,8},{8,16},{16,24},{56,32},{32,40},{40,48},{48,56},{88,64... | collective-permute-start | bytes 122888 | tf_op jit(solution)/shard_map/ppermute | solution.py:57
  14.4 2.6 %collective-permute-start.4 = (f32[16,640]{1,0:T(8,128)S(1)}, f32[16,640]{1,0:T(8,128)S(1)}, u32[]{:S(2)}, u32[]{:S(2)}) collective-permute-start(f32[16,640]{1,0:T(8,128)S(1)} %gram.1.a_ref._), channel_id=1, source_target_pairs={{16,0},{24,8},{0,16},{8,24},{48,32},{56,40},{32,48},{40,56},{80,64... | collective-permute-start | bytes 122888 | tf_op jit(solution)/shard_map/ppermute | solution.py:57
  17.0 1.1 %collective-permute-start.3 = (f32[16,640]{1,0:T(8,128)S(1)}, f32[16,640]{1,0:T(8,128)S(1)}, u32[]{:S(2)}, u32[]{:S(2)}) collective-permute-start(f32[16,640]{1,0:T(8,128)S(1)} %gram.1.a_ref._), channel_id=1, source_target_pairs={{8,0},{16,8},{24,16},{0,24},{40,32},{48,40},{56,48},{32,56},{72,64... | collective-permute-start | bytes 122888 | tf_op jit(solution)/shard_map/ppermute | solution.py:57
  18.1 0.0 collective-permute-done.5.d_ref
  18.1 1.9 %collective-permute-done.4.c_ref = f32[16,640]{1,0:T(8,128)S(1)} collective-permute-done((f32[16,640]{1,0:T(8,128)S(1)}, f32[16,640]{1,0:T(8,128)S(1)}, u32[]{:S(2)}, u32[]{:S(2)}) %collective-permute-start.4) | collective-permute-done | bytes 40992 | tf_op jit(solution)/shard_map/ppermute | solution.py:57
  20.0 0.2 collective-permute-done.3.b_ref
  20.2 0.0 collective-permute-done.14.both_ref.beside_ref
  20.3 2.2 %collective-permute-start.16 = (bf16[32,4096]{1,0:T(8,128)(2,1)S(1)}, bf16[32,4096]{1,0:T(8,128)(2,1)S(1)}, u32[]{:S(2)}, u32[]{:S(2)}) collective-permute-start(bf16[32,4096]{1,0:T(8,128)(2,1)S(1)} %relay.1), channel_id=1, source_target_pairs={{6,0},{3,1},{0,2},{5,3},{2,4},{7,5},{4,6},{1,7},{14,8},{11,9},{8,1... | collective-permute-start | bytes 786440 | tf_op jit(solution)/shard_map/ppermute | solution.py:40
  22.5 0.7 %collective-permute-start.15 = (bf16[64,4096]{1,0:T(8,128)(2,1)S(1)}, bf16[64,4096]{1,0:T(8,128)(2,1)S(1)}, u32[]{:S(2)}, u32[]{:S(2)}) collective-permute-start(bf16[64,4096]{1,0:T(8,128)(2,1)S(1)} %collective-permute-done.14.both_ref.beside_ref), channel_id=1, source_target_pairs={{1,0},{0,1},{3,2},{2,3},{5,4},{4,5},{7,6},{6,7},{9,8},{8,9},{11,10... | collective-permute-start | bytes 1572872 | tf_op jit(solution)/shard_map/ppermute | solution.py:40
  23.2 1.7 %collective-permute-start.8 = (f32[16,640]{1,0:T(8,128)S(1)}, f32[16,640]{1,0:T(8,128)S(1)}, u32[]{:S(2)}, u32[]{:S(2)}) collective-permute-start(f32[16,640]{1,0:T(8,128)S(1)} %add.1.a_ref._), channel_id=1, source_target_pairs={{96,0},{104,8},{112,16},{120,24},{0,32},{8,40},{16,48},{24,56},{32... | collective-permute-start | bytes 122888 | tf_op jit(solution)/shard_map/ppermute | solution.py:57
  24.8 3.3 %collective-permute-start.7 = (f32[16,640]{1,0:T(8,128)S(1)}, f32[16,640]{1,0:T(8,128)S(1)}, u32[]{:S(2)}, u32[]{:S(2)}) collective-permute-start(f32[16,640]{1,0:T(8,128)S(1)} %add.1.a_ref._), channel_id=1, source_target_pairs={{64,0},{72,8},{80,16},{88,24},{96,32},{104,40},{112,48},{120,56},{... | collective-permute-start | bytes 122888 | tf_op jit(solution)/shard_map/ppermute | solution.py:57
  28.1 0.7 %collective-permute-start.6 = (f32[16,640]{1,0:T(8,128)S(1)}, f32[16,640]{1,0:T(8,128)S(1)}, u32[]{:S(2)}, u32[]{:S(2)}) collective-permute-start(f32[16,640]{1,0:T(8,128)S(1)} %add.1.a_ref._), channel_id=1, source_target_pairs={{32,0},{40,8},{48,16},{56,24},{64,32},{72,40},{80,48},{88,56},{96,... | collective-permute-start | bytes 122888 | tf_op jit(solution)/shard_map/ppermute | solution.py:57
  28.9 0.0 collective-permute-done.8.d_ref
  28.9 1.5 %collective-permute-done.7.c_ref = f32[16,640]{1,0:T(8,128)S(1)} collective-permute-done((f32[16,640]{1,0:T(8,128)S(1)}, f32[16,640]{1,0:T(8,128)S(1)}, u32[]{:S(2)}, u32[]{:S(2)}) %collective-permute-start.7) | collective-permute-done | bytes 40992 | tf_op jit(solution)/shard_map/ppermute | solution.py:57
  30.4 0.8 %collective-permute-done.6.b_ref = f32[16,640]{1,0:T(8,128)S(1)} collective-permute-done((f32[16,640]{1,0:T(8,128)S(1)}, f32[16,640]{1,0:T(8,128)S(1)}, u32[]{:S(2)}, u32[]{:S(2)}) %collective-permute-start.6) | collective-permute-done | bytes 40992 | tf_op jit(solution)/shard_map/ppermute | solution.py:57
  31.2 0.0 collective-permute-done.16.value_ref.across_ref
  31.2 1.7 %collective-permute-start.17 = (bf16[32,4096]{1,0:T(8,128)(2,1)S(1)}, bf16[32,4096]{1,0:T(8,128)(2,1)S(1)}, u32[]{:S(2)}, u32[]{:S(2)}) collective-permute-start(bf16[32,4096]{1,0:T(8,128)(2,1)S(1)} %later.1), channel_id=1, source_target_pairs={{1,0},{0,1},{3,2},{2,3},{5,4},{4,5},{7,6},{6,7},{9,8},{8,9},{11,10... | collective-permute-start | bytes 786440 | tf_op jit(solution)/shard_map/ppermute | solution.py:40
  32.9 0.8 %collective-permute-start.11 = (bf16[16,896]{1,0:T(8,128)(2,1)S(1)}, bf16[16,896]{1,0:T(8,128)(2,1)S(1)}, u32[]{:S(2)}, u32[]{:S(2)}) collective-permute-start(bf16[16,896]{1,0:T(8,128)(2,1)S(1)} %total.1.refs_0_._), channel_id=1, source_target_pairs={{6,0},{7,1},{0,2},{1,3},{2,4},{3,5},{4,6},{5,7},{14,8},{15,9},{8,1... | collective-permute-start | bytes 86024 | tf_op jit(solution)/shard_map/ppermute | solution.py:57
  33.7 3.2 %collective-permute-start.10 = (bf16[16,896]{1,0:T(8,128)(2,1)S(1)}, bf16[16,896]{1,0:T(8,128)(2,1)S(1)}, u32[]{:S(2)}, u32[]{:S(2)}) collective-permute-start(bf16[16,896]{1,0:T(8,128)(2,1)S(1)} %total.1.refs_0_._), channel_id=1, source_target_pairs={{4,0},{5,1},{6,2},{7,3},{0,4},{1,5},{2,6},{3,7},{12,8},{13,9},{14,... | collective-permute-start | bytes 86024 | tf_op jit(solution)/shard_map/ppermute | solution.py:57
  36.9 0.5 %collective-permute-start.9 = (bf16[16,896]{1,0:T(8,128)(2,1)S(1)}, bf16[16,896]{1,0:T(8,128)(2,1)S(1)}, u32[]{:S(2)}, u32[]{:S(2)}) collective-permute-start(bf16[16,896]{1,0:T(8,128)(2,1)S(1)} %total.1.refs_0_._), channel_id=1, source_target_pairs={{2,0},{3,1},{4,2},{5,3},{6,4},{7,5},{0,6},{1,7},{10,8},{11,9},{12,... | collective-permute-start | bytes 86024 | tf_op jit(solution)/shard_map/ppermute | solution.py:57
  37.4 0.0 collective-permute-done.11.refs_3_
  37.4 1.2 %collective-permute-done.10.refs_2_ = bf16[16,896]{1,0:T(8,128)(2,1)S(1)} collective-permute-done((bf16[16,896]{1,0:T(8,128)(2,1)S(1)}, bf16[16,896]{1,0:T(8,128)(2,1)S(1)}, u32[]{:S(2)}, u32[]{:S(2)}) %collective-permute-start.10) | collective-permute-done | bytes 28704 | tf_op jit(solution)/shard_map/ppermute | solution.py:57
  38.6 1.0 %collective-permute-done.9.refs_1_ = bf16[16,896]{1,0:T(8,128)(2,1)S(1)} collective-permute-done((bf16[16,896]{1,0:T(8,128)(2,1)S(1)}, bf16[16,896]{1,0:T(8,128)(2,1)S(1)}, u32[]{:S(2)}, u32[]{:S(2)}) %collective-permute-start.9) | collective-permute-done | bytes 28704 | tf_op jit(solution)/shard_map/ppermute | solution.py:57
  39.6 1.9 %collective-permute-start.12 = (bf16[64,896]{1,0:T(8,128)(2,1)S(1)}, bf16[64,896]{1,0:T(8,128)(2,1)S(1)}, u32[]{:S(2)}, u32[]{:S(2)}) collective-permute-start(bf16[64,896]{1,0:T(8,128)(2,1)S(1)} %collect.1.refs_0_), channel_id=1, source_target_pairs={{1,0},{0,1},{3,2},{2,3},{5,4},{4,5},{7,6},{6,7},{9,8},{8,9},{11,10... | collective-permute-start | bytes 344072 | tf_op jit(solution)/shard_map/ppermute | solution.py:40
  41.5 0.0 collective-permute-done.15.beside_sibling_ref
  41.5 0.0 collective-permute-done.17.across_sibling_ref
  41.5 0.2 order.1.refs_2_
  41.7 0.8 %collective-permute-done.12.refs_1_ = bf16[64,896]{1,0:T(8,128)(2,1)S(1)} collective-permute-done((bf16[64,896]{1,0:T(8,128)(2,1)S(1)}, bf16[64,896]{1,0:T(8,128)(2,1)S(1)}, u32[]{:S(2)}, u32[]{:S(2)}) %collective-permute-start.12) | collective-permute-done | bytes 114720 | tf_op jit(solution)/shard_map/ppermute | solution.py:40
  42.5 3.2 %outputs.1 = (bf16[512,4096]{1,0:T(8,128)(2,1)}, f32[64,4096]{1,0:T(8,128)}) custom-call(bf16[64,896]{1,0:T(8,128)(2,1)S(1)} %collect.1.refs_0_, bf16[64,896]{1,0:T(8,128)(2,1)S(1)} %collective-permute-done.12.refs_1_, bf16[256,4096]{1,0:T(8,128)(2,1)S(1)} %order.1.refs_2_), custom_call_target="tpu_custom_call" | custom-call | flops 603979776 | bytes 7340032 | tf_op jit(solution)/shard_map/outputs/pallas_call | solution.py:272
  (7 shorter events, 0.1 us)
Async XLA Ops:
  0.6 6.0 %copy-start.1 = (bf16[16,4096]{1,0:T(8,128)(2,1)S(1)}, bf16[16,4096]{1,0:T(8,128)(2,1)}, u32[]{:S(2)}) copy-start(bf16[16,4096]{1,0:T(8,128)(2,1)} %stream_ref.3) | copy-start | bytes 393220
  0.6 6.0 %copy-start = (bf16[512,4096]{1,0:T(8,128)(2,1)S(1)}, bf16[512,4096]{1,0:T(8,128)(2,1)}, u32[]{:S(2)}) copy-start(bf16[512,4096]{1,0:T(8,128)(2,1)} %probe_ref.1) | copy-start | bytes 12582916
  0.6 10.5 %collective-permute-start.2 = (bf16[16,4096]{1,0:T(8,128)(2,1)}, bf16[16,4096]{1,0:T(8,128)(2,1)S(1)}, u32[]{:S(2)}, u32[]{:S(2)}) collective-permute-start(bf16[16,4096]{1,0:T(8,128)(2,1)} %temp_ref.3), channel_id=1, source_target_pairs={{1,0},{0,1},{3,2},{2,3},{5,4},{4,5},{7,6},{6,7},{9,8},{8,9},{11,10... | collective-permute-start | bytes 393224 | tf_op jit(solution)/shard_map/ppermute | solution.py:40
  2.2 9.0 %collective-permute-start = (bf16[16,4096]{1,0:T(8,128)(2,1)}, bf16[16,4096]{1,0:T(8,128)(2,1)S(1)}, u32[]{:S(2)}, u32[]{:S(2)}) collective-permute-start(bf16[16,4096]{1,0:T(8,128)(2,1)} %temp_ref.3), channel_id=1, source_target_pairs={{2,0},{3,1},{4,2},{5,3},{6,4},{7,5},{0,6},{1,7},{10,8},{11,9},{12,... | collective-permute-start | bytes 393224 | tf_op jit(solution)/shard_map/ppermute | solution.py:40
  4.7 6.8 %collective-permute-start.13 = (bf16[16,4096]{1,0:T(8,128)(2,1)}, bf16[16,4096]{1,0:T(8,128)(2,1)S(1)}, u32[]{:S(2)}, u32[]{:S(2)}) collective-permute-start(bf16[16,4096]{1,0:T(8,128)(2,1)} %stream_ref.3), channel_id=1, source_target_pairs={{1,0},{0,1},{3,2},{2,3},{5,4},{4,5},{7,6},{6,7},{9,8},{8,9},{11,10... | collective-permute-start | bytes 393224 | tf_op jit(solution)/shard_map/ppermute | solution.py:40
  5.1 0.9 %copy-start.2 = (bf16[16,4096]{1,0:T(8,128)(2,1)S(1)}, bf16[16,4096]{1,0:T(8,128)(2,1)}, u32[]{:S(2)}) copy-start(bf16[16,4096]{1,0:T(8,128)(2,1)} %temp_ref.3) | copy-start | bytes 393220
  6.0 5.1 %copy-start.3 = (bf16[16,4096]{1,0:T(8,128)(2,1)S(1)}, bf16[16,4096]{1,0:T(8,128)(2,1)}, u32[]{:S(2)}) copy-start(bf16[16,4096]{1,0:T(8,128)(2,1)} %temp_ref.3) | copy-start | bytes 393220
  6.0 5.1 %collective-permute-start.1 = (bf16[16,2048]{1,0:T(8,128)(2,1)S(1)}, bf16[16,2048]{1,0:T(8,128)(2,1)S(1)}, u32[]{:S(2)}, u32[]{:S(2)}) collective-permute-start(bf16[16,2048]{1,0:T(8,128)(2,1)S(1)} %half.1), channel_id=1, source_target_pairs={{4,0},{5,1},{6,2},{7,3},{0,4},{1,5},{2,6},{3,7},{12,8},{13,9},{14,... | collective-permute-start | bytes 196616 | tf_op jit(solution)/shard_map/ppermute | solution.py:40
  11.6 8.6 %collective-permute-start.14 = (bf16[64,4096]{1,0:T(8,128)(2,1)S(1)}, bf16[64,4096]{1,0:T(8,128)(2,1)S(1)}, u32[]{:S(2)}, u32[]{:S(2)}) collective-permute-start(bf16[64,4096]{1,0:T(8,128)(2,1)S(1)} %chip.1.chip_ref), channel_id=1, source_target_pairs={{6,0},{3,1},{0,2},{5,3},{2,4},{7,5},{4,6},{1,7},{14,8},{11,9},{8,1... | collective-permute-start | bytes 1572872 | tf_op jit(solution)/shard_map/ppermute | solution.py:40
  13.1 5.0 %collective-permute-start.5 = (f32[16,640]{1,0:T(8,128)S(1)}, f32[16,640]{1,0:T(8,128)S(1)}, u32[]{:S(2)}, u32[]{:S(2)}) collective-permute-start(f32[16,640]{1,0:T(8,128)S(1)} %gram.1.a_ref._), channel_id=1, source_target_pairs={{24,0},{0,8},{8,16},{16,24},{56,32},{32,40},{40,48},{48,56},{88,64... | collective-permute-start | bytes 122888 | tf_op jit(solution)/shard_map/ppermute | solution.py:57
  14.4 5.6 %collective-permute-start.4 = (f32[16,640]{1,0:T(8,128)S(1)}, f32[16,640]{1,0:T(8,128)S(1)}, u32[]{:S(2)}, u32[]{:S(2)}) collective-permute-start(f32[16,640]{1,0:T(8,128)S(1)} %gram.1.a_ref._), channel_id=1, source_target_pairs={{16,0},{24,8},{0,16},{8,24},{48,32},{56,40},{32,48},{40,56},{80,64... | collective-permute-start | bytes 122888 | tf_op jit(solution)/shard_map/ppermute | solution.py:57
  17.0 3.1 %collective-permute-start.3 = (f32[16,640]{1,0:T(8,128)S(1)}, f32[16,640]{1,0:T(8,128)S(1)}, u32[]{:S(2)}, u32[]{:S(2)}) collective-permute-start(f32[16,640]{1,0:T(8,128)S(1)} %gram.1.a_ref._), channel_id=1, source_target_pairs={{8,0},{16,8},{24,16},{0,24},{40,32},{48,40},{56,48},{32,56},{72,64... | collective-permute-start | bytes 122888 | tf_op jit(solution)/shard_map/ppermute | solution.py:57
  20.3 10.9 %collective-permute-start.16 = (bf16[32,4096]{1,0:T(8,128)(2,1)S(1)}, bf16[32,4096]{1,0:T(8,128)(2,1)S(1)}, u32[]{:S(2)}, u32[]{:S(2)}) collective-permute-start(bf16[32,4096]{1,0:T(8,128)(2,1)S(1)} %relay.1), channel_id=1, source_target_pairs={{6,0},{3,1},{0,2},{5,3},{2,4},{7,5},{4,6},{1,7},{14,8},{11,9},{8,1... | collective-permute-start | bytes 786440 | tf_op jit(solution)/shard_map/ppermute | solution.py:40
  22.5 19.0 %collective-permute-start.15 = (bf16[64,4096]{1,0:T(8,128)(2,1)S(1)}, bf16[64,4096]{1,0:T(8,128)(2,1)S(1)}, u32[]{:S(2)}, u32[]{:S(2)}) collective-permute-start(bf16[64,4096]{1,0:T(8,128)(2,1)S(1)} %collective-permute-done.14.both_ref.beside_ref), channel_id=1, source_target_pairs={{1,0},{0,1},{3,2},{2,3},{5,4},{4,5},{7,6},{6,7},{9,8},{8,9},{11,10... | collective-permute-start | bytes 1572872 | tf_op jit(solution)/shard_map/ppermute | solution.py:40
  23.2 5.7 %collective-permute-start.8 = (f32[16,640]{1,0:T(8,128)S(1)}, f32[16,640]{1,0:T(8,128)S(1)}, u32[]{:S(2)}, u32[]{:S(2)}) collective-permute-start(f32[16,640]{1,0:T(8,128)S(1)} %add.1.a_ref._), channel_id=1, source_target_pairs={{96,0},{104,8},{112,16},{120,24},{0,32},{8,40},{16,48},{24,56},{32... | collective-permute-start | bytes 122888 | tf_op jit(solution)/shard_map/ppermute | solution.py:57
  24.8 5.5 %collective-permute-start.7 = (f32[16,640]{1,0:T(8,128)S(1)}, f32[16,640]{1,0:T(8,128)S(1)}, u32[]{:S(2)}, u32[]{:S(2)}) collective-permute-start(f32[16,640]{1,0:T(8,128)S(1)} %add.1.a_ref._), channel_id=1, source_target_pairs={{64,0},{72,8},{80,16},{88,24},{96,32},{104,40},{112,48},{120,56},{... | collective-permute-start | bytes 122888 | tf_op jit(solution)/shard_map/ppermute | solution.py:57
  28.1 3.0 %collective-permute-start.6 = (f32[16,640]{1,0:T(8,128)S(1)}, f32[16,640]{1,0:T(8,128)S(1)}, u32[]{:S(2)}, u32[]{:S(2)}) collective-permute-start(f32[16,640]{1,0:T(8,128)S(1)} %add.1.a_ref._), channel_id=1, source_target_pairs={{32,0},{40,8},{48,16},{56,24},{64,32},{72,40},{80,48},{88,56},{96,... | collective-permute-start | bytes 122888 | tf_op jit(solution)/shard_map/ppermute | solution.py:57
  31.2 10.3 %collective-permute-start.17 = (bf16[32,4096]{1,0:T(8,128)(2,1)S(1)}, bf16[32,4096]{1,0:T(8,128)(2,1)S(1)}, u32[]{:S(2)}, u32[]{:S(2)}) collective-permute-start(bf16[32,4096]{1,0:T(8,128)(2,1)S(1)} %later.1), channel_id=1, source_target_pairs={{1,0},{0,1},{3,2},{2,3},{5,4},{4,5},{7,6},{6,7},{9,8},{8,9},{11,10... | collective-permute-start | bytes 786440 | tf_op jit(solution)/shard_map/ppermute | solution.py:40
  32.9 4.5 %collective-permute-start.11 = (bf16[16,896]{1,0:T(8,128)(2,1)S(1)}, bf16[16,896]{1,0:T(8,128)(2,1)S(1)}, u32[]{:S(2)}, u32[]{:S(2)}) collective-permute-start(bf16[16,896]{1,0:T(8,128)(2,1)S(1)} %total.1.refs_0_._), channel_id=1, source_target_pairs={{6,0},{7,1},{0,2},{1,3},{2,4},{3,5},{4,6},{5,7},{14,8},{15,9},{8,1... | collective-permute-start | bytes 86024 | tf_op jit(solution)/shard_map/ppermute | solution.py:57
  33.7 4.9 %collective-permute-start.10 = (bf16[16,896]{1,0:T(8,128)(2,1)S(1)}, bf16[16,896]{1,0:T(8,128)(2,1)S(1)}, u32[]{:S(2)}, u32[]{:S(2)}) collective-permute-start(bf16[16,896]{1,0:T(8,128)(2,1)S(1)} %total.1.refs_0_._), channel_id=1, source_target_pairs={{4,0},{5,1},{6,2},{7,3},{0,4},{1,5},{2,6},{3,7},{12,8},{13,9},{14,... | collective-permute-start | bytes 86024 | tf_op jit(solution)/shard_map/ppermute | solution.py:57
  36.9 2.7 %collective-permute-start.9 = (bf16[16,896]{1,0:T(8,128)(2,1)S(1)}, bf16[16,896]{1,0:T(8,128)(2,1)S(1)}, u32[]{:S(2)}, u32[]{:S(2)}) collective-permute-start(bf16[16,896]{1,0:T(8,128)(2,1)S(1)} %total.1.refs_0_._), channel_id=1, source_target_pairs={{2,0},{3,1},{4,2},{5,3},{6,4},{7,5},{0,6},{1,7},{10,8},{11,9},{12,... | collective-permute-start | bytes 86024 | tf_op jit(solution)/shard_map/ppermute | solution.py:57
  39.6 2.8 %collective-permute-start.12 = (bf16[64,896]{1,0:T(8,128)(2,1)S(1)}, bf16[64,896]{1,0:T(8,128)(2,1)S(1)}, u32[]{:S(2)}, u32[]{:S(2)}) collective-permute-start(bf16[64,896]{1,0:T(8,128)(2,1)S(1)} %collect.1.refs_0_), channel_id=1, source_target_pairs={{1,0},{0,1},{3,2},{2,3},{5,4},{4,5},{7,6},{6,7},{9,8},{8,9},{11,10... | collective-permute-start | bytes 344072 | tf_op jit(solution)/shard_map/ppermute | solution.py:40

commit v2 on v1

--- a/solution.py
+++ b/solution.py
@@ -10,7 +10,7 @@
 F32 = jnp.float32
 BF16 = jnp.bfloat16
 CORES = 2
-HALF_WORK = 1 << 33
+LEAD_WORK = 1 << 33
 
 
 def dot(left, right, dims):
@@ -55,76 +55,109 @@
         [(n // span * span + (n + step * stride) % span, n) for n in range(size)] for step in (1, 3, 2)
     ]
     first, last, opposite = [lax.ppermute(value, axis, pairs) for pairs in steps]
-    return [value, first, opposite, last]
+    return [value, first, last, opposite]
 
 
 def rows_at(place, height):
     return pl.ds(pl.multiple_of(place * height, height), height)
 
 
-def gram_kernel(part_ref, own_ref, next_ref, half_ref, sibling_ref, message_ref, temp):
+def gram_kernel(
+    part_ref, own_ref, sibling_ref, before_ref, before_sibling_ref, after_ref, message_ref
+):
     height, columns = part_ref.shape
-    chips = temp.shape[0] // height
-    span = half_ref.shape[1]
+    chips = lax.axis_size("samp") // CORES
     chip = lax.axis_index("samp") // CORES
-    opposite = rows_at(lax.rem(chip + 2, chips), height)
-    temp[rows_at(chip, height), :] = own_ref[...]
-    temp[rows_at(lax.rem(chip + 1, chips), height), :] = next_ref[...]
-    temp[opposite, :] = jnp.zeros(own_ref.shape, BF16)
-    temp[opposite, rows_at(chip // 2, span)] = half_ref[...]
-    temp[rows_at(lax.rem(chip + 3, chips), height), :] = jnp.zeros(own_ref.shape, BF16)
     mine = jnp.concatenate([own_ref[...], sibling_ref[...]], axis=0)
-    gram = dot(mine, temp[...], ((1,), (1,)))
-    place = lax.broadcasted_iota(jnp.int32, gram.shape, 1) // height
-    gram = jnp.where(place == chip, 0.5 * gram, gram)
-    gram = jnp.concatenate([gram[:height], gram[height:]], axis=1)
+    others = jnp.concatenate([own_ref[...], after_ref[...]], axis=0)
+    near = dot(mine, others, ((1,), (1,)))
+    place = lax.broadcasted_iota(jnp.int32, near.shape, 1) // height
+    near = jnp.where(place == 0, 0.5 * near, near)
+    span = own_ref.shape[1] // 2
+    here = rows_at(chip // 2, span)
+    across = jnp.concatenate([before_ref[:, here], before_sibling_ref[:, here]], axis=0)
+    across = dot(across, after_ref[:, here], ((1,), (1,)))
+    gram = jnp.concatenate([near, across, jnp.zeros(across.shape, F32)], axis=1)
+    gram = pltpu.roll(jnp.concatenate([gram, gram], axis=1), chip * height, 1)[:, : chips * height]
     message_ref[:, :columns] = part_ref[...]
-    message_ref[:, columns:] = gram
-
-
-def half_kernel(temp_ref, out_ref):
-    span = out_ref.shape[1]
-    out_ref[...] = temp_ref[:, rows_at(1 - lax.axis_index("samp") // CORES // 2, span)]
+    message_ref[:, columns:] = jnp.concatenate([gram[:height], gram[height:]], axis=1)
+
+
+def collect_kernel(*refs):
+    *blocks, out_ref = refs
+    height = blocks[0].shape[0]
+    chip = lax.axis_index("samp") // CORES
+    for step, block in zip((0, 1, 3, 2), blocks):
+        out_ref[rows_at(lax.rem(chip + step, len(blocks)), height), :] = block[...]
+
+
+def lead_kernel(out_ref):
+    out_ref[...] = jnp.zeros(out_ref.shape, F32)
+
+
+def copy_kernel(value_ref, _, out_ref):
+    out_ref[...] = value_ref[...]
 
 
 def part_kernel(stream_ref, probe_ref, part_ref):
     part_ref[...] = dot(stream_ref[...], probe_ref[...], ((1,), (1,)))
 
 
-def chip_kernel(temp_ref, temp_sibling_ref, stream_ref, stream_sibling_ref, _, out_ref):
-    height = temp_ref.shape[0]
+def beside_kernel(own_ref, sibling_ref, before_ref, after_ref, _, out_ref):
+    height = own_ref.shape[0]
     core = lax.rem(lax.axis_index("samp"), CORES)
-    for base, (own, other) in enumerate(((temp_ref, temp_sibling_ref), (stream_ref, stream_sibling_ref))):
-        out_ref[rows_at(CORES * base + core, height), :] = own[...]
-        out_ref[rows_at(CORES * base + 1 - core, height), :] = other[...]
-
-
-def copy_kernel(value_ref, _, out_ref):
-    out_ref[...] = value_ref[...]
-
-
-def relay_kernel(both_ref, _, out_ref):
+    out_ref[rows_at(core, height), :] = own_ref[...]
+    out_ref[rows_at(1 - core, height), :] = sibling_ref[...]
+
+    @pl.when(core == 0)
+    def _():
+        out_ref[CORES * height :] = before_ref[...]
+
+    @pl.when(core == 1)
+    def _():
+        out_ref[CORES * height :] = after_ref[...]
+
+
+def relay_kernel(beside_ref, _, out_ref):
     core = lax.rem(lax.axis_index("samp"), CORES)
-    out_ref[...] = both_ref[rows_at(core, out_ref.shape[0]), :]
-
-
-def order_kernel(chip_ref, beside_ref, beside_sibling_ref, across_ref, across_sibling_ref, out_ref):
+    out_ref[...] = beside_ref[rows_at(core, out_ref.shape[0]), :]
+
+
+def both_kernel(beside_ref, after_ref, _, out_ref):
+    height = after_ref.shape[0]
+    out_ref[:-height] = beside_ref[...]
+    out_ref[-height:] = after_ref[...]
+
+
+def order_kernel(
+    temp_ref, temp_sibling_ref, before_ref, before_sibling_ref, after_ref, stream_ref, stream_sibling_ref,
+    beside_ref, both_ref, across_ref, across_sibling_ref, out_ref,
+):
     own = lax.axis_index("samp")
     chip, core = own // CORES, lax.rem(own, CORES)
-    height = chip_ref.shape[0] // (2 * CORES)
-    chips = out_ref.shape[0] // chip_ref.shape[0]
-
-    def put(ref, step, bases):
-        place = lax.rem(chip + step, chips)
-        for n in range(ref.shape[0] // height):
-            base = bases * CORES + n
-            out_ref[rows_at(base * chips + place, height), :] = ref[n * height : (n + 1) * height]
-
-    put(chip_ref, 0, 0)
-    put(beside_ref, chips - 1 - core * (chips - 2), 0)
-    put(beside_sibling_ref, 1 + core * (chips - 2), 0)
-    put(across_ref, 2, core)
-    put(across_sibling_ref, 2, 1 - core)
+    height = temp_ref.shape[0]
+    chips = out_ref.shape[0] // (2 * CORES * height)
+
+    def put(base, owner, step, value):
+        place = (base * CORES + owner) * chips + lax.rem(chip + step, chips)
+        out_ref[rows_at(place, height), :] = value
+
+    rows = [slice(n * height, (n + 1) * height) for n in range(2 * CORES)]
+    put(0, core, 0, temp_ref[...])
+    put(0, 1 - core, 0, temp_sibling_ref[...])
+    put(0, core, chips - 1, before_ref[...])
+    put(0, 1 - core, chips - 1, before_sibling_ref[...])
+    put(0, core, 1, after_ref[...])
+    put(0, 1 - core, 1, both_ref[rows[3]])
+    put(0, core, 2, beside_ref[rows[2]])
+    put(0, 1 - core, 2, both_ref[rows[2]])
+    put(1, core, 0, stream_ref[...])
+    put(1, 1 - core, 0, stream_sibling_ref[...])
+    for n in range(CORES):
+        put(1, n, chips - 1 - core * (chips - 2), beside_ref[rows[n]])
+        put(1, n, 1 + core * (chips - 2), both_ref[rows[n]])
+    put(1, core, 2, across_ref[...])
+    put(1, 1 - core, 2, across_sibling_ref[...])
 
 
 def add_kernel(a_ref, b_ref, c_ref, d_ref, out_ref):
@@ -136,14 +169,6 @@
     pieces = [total[:, :columns].astype(BF16), *split3(total[:, columns:])]
     pieces = jnp.concatenate(pieces, axis=1)
     message_ref[...] = pieces
-
-
-def collect_kernel(*refs):
-    *blocks, out_ref = refs
-    height = blocks[0].shape[0]
-    chip = lax.axis_index("samp") // CORES
-    for step, block in enumerate(blocks):
-        out_ref[rows_at(lax.rem(chip + step, len(blocks)), height), :] = block[...]
 
 
 def output_kernel(columns, scales, *refs):
@@ -165,6 +190,19 @@
     bottom = jnp.where(first, products[half:], products[:half])
     bottom = jnp.concatenate([bottom[:, half:], bottom[:, :half]], axis=1)
     gram = jnp.concatenate([top, bottom], axis=0)
+    height = samples // lax.axis_size("samp")
+    row, lane = [lax.broadcasted_iota(jnp.int32, gram.shape, axis) // height for axis in (0, 1)]
+    chips = half // height
+    moves = lax.rem(lane + 2 * chips - row - 2, chips) == 0
+    moved = jnp.where(moves, gram, 0.0)
+    moved = jnp.concatenate(
+        [moved[start : start + size] for base in (0, half) for start, size in ((base + height, half - height), (base, height))],
+        axis=0,
+    )
+    ahead = jnp.concatenate([moved[:, height:], moved[:, :height]], axis=1)
+    back_end = jnp.concatenate([moved[:, samples - half + height :], moved[:, : samples - half + height]], axis=1)
+    moved = jnp.where(lax.rem(lane, chips) < chips - 1, ahead, back_end)
+    gram = jnp.where(moves, 0.0, gram) + moved
     product = sum(dot(left[...], piece, ((1,), (0,))) for piece in split3(gram + gram.T))
     power = jnp.maximum(jnp.sum(product * turned, axis=1, keepdims=True), 0.0)
     power = power * (image_scale * image_scale)
@@ -216,50 +254,55 @@
             name=name,
         )(*operands)
 
+    slab = ((height, local_rows), BF16)
     packed = columns + 3 * samples
-    span = local_rows // 2
-    chips = groups // CORES
-
-    (temp_half,) = call(half_kernel, "half", [temp_slab], [((height, span), BF16)], work=HALF_WORK)
-    temp_half = chip_step(temp_half, 2)
-    temp_next = chip_step(temp_slab, 1)
+
+    (lead,) = call(lead_kernel, "lead", [], [((8, 128), F32)], work=LEAD_WORK)
+    (temp_copy,) = call(copy_kernel, "ahead", [temp_slab, lead], [slab])
+    before = chip_step(temp_slab, 3)
+    after = chip_step(temp_copy, 1)
     temp_sibling = sibling(temp_slab)
     stream_sibling = sibling(stream_slab)
     (part,) = call(
         part_kernel, "part", [stream_slab, probe], [((height, columns), F32)], work=2 * height * columns * local_rows
     )
+    (before_copy,) = call(copy_kernel, "before", [before, part], [slab])
+    before_sibling = sibling(before_copy)
     (message,) = call(
         gram_kernel,
         "gram",
-        [part, temp_slab, temp_next, temp_half, temp_sibling],
+        [part, temp_slab, temp_sibling, before, before_sibling, after],
         [((height, wide), F32)],
-        [((half, local_rows), BF16)],
-        4 * height * half * local_rows,
-    )
-    (chip,) = call(
-        chip_kernel,
-        "chip",
-        [temp_slab, temp_sibling, stream_slab, stream_sibling, message],
-        [((4 * height, local_rows), BF16)],
-    )
-    beside = permute(chip, lambda n: (n - CORES if n % CORES == 0 else n + CORES) % groups)
+        work=4 * height * half * local_rows,
+    )
+    (beside,) = call(
+        beside_kernel,
+        "beside",
+        [stream_slab, stream_sibling, before, after, message],
+        [((3 * height, local_rows), BF16)],
+    )
+    beside = permute(beside, lambda n: (n - CORES if n % CORES == 0 else n + CORES) % groups)
     (message,) = call(add_kernel, "add", around(message, 1), [((height, wide), F32)])
-    (across,) = call(relay_kernel, "relay", [beside, message], [((2 * height, local_rows), BF16)])
-    across = permute(across, lambda n: (n - CORES if n % CORES == 0 else n + CORES) % groups)
-    beside_sibling = sibling(beside)
     (message,) = call(
         functools.partial(sum_kernel, columns), "total", around(message, 4), [((height, packed), BF16)]
     )
-    (later,) = call(copy_kernel, "later", [across, message], [((2 * height, local_rows), BF16)])
+    (across,) = call(relay_kernel, "relay", [beside, message], [slab])
+    across = permute(across, lambda n: (n - CORES if n % CORES == 0 else n + CORES) % groups)
+    (both,) = call(both_kernel, "both", [beside, after, message], [((4 * height, local_rows), BF16)])
+    both_sibling = sibling(both)
+    (message,) = call(collect_kernel, "collect", around(message, CORES, "samp"), [((half, packed), BF16)])
+    message_other = sibling(message)
+    (later,) = call(copy_kernel, "later", [across, message], [slab])
     across_sibling = sibling(later)
     (slabs,) = call(
         order_kernel,
         "order",
-        [chip, beside, beside_sibling, across, across_sibling],
+        [
+            temp_slab, temp_sibling, before, before_sibling, after, stream_slab, stream_sibling,
+            beside, both_sibling, across, across_sibling,
+        ],
         [((2 * samples, local_rows), BF16)],
     )
-    (message,) = call(collect_kernel, "collect", around(message, CORES, "samp"), [((half, packed), BF16)])
-    message_other = sibling(message)
 
     scales = (
         1.0 / (samples - 1.0),

time: 45.8 us -> 43.5 us (0.950)
  waiting for transfers between devices: 10.7 us -> 7.34 us
  starting transfers between devices: 28.2 us -> 30 us
  local copies, waits for them, and re-layouts: 0.92 us -> 0.01 us
    ppermute x9, waiting for transfers between devices: 6.58 us -> 4.72 us  [around(): lax.ppermute(value, axis, pairs)]
    ppermute x9 -> x10, starting transfers between devices: 13.1 us -> 14.7 us  [permute(): lax.ppermute(value, 'samp', [(source(n), n) for n in range(lax.axis_size(...]
    ppermute x9 -> x10, waiting for transfers between devices: 4.16 us -> 2.62 us  [permute(): lax.ppermute(value, 'samp', [(source(n), n) for n in range(lax.axis_size(...]
    unnamed x8 -> x6, local copies, waits for them, and re-layouts: 0.92 us -> 0.01 us
    pallas_call x10 -> x13, Pallas kernels: 1.88 us -> 2.02 us  [call(): pl.pallas_call(kernel, out_shape=tuple(outs), in_specs=whole(len(operands...]
  transfers between devices with their start and end apart: 18 -> 19, of which waited for: 8 -> 9; matrix products, arithmetic and copies ran while one was open for 0% -> 0% of each run, Pallas kernels for 4% -> 4%
where the time goes in v2:
time: 43.5 us; the launch traced here: 43.4 us
  starting transfers between devices  30 us (69%)
  waiting for transfers between devices  7.34 us (17%)
  Pallas kernels  5.29 us (12%)
  between operations  0.75 us (2%)
    ppermute x9, starting transfers between devices, around(): lax.ppermute(value, axis, pairs)  15.3 us
    ppermute x10, starting transfers between devices, permute(): lax.ppermute(value, 'samp', [(source(n), n) for n in range(lax.axis_size(...  14.7 us
    ppermute x9, waiting for transfers between devices, around(): lax.ppermute(value, axis, pairs)  4.72 us
    pallas_call x1, Pallas kernels, shards(): pl.pallas_call(functools.partial(output_kernel, columns, scales), out_sha...  3.27 us
    ppermute x10, waiting for transfers between devices, permute(): lax.ppermute(value, 'samp', [(source(n), n) for n in range(lax.axis_size(...  2.62 us
    pallas_call x13, Pallas kernels, call(): pl.pallas_call(kernel, out_shape=tuple(outs), in_specs=whole(len(operands...  2.02 us
  transfers between devices with their start and end apart: 19, of which 9 were waited for; matrix products, arithmetic and copies ran while one was open for 0% of the time, Pallas kernels for 4%

profile of v2, /device:TPU:1, one launch (start us, length us, event | category | flops | bytes accessed | tf_op | source)
XLA Modules:
  0.0 43.4 jit_solution(6457303506570697479)
XLA Ops:
  0.6 0.0 copy-start.1
  0.6 0.0 copy-start.2
  0.6 0.0 copy-start
  0.7 2.1 %collective-permute-start.1 = (bf16[16,4096]{1,0:T(8,128)(2,1)}, bf16[16,4096]{1,0:T(8,128)(2,1)S(1)}, u32[]{:S(2)}, u32[]{:S(2)}) collective-permute-start(bf16[16,4096]{1,0:T(8,128)(2,1)} %temp_ref.1), channel_id=1, source_target_pairs={{6,0},{7,1},{0,2},{1,3},{2,4},{3,5},{4,6},{5,7},{14,8},{15,9},{8,1... | collective-permute-start | bytes 393224 | tf_op jit(solution)/shard_map/ppermute | solution.py:40
  2.8 1.0 %collective-permute-start = (bf16[16,4096]{1,0:T(8,128)(2,1)}, bf16[16,4096]{1,0:T(8,128)(2,1)S(1)}, u32[]{:S(2)}, u32[]{:S(2)}) collective-permute-start(bf16[16,4096]{1,0:T(8,128)(2,1)} %temp_ref.1), channel_id=1, source_target_pairs={{1,0},{0,1},{3,2},{2,3},{5,4},{4,5},{7,6},{6,7},{9,8},{8,9},{11,10... | collective-permute-start | bytes 393224 | tf_op jit(solution)/shard_map/ppermute | solution.py:40
  3.7 0.0 copy-done.1
  3.7 1.5 %collective-permute-start.3 = (bf16[16,4096]{1,0:T(8,128)(2,1)S(1)}, bf16[16,4096]{1,0:T(8,128)(2,1)S(1)}, u32[]{:S(2)}, u32[]{:S(2)}) collective-permute-start(bf16[16,4096]{1,0:T(8,128)(2,1)S(1)} %ahead.1), channel_id=1, source_target_pairs={{2,0},{3,1},{4,2},{5,3},{6,4},{7,5},{0,6},{1,7},{10,8},{11,9},{12,... | collective-permute-start | bytes 393224 | tf_op jit(solution)/shard_map/ppermute | solution.py:40
  5.2 0.0 copy-done
  5.2 1.2 %part.1._.part_ref = f32[16,512]{1,0:T(8,128)S(1)} custom-call(bf16[16,4096]{1,0:T(8,128)(2,1)S(1)} %copy-done.2, bf16[512,4096]{1,0:T(8,128)(2,1)S(1)} %copy-done), custom_call_target="tpu_custom_call" | custom-call | flops 67108864 | bytes 4358144 | tf_op jit(solution)/shard_map/part/pallas_call | solution.py:246
  6.4 0.6 %collective-permute-done.1.value_ref.before_ref = bf16[16,4096]{1,0:T(8,128)(2,1)S(1)} collective-permute-done((bf16[16,4096]{1,0:T(8,128)(2,1)}, bf16[16,4096]{1,0:T(8,128)(2,1)S(1)}, u32[]{:S(2)}, u32[]{:S(2)}) %collective-permute-start.1) | collective-permute-done | bytes 131104 | tf_op jit(solution)/shard_map/ppermute | solution.py:40
  7.0 1.8 %collective-permute-start.2 = (bf16[16,4096]{1,0:T(8,128)(2,1)S(1)}, bf16[16,4096]{1,0:T(8,128)(2,1)S(1)}, u32[]{:S(2)}, u32[]{:S(2)}) collective-permute-start(bf16[16,4096]{1,0:T(8,128)(2,1)S(1)} %before.1), channel_id=1, source_target_pairs={{1,0},{0,1},{3,2},{2,3},{5,4},{4,5},{7,6},{6,7},{9,8},{8,9},{11,10... | collective-permute-start | bytes 393224 | tf_op jit(solution)/shard_map/ppermute | solution.py:40
  8.8 0.1 collective-permute-start.14
  8.9 0.1 collective-permute-done.3.after_ref
  8.9 0.0 collective-permute-done.sibling_ref.temp_sibling_ref
  8.9 0.8 %collective-permute-done.2.before_sibling_ref = bf16[16,4096]{1,0:T(8,128)(2,1)S(1)} collective-permute-done((bf16[16,4096]{1,0:T(8,128)(2,1)S(1)}, bf16[16,4096]{1,0:T(8,128)(2,1)S(1)}, u32[]{:S(2)}, u32[]{:S(2)}) %collective-permute-start.2) | collective-permute-done | bytes 131104 | tf_op jit(solution)/shard_map/ppermute | solution.py:40
  9.8 0.5 %gram.1.a_ref._ = f32[16,640]{1,0:T(8,128)S(1)} custom-call(f32[16,512]{1,0:T(8,128)S(1)} %part.1._.part_ref, bf16[16,4096]{1,0:T(8,128)(2,1)S(1)} %copy-done.1, bf16[16,4096]{1,0:T(8,128)(2,1)S(1)} %collective-permute-done.sibling_ref.temp_sibling_ref, bf16[16,4096]{1,0:T(8,128)(2,1)S(1)} %collective-permute-done.1.value_ref.before_ref, ...), custom_call_target="tpu_custom_call" | custom-call | flops 16777216 | bytes 729088 | tf_op jit(solution)/shard_map/gram/pallas_call | solution.py:246
  10.2 0.0 collective-permute-done.14.sibling_ref.stream_sibling_ref
  10.3 0.1 beside.1
  10.3 1.5 %collective-permute-start.15 = (bf16[48,4096]{1,0:T(8,128)(2,1)S(1)}, bf16[48,4096]{1,0:T(8,128)(2,1)S(1)}, u32[]{:S(2)}, u32[]{:S(2)}) collective-permute-start(bf16[48,4096]{1,0:T(8,128)(2,1)S(1)} %beside.1), channel_id=1, source_target_pairs={{6,0},{3,1},{0,2},{5,3},{2,4},{7,5},{4,6},{1,7},{14,8},{11,9},{8,1... | collective-permute-start | bytes 1179656 | tf_op jit(solution)/shard_map/ppermute | solution.py:40
  11.9 2.9 %collective-permute-start.6 = (f32[16,640]{1,0:T(8,128)S(1)}, f32[16,640]{1,0:T(8,128)S(1)}, u32[]{:S(2)}, u32[]{:S(2)}) collective-permute-start(f32[16,640]{1,0:T(8,128)S(1)} %gram.1.a_ref._), channel_id=1, source_target_pairs={{16,0},{24,8},{0,16},{8,24},{48,32},{56,40},{32,48},{40,56},{80,64... | collective-permute-start | bytes 122888 | tf_op jit(solution)/shard_map/ppermute | solution.py:57
  14.8 0.4 collective-permute-start.5
  15.2 2.3 %collective-permute-start.4 = (f32[16,640]{1,0:T(8,128)S(1)}, f32[16,640]{1,0:T(8,128)S(1)}, u32[]{:S(2)}, u32[]{:S(2)}) collective-permute-start(f32[16,640]{1,0:T(8,128)S(1)} %gram.1.a_ref._), channel_id=1, source_target_pairs={{8,0},{16,8},{24,16},{0,24},{40,32},{48,40},{56,48},{32,56},{72,64... | collective-permute-start | bytes 122888 | tf_op jit(solution)/shard_map/ppermute | solution.py:57
  17.5 0.0 collective-permute-done.6.d_ref
  17.5 1.7 %collective-permute-done.5.c_ref = f32[16,640]{1,0:T(8,128)S(1)} collective-permute-done((f32[16,640]{1,0:T(8,128)S(1)}, f32[16,640]{1,0:T(8,128)S(1)}, u32[]{:S(2)}, u32[]{:S(2)}) %collective-permute-start.5) | collective-permute-done | bytes 40992 | tf_op jit(solution)/shard_map/ppermute | solution.py:57
  19.2 0.0 collective-permute-done.4.b_ref
  19.2 3.7 %collective-permute-start.9 = (f32[16,640]{1,0:T(8,128)S(1)}, f32[16,640]{1,0:T(8,128)S(1)}, u32[]{:S(2)}, u32[]{:S(2)}) collective-permute-start(f32[16,640]{1,0:T(8,128)S(1)} %add.1.a_ref), channel_id=1, source_target_pairs={{64,0},{72,8},{80,16},{88,24},{96,32},{104,40},{112,48},{120,56},{... | collective-permute-start | bytes 122888 | tf_op jit(solution)/shard_map/ppermute | solution.py:57
  22.9 0.7 %collective-permute-start.8 = (f32[16,640]{1,0:T(8,128)S(1)}, f32[16,640]{1,0:T(8,128)S(1)}, u32[]{:S(2)}, u32[]{:S(2)}) collective-permute-start(f32[16,640]{1,0:T(8,128)S(1)} %add.1.a_ref), channel_id=1, source_target_pairs={{96,0},{104,8},{112,16},{120,24},{0,32},{8,40},{16,48},{24,56},{32... | collective-permute-start | bytes 122888 | tf_op jit(solution)/shard_map/ppermute | solution.py:57
  23.6 1.9 %collective-permute-start.7 = (f32[16,640]{1,0:T(8,128)S(1)}, f32[16,640]{1,0:T(8,128)S(1)}, u32[]{:S(2)}, u32[]{:S(2)}) collective-permute-start(f32[16,640]{1,0:T(8,128)S(1)} %add.1.a_ref), channel_id=1, source_target_pairs={{32,0},{40,8},{48,16},{56,24},{64,32},{72,40},{80,48},{88,56},{96,... | collective-permute-start | bytes 122888 | tf_op jit(solution)/shard_map/ppermute | solution.py:57
  25.5 0.0 collective-permute-done.9.d_ref
  25.5 1.4 %collective-permute-done.8.c_ref = f32[16,640]{1,0:T(8,128)S(1)} collective-permute-done((f32[16,640]{1,0:T(8,128)S(1)}, f32[16,640]{1,0:T(8,128)S(1)}, u32[]{:S(2)}, u32[]{:S(2)}) %collective-permute-start.8) | collective-permute-done | bytes 40992 | tf_op jit(solution)/shard_map/ppermute | solution.py:57
  26.9 0.0 collective-permute-done.7.b_ref
  27.0 0.0 collective-permute-done.15.beside_ref
  27.0 2.6 %collective-permute-start.16 = (bf16[64,4096]{1,0:T(8,128)(2,1)S(1)}, bf16[64,4096]{1,0:T(8,128)(2,1)S(1)}, u32[]{:S(2)}, u32[]{:S(2)}) collective-permute-start(bf16[64,4096]{1,0:T(8,128)(2,1)S(1)} %both.1), channel_id=1, source_target_pairs={{1,0},{0,1},{3,2},{2,3},{5,4},{4,5},{7,6},{6,7},{9,8},{8,9},{11,10... | collective-permute-start | bytes 1572872 | tf_op jit(solution)/shard_map/ppermute | solution.py:40
  29.6 2.1 %collective-permute-start.17 = (bf16[16,4096]{1,0:T(8,128)(2,1)S(1)}, bf16[16,4096]{1,0:T(8,128)(2,1)S(1)}, u32[]{:S(2)}, u32[]{:S(2)}) collective-permute-start(bf16[16,4096]{1,0:T(8,128)(2,1)S(1)} %relay.1), channel_id=1, source_target_pairs={{6,0},{3,1},{0,2},{5,3},{2,4},{7,5},{4,6},{1,7},{14,8},{11,9},{8,1... | collective-permute-start | bytes 393224 | tf_op jit(solution)/shard_map/ppermute | solution.py:40
  31.8 0.7 %collective-permute-start.12 = (bf16[16,896]{1,0:T(8,128)(2,1)S(1)}, bf16[16,896]{1,0:T(8,128)(2,1)S(1)}, u32[]{:S(2)}, u32[]{:S(2)}) collective-permute-start(bf16[16,896]{1,0:T(8,128)(2,1)S(1)} %total.1.refs_0_._), channel_id=1, source_target_pairs={{4,0},{5,1},{6,2},{7,3},{0,4},{1,5},{2,6},{3,7},{12,8},{13,9},{14,... | collective-permute-start | bytes 86024 | tf_op jit(solution)/shard_map/ppermute | solution.py:57
  32.4 0.8 %collective-permute-start.11 = (bf16[16,896]{1,0:T(8,128)(2,1)S(1)}, bf16[16,896]{1,0:T(8,128)(2,1)S(1)}, u32[]{:S(2)}, u32[]{:S(2)}) collective-permute-start(bf16[16,896]{1,0:T(8,128)(2,1)S(1)} %total.1.refs_0_._), channel_id=1, source_target_pairs={{6,0},{7,1},{0,2},{1,3},{2,4},{3,5},{4,6},{5,7},{14,8},{15,9},{8,1... | collective-permute-start | bytes 86024 | tf_op jit(solution)/shard_map/ppermute | solution.py:57
  33.2 1.9 %collective-permute-start.10 = (bf16[16,896]{1,0:T(8,128)(2,1)S(1)}, bf16[16,896]{1,0:T(8,128)(2,1)S(1)}, u32[]{:S(2)}, u32[]{:S(2)}) collective-permute-start(bf16[16,896]{1,0:T(8,128)(2,1)S(1)} %total.1.refs_0_._), channel_id=1, source_target_pairs={{2,0},{3,1},{4,2},{5,3},{6,4},{7,5},{0,6},{1,7},{10,8},{11,9},{12,... | collective-permute-start | bytes 86024 | tf_op jit(solution)/shard_map/ppermute | solution.py:57
  35.1 1.5 %collective-permute-done.12.refs_3_ = bf16[16,896]{1,0:T(8,128)(2,1)S(1)} collective-permute-done((bf16[16,896]{1,0:T(8,128)(2,1)S(1)}, bf16[16,896]{1,0:T(8,128)(2,1)S(1)}, u32[]{:S(2)}, u32[]{:S(2)}) %collective-permute-start.12) | collective-permute-done | bytes 28704 | tf_op jit(solution)/shard_map/ppermute | solution.py:57
  36.6 0.1 collective-permute-done.11.refs_2_
  36.8 0.0 collective-permute-done.10.refs_1_
  36.8 0.0 collective-permute-done.17.value_ref.across_ref
  36.8 1.9 %collective-permute-start.18 = (bf16[16,4096]{1,0:T(8,128)(2,1)S(1)}, bf16[16,4096]{1,0:T(8,128)(2,1)S(1)}, u32[]{:S(2)}, u32[]{:S(2)}) collective-permute-start(bf16[16,4096]{1,0:T(8,128)(2,1)S(1)} %later.1), channel_id=1, source_target_pairs={{1,0},{0,1},{3,2},{2,3},{5,4},{4,5},{7,6},{6,7},{9,8},{8,9},{11,10... | collective-permute-start | bytes 393224 | tf_op jit(solution)/shard_map/ppermute | solution.py:40
  38.8 0.1 collective-permute-start.13
  38.9 0.9 %collective-permute-done.18.across_sibling_ref = bf16[16,4096]{1,0:T(8,128)(2,1)S(1)} collective-permute-done((bf16[16,4096]{1,0:T(8,128)(2,1)S(1)}, bf16[16,4096]{1,0:T(8,128)(2,1)S(1)}, u32[]{:S(2)}, u32[]{:S(2)}) %collective-permute-start.18) | collective-permute-done | bytes 131104 | tf_op jit(solution)/shard_map/ppermute | solution.py:40
  39.8 0.0 collective-permute-done.16.both_ref
  39.8 0.1 order.1.refs_2_
  39.9 0.2 collective-permute-done.13.refs_1_
  40.1 3.3 %outputs.1 = (bf16[512,4096]{1,0:T(8,128)(2,1)}, f32[64,4096]{1,0:T(8,128)}) custom-call(bf16[64,896]{1,0:T(8,128)(2,1)S(1)} %collect.1._.refs_0_, bf16[64,896]{1,0:T(8,128)(2,1)S(1)} %collective-permute-done.13.refs_1_, bf16[256,4096]{1,0:T(8,128)(2,1)S(1)} %order.1.refs_2_), custom_call_target="tpu_custom_call" | custom-call | flops 603979776 | bytes 7340032 | tf_op jit(solution)/shard_map/outputs/pallas_call | solution.py:315
  (10 shorter events, 0.1 us)
Async XLA Ops:
  0.6 3.1 %copy-start.1 = (bf16[16,4096]{1,0:T(8,128)(2,1)S(1)}, bf16[16,4096]{1,0:T(8,128)(2,1)}, u32[]{:S(2)}) copy-start(bf16[16,4096]{1,0:T(8,128)(2,1)} %temp_ref.1) | copy-start | bytes 393220
  0.6 4.6 %copy-start.2 = (bf16[16,4096]{1,0:T(8,128)(2,1)S(1)}, bf16[16,4096]{1,0:T(8,128)(2,1)}, u32[]{:S(2)}) copy-start(bf16[16,4096]{1,0:T(8,128)(2,1)} %stream_ref.3) | copy-start | bytes 393220
  0.6 4.5 %copy-start = (bf16[512,4096]{1,0:T(8,128)(2,1)S(1)}, bf16[512,4096]{1,0:T(8,128)(2,1)}, u32[]{:S(2)}) copy-start(bf16[512,4096]{1,0:T(8,128)(2,1)} %probe_ref.1) | copy-start | bytes 12582916
  0.7 6.4 %collective-permute-start.1 = (bf16[16,4096]{1,0:T(8,128)(2,1)}, bf16[16,4096]{1,0:T(8,128)(2,1)S(1)}, u32[]{:S(2)}, u32[]{:S(2)}) collective-permute-start(bf16[16,4096]{1,0:T(8,128)(2,1)} %temp_ref.1), channel_id=1, source_target_pairs={{6,0},{7,1},{0,2},{1,3},{2,4},{3,5},{4,6},{5,7},{14,8},{15,9},{8,1... | collective-permute-start | bytes 393224 | tf_op jit(solution)/shard_map/ppermute | solution.py:40
  2.8 6.2 %collective-permute-start = (bf16[16,4096]{1,0:T(8,128)(2,1)}, bf16[16,4096]{1,0:T(8,128)(2,1)S(1)}, u32[]{:S(2)}, u32[]{:S(2)}) collective-permute-start(bf16[16,4096]{1,0:T(8,128)(2,1)} %temp_ref.1), channel_id=1, source_target_pairs={{1,0},{0,1},{3,2},{2,3},{5,4},{4,5},{7,6},{6,7},{9,8},{8,9},{11,10... | collective-permute-start | bytes 393224 | tf_op jit(solution)/shard_map/ppermute | solution.py:40
  3.7 5.2 %collective-permute-start.3 = (bf16[16,4096]{1,0:T(8,128)(2,1)S(1)}, bf16[16,4096]{1,0:T(8,128)(2,1)S(1)}, u32[]{:S(2)}, u32[]{:S(2)}) collective-permute-start(bf16[16,4096]{1,0:T(8,128)(2,1)S(1)} %ahead.1), channel_id=1, source_target_pairs={{2,0},{3,1},{4,2},{5,3},{6,4},{7,5},{0,6},{1,7},{10,8},{11,9},{12,... | collective-permute-start | bytes 393224 | tf_op jit(solution)/shard_map/ppermute | solution.py:40
  7.0 2.7 %collective-permute-start.2 = (bf16[16,4096]{1,0:T(8,128)(2,1)S(1)}, bf16[16,4096]{1,0:T(8,128)(2,1)S(1)}, u32[]{:S(2)}, u32[]{:S(2)}) collective-permute-start(bf16[16,4096]{1,0:T(8,128)(2,1)S(1)} %before.1), channel_id=1, source_target_pairs={{1,0},{0,1},{3,2},{2,3},{5,4},{4,5},{7,6},{6,7},{9,8},{8,9},{11,10... | collective-permute-start | bytes 393224 | tf_op jit(solution)/shard_map/ppermute | solution.py:40
  8.8 1.5 %collective-permute-start.14 = (bf16[16,4096]{1,0:T(8,128)(2,1)S(1)}, bf16[16,4096]{1,0:T(8,128)(2,1)S(1)}, u32[]{:S(2)}, u32[]{:S(2)}) collective-permute-start(bf16[16,4096]{1,0:T(8,128)(2,1)S(1)} %copy-done.2), channel_id=1, source_target_pairs={{1,0},{0,1},{3,2},{2,3},{5,4},{4,5},{7,6},{6,7},{9,8},{8,9},{11,10... | collective-permute-start | bytes 393224 | tf_op jit(solution)/shard_map/ppermute | solution.py:40
  10.3 16.6 %collective-permute-start.15 = (bf16[48,4096]{1,0:T(8,128)(2,1)S(1)}, bf16[48,4096]{1,0:T(8,128)(2,1)S(1)}, u32[]{:S(2)}, u32[]{:S(2)}) collective-permute-start(bf16[48,4096]{1,0:T(8,128)(2,1)S(1)} %beside.1), channel_id=1, source_target_pairs={{6,0},{3,1},{0,2},{5,3},{2,4},{7,5},{4,6},{1,7},{14,8},{11,9},{8,1... | collective-permute-start | bytes 1179656 | tf_op jit(solution)/shard_map/ppermute | solution.py:40
  11.9 5.6 %collective-permute-start.6 = (f32[16,640]{1,0:T(8,128)S(1)}, f32[16,640]{1,0:T(8,128)S(1)}, u32[]{:S(2)}, u32[]{:S(2)}) collective-permute-start(f32[16,640]{1,0:T(8,128)S(1)} %gram.1.a_ref._), channel_id=1, source_target_pairs={{16,0},{24,8},{0,16},{8,24},{48,32},{56,40},{32,48},{40,56},{80,64... | collective-permute-start | bytes 122888 | tf_op jit(solution)/shard_map/ppermute | solution.py:57
  14.8 4.4 %collective-permute-start.5 = (f32[16,640]{1,0:T(8,128)S(1)}, f32[16,640]{1,0:T(8,128)S(1)}, u32[]{:S(2)}, u32[]{:S(2)}) collective-permute-start(f32[16,640]{1,0:T(8,128)S(1)} %gram.1.a_ref._), channel_id=1, source_target_pairs={{24,0},{0,8},{8,16},{16,24},{56,32},{32,40},{40,48},{48,56},{88,64... | collective-permute-start | bytes 122888 | tf_op jit(solution)/shard_map/ppermute | solution.py:57
  15.2 4.0 %collective-permute-start.4 = (f32[16,640]{1,0:T(8,128)S(1)}, f32[16,640]{1,0:T(8,128)S(1)}, u32[]{:S(2)}, u32[]{:S(2)}) collective-permute-start(f32[16,640]{1,0:T(8,128)S(1)} %gram.1.a_ref._), channel_id=1, source_target_pairs={{8,0},{16,8},{24,16},{0,24},{40,32},{48,40},{56,48},{32,56},{72,64... | collective-permute-start | bytes 122888 | tf_op jit(solution)/shard_map/ppermute | solution.py:57
  19.2 6.4 %collective-permute-start.9 = (f32[16,640]{1,0:T(8,128)S(1)}, f32[16,640]{1,0:T(8,128)S(1)}, u32[]{:S(2)}, u32[]{:S(2)}) collective-permute-start(f32[16,640]{1,0:T(8,128)S(1)} %add.1.a_ref), channel_id=1, source_target_pairs={{64,0},{72,8},{80,16},{88,24},{96,32},{104,40},{112,48},{120,56},{... | collective-permute-start | bytes 122888 | tf_op jit(solution)/shard_map/ppermute | solution.py:57
  22.9 4.1 %collective-permute-start.8 = (f32[16,640]{1,0:T(8,128)S(1)}, f32[16,640]{1,0:T(8,128)S(1)}, u32[]{:S(2)}, u32[]{:S(2)}) collective-permute-start(f32[16,640]{1,0:T(8,128)S(1)} %add.1.a_ref), channel_id=1, source_target_pairs={{96,0},{104,8},{112,16},{120,24},{0,32},{8,40},{16,48},{24,56},{32... | collective-permute-start | bytes 122888 | tf_op jit(solution)/shard_map/ppermute | solution.py:57
  23.6 3.3 %collective-permute-start.7 = (f32[16,640]{1,0:T(8,128)S(1)}, f32[16,640]{1,0:T(8,128)S(1)}, u32[]{:S(2)}, u32[]{:S(2)}) collective-permute-start(f32[16,640]{1,0:T(8,128)S(1)} %add.1.a_ref), channel_id=1, source_target_pairs={{32,0},{40,8},{48,16},{56,24},{64,32},{72,40},{80,48},{88,56},{96,... | collective-permute-start | bytes 122888 | tf_op jit(solution)/shard_map/ppermute | solution.py:57
  27.0 12.7 %collective-permute-start.16 = (bf16[64,4096]{1,0:T(8,128)(2,1)S(1)}, bf16[64,4096]{1,0:T(8,128)(2,1)S(1)}, u32[]{:S(2)}, u32[]{:S(2)}) collective-permute-start(bf16[64,4096]{1,0:T(8,128)(2,1)S(1)} %both.1), channel_id=1, source_target_pairs={{1,0},{0,1},{3,2},{2,3},{5,4},{4,5},{7,6},{6,7},{9,8},{8,9},{11,10... | collective-permute-start | bytes 1572872 | tf_op jit(solution)/shard_map/ppermute | solution.py:40
  29.6 7.2 %collective-permute-start.17 = (bf16[16,4096]{1,0:T(8,128)(2,1)S(1)}, bf16[16,4096]{1,0:T(8,128)(2,1)S(1)}, u32[]{:S(2)}, u32[]{:S(2)}) collective-permute-start(bf16[16,4096]{1,0:T(8,128)(2,1)S(1)} %relay.1), channel_id=1, source_target_pairs={{6,0},{3,1},{0,2},{5,3},{2,4},{7,5},{4,6},{1,7},{14,8},{11,9},{8,1... | collective-permute-start | bytes 393224 | tf_op jit(solution)/shard_map/ppermute | solution.py:40
  31.8 4.9 %collective-permute-start.12 = (bf16[16,896]{1,0:T(8,128)(2,1)S(1)}, bf16[16,896]{1,0:T(8,128)(2,1)S(1)}, u32[]{:S(2)}, u32[]{:S(2)}) collective-permute-start(bf16[16,896]{1,0:T(8,128)(2,1)S(1)} %total.1.refs_0_._), channel_id=1, source_target_pairs={{4,0},{5,1},{6,2},{7,3},{0,4},{1,5},{2,6},{3,7},{12,8},{13,9},{14,... | collective-permute-start | bytes 86024 | tf_op jit(solution)/shard_map/ppermute | solution.py:57
  32.4 4.3 %collective-permute-start.11 = (bf16[16,896]{1,0:T(8,128)(2,1)S(1)}, bf16[16,896]{1,0:T(8,128)(2,1)S(1)}, u32[]{:S(2)}, u32[]{:S(2)}) collective-permute-start(bf16[16,896]{1,0:T(8,128)(2,1)S(1)} %total.1.refs_0_._), channel_id=1, source_target_pairs={{6,0},{7,1},{0,2},{1,3},{2,4},{3,5},{4,6},{5,7},{14,8},{15,9},{8,1... | collective-permute-start | bytes 86024 | tf_op jit(solution)/shard_map/ppermute | solution.py:57
  33.2 3.6 %collective-permute-start.10 = (bf16[16,896]{1,0:T(8,128)(2,1)S(1)}, bf16[16,896]{1,0:T(8,128)(2,1)S(1)}, u32[]{:S(2)}, u32[]{:S(2)}) collective-permute-start(bf16[16,896]{1,0:T(8,128)(2,1)S(1)} %total.1.refs_0_._), channel_id=1, source_target_pairs={{2,0},{3,1},{4,2},{5,3},{6,4},{7,5},{0,6},{1,7},{10,8},{11,9},{12,... | collective-permute-start | bytes 86024 | tf_op jit(solution)/shard_map/ppermute | solution.py:57
  36.8 2.9 %collective-permute-start.18 = (bf16[16,4096]{1,0:T(8,128)(2,1)S(1)}, bf16[16,4096]{1,0:T(8,128)(2,1)S(1)}, u32[]{:S(2)}, u32[]{:S(2)}) collective-permute-start(bf16[16,4096]{1,0:T(8,128)(2,1)S(1)} %later.1), channel_id=1, source_target_pairs={{1,0},{0,1},{3,2},{2,3},{5,4},{4,5},{7,6},{6,7},{9,8},{8,9},{11,10... | collective-permute-start | bytes 393224 | tf_op jit(solution)/shard_map/ppermute | solution.py:40
  38.8 1.3 %collective-permute-start.13 = (bf16[64,896]{1,0:T(8,128)(2,1)S(1)}, bf16[64,896]{1,0:T(8,128)(2,1)S(1)}, u32[]{:S(2)}, u32[]{:S(2)}) collective-permute-start(bf16[64,896]{1,0:T(8,128)(2,1)S(1)} %collect.1._.refs_0_), channel_id=1, source_target_pairs={{1,0},{0,1},{3,2},{2,3},{5,4},{4,5},{7,6},{6,7},{9,8},{8,9},{11,10... | collective-permute-start | bytes 344072 | tf_op jit(solution)/shard_map/ppermute | solution.py:40

commit v3 on v2

--- a/solution.py
+++ b/solution.py
@@ -10,6 +10,7 @@
 F32 = jnp.float32
 BF16 = jnp.bfloat16
 CORES = 2
+SIDE = 4
 LEAD_WORK = 1 << 33
 
 
@@ -36,49 +37,84 @@
     return pl.CostEstimate(flops=flops, bytes_accessed=traffic, transcendentals=0)
 
 
-def permute(value, source):
-    return lax.ppermute(value, "samp", [(source(n), n) for n in range(lax.axis_size("samp"))])
+def parity(row):
+    return (row // SIDE + row % SIDE) % 2
+
+
+def place(row, chip, role):
+    return (row * SIDE + chip) * CORES + (role ^ parity(row))
+
+
+def move(value, source):
+    everyone = [
+        (row, chip, role)
+        for row in range(lax.axis_size("rows"))
+        for chip in range(SIDE)
+        for role in range(CORES)
+    ]
+    pairs = [(place(*source(*one)), place(*one)) for one in everyone]
+    return lax.ppermute(value, ("rows", "samp"), pairs)
 
 
 def chip_step(value, step):
-    groups = lax.axis_size("samp")
-    return permute(value, lambda n: (n + step * CORES) % groups)
+    return move(value, lambda row, chip, role: (row, (chip + step) % SIDE, role ^ parity(row)))
 
 
 def sibling(value):
-    return permute(value, lambda n: n ^ 1)
-
-
-def around(value, stride, axis="rows"):
-    size, span = lax.axis_size(axis), 4 * stride
-    steps = [
-        [(n // span * span + (n + step * stride) % span, n) for n in range(size)] for step in (1, 3, 2)
-    ]
-    first, last, opposite = [lax.ppermute(value, axis, pairs) for pairs in steps]
+    return move(value, lambda row, chip, role: (row, chip, 1 - role))
+
+
+def beside_step(value):
+    return move(value, lambda row, chip, role: (row, (chip + 2 * role - 1) % SIDE, role))
+
+
+def around(value, axis):
+    def source(step):
+        def of(row, chip, role):
+            z, y = divmod(row, SIDE)
+            if axis == "y":
+                return z * SIDE + (y + step) % SIDE, chip, role
+            if axis == "z":
+                return (z + step) % SIDE * SIDE + y, chip, role
+            return row, (chip + step) % SIDE, 1 - role
+
+        return of
+
+    first, last, opposite = [move(value, source(step)) for step in (1, 3, 2)]
     return [value, first, last, opposite]
+
+
+def whereabouts():
+    own, row = lax.axis_index("samp"), lax.axis_index("rows")
+    chip, core = own // CORES, lax.rem(own, CORES)
+    return chip, core, lax.rem(core + row // SIDE + lax.rem(row, SIDE), 2)
 
 
 def rows_at(place, height):
     return pl.ds(pl.multiple_of(place * height, height), height)
+
+
+def by_role(own_ref, sibling_ref):
+    _, core, role = whereabouts()
+    own, other = own_ref[...], sibling_ref[...]
+    return jnp.where(core == role, own, other), jnp.where(core == role, other, own)
 
 
 def gram_kernel(
     part_ref, own_ref, sibling_ref, before_ref, before_sibling_ref, after_ref, message_ref
 ):
     height, columns = part_ref.shape
-    chips = lax.axis_size("samp") // CORES
-    chip = lax.axis_index("samp") // CORES
-    mine = jnp.concatenate([own_ref[...], sibling_ref[...]], axis=0)
-    others = jnp.concatenate([own_ref[...], after_ref[...]], axis=0)
-    near = dot(mine, others, ((1,), (1,)))
+    chip, _, _ = whereabouts()
+    mine = by_role(own_ref, sibling_ref)
+    others = jnp.concatenate([mine[0], after_ref[...]], axis=0)
+    near = dot(jnp.concatenate(mine, axis=0), others, ((1,), (1,)))
     place = lax.broadcasted_iota(jnp.int32, near.shape, 1) // height
     near = jnp.where(place == 0, 0.5 * near, near)
-    span = own_ref.shape[1] // 2
-    here = rows_at(chip // 2, span)
-    across = jnp.concatenate([before_ref[:, here], before_sibling_ref[:, here]], axis=0)
-    across = dot(across, after_ref[:, here], ((1,), (1,)))
+    half = rows_at(chip // 2, own_ref.shape[1] // 2)
+    across = jnp.concatenate([before_ref[:, half], before_sibling_ref[:, half]], axis=0)
+    across = dot(across, after_ref[:, half], ((1,), (1,)))
     gram = jnp.concatenate([near, across, jnp.zeros(across.shape, F32)], axis=1)
-    gram = pltpu.roll(jnp.concatenate([gram, gram], axis=1), chip * height, 1)[:, : chips * height]
+    gram = pltpu.roll(jnp.concatenate([gram, gram], axis=1), chip * height, 1)[:, : SIDE * height]
     message_ref[:, :columns] = part_ref[...]
     message_ref[:, columns:] = jnp.concatenate([gram[:height], gram[height:]], axis=1)
 
@@ -86,9 +122,9 @@
 def collect_kernel(*refs):
     *blocks, out_ref = refs
     height = blocks[0].shape[0]
-    chip = lax.axis_index("samp") // CORES
+    chip, _, _ = whereabouts()
     for step, block in zip((0, 1, 3, 2), blocks):
-        out_ref[rows_at(lax.rem(chip + step, len(blocks)), height), :] = block[...]
+        out_ref[rows_at(lax.rem(chip + step, SIDE), height), :] = block[...]
 
 
 def lead_kernel(out_ref):
@@ -99,65 +135,65 @@
     out_ref[...] = value_ref[...]
 
 
-def part_kernel(stream_ref, probe_ref, part_ref):
-    part_ref[...] = dot(stream_ref[...], probe_ref[...], ((1,), (1,)))
+def part_kernel(stream_ref, sibling_ref, probe_ref, part_ref):
+    stream, _ = by_role(stream_ref, sibling_ref)
+    part_ref[...] = dot(stream, probe_ref[...], ((1,), (1,)))
 
 
 def beside_kernel(own_ref, sibling_ref, before_ref, after_ref, _, out_ref):
     height = own_ref.shape[0]
-    core = lax.rem(lax.axis_index("samp"), CORES)
+    _, core, role = whereabouts()
     out_ref[rows_at(core, height), :] = own_ref[...]
     out_ref[rows_at(1 - core, height), :] = sibling_ref[...]
 
-    @pl.when(core == 0)
+    @pl.when(role == 0)
     def _():
         out_ref[CORES * height :] = before_ref[...]
 
-    @pl.when(core == 1)
+    @pl.when(role == 1)
     def _():
         out_ref[CORES * height :] = after_ref[...]
 
 
 def relay_kernel(beside_ref, _, out_ref):
-    core = lax.rem(lax.axis_index("samp"), CORES)
-    out_ref[...] = beside_ref[rows_at(core, out_ref.shape[0]), :]
-
-
-def both_kernel(beside_ref, after_ref, _, out_ref):
+    _, _, role = whereabouts()
+    out_ref[...] = beside_ref[rows_at(role, out_ref.shape[0]), :]
+
+
+def both_kernel(beside_ref, after_ref, across_ref, _, out_ref):
     height = after_ref.shape[0]
-    out_ref[:-height] = beside_ref[...]
-    out_ref[-height:] = after_ref[...]
+    out_ref[: -2 * height] = beside_ref[...]
+    out_ref[-2 * height : -height] = after_ref[...]
+    out_ref[-height:] = across_ref[...]
 
 
 def order_kernel(
     temp_ref, temp_sibling_ref, before_ref, before_sibling_ref, after_ref, stream_ref, stream_sibling_ref,
-    beside_ref, both_ref, across_ref, across_sibling_ref, out_ref,
+    beside_ref, both_ref, across_ref, out_ref,
 ):
-    own = lax.axis_index("samp")
-    chip, core = own // CORES, lax.rem(own, CORES)
+    chip, core, role = whereabouts()
     height = temp_ref.shape[0]
-    chips = out_ref.shape[0] // (2 * CORES * height)
 
     def put(base, owner, step, value):
-        place = (base * CORES + owner) * chips + lax.rem(chip + step, chips)
+        place = (base * CORES + owner) * SIDE + lax.rem(chip + step, SIDE)
         out_ref[rows_at(place, height), :] = value
 
-    rows = [slice(n * height, (n + 1) * height) for n in range(2 * CORES)]
+    rows = [slice(n * height, (n + 1) * height) for n in range(5)]
     put(0, core, 0, temp_ref[...])
     put(0, 1 - core, 0, temp_sibling_ref[...])
-    put(0, core, chips - 1, before_ref[...])
-    put(0, 1 - core, chips - 1, before_sibling_ref[...])
-    put(0, core, 1, after_ref[...])
-    put(0, 1 - core, 1, both_ref[rows[3]])
-    put(0, core, 2, beside_ref[rows[2]])
-    put(0, 1 - core, 2, both_ref[rows[2]])
+    put(0, role, SIDE - 1, before_ref[...])
+    put(0, 1 - role, SIDE - 1, before_sibling_ref[...])
+    put(0, role, 1, after_ref[...])
+    put(0, 1 - role, 1, both_ref[rows[3]])
+    put(0, role, 2, beside_ref[rows[2]])
+    put(0, 1 - role, 2, both_ref[rows[2]])
     put(1, core, 0, stream_ref[...])
     put(1, 1 - core, 0, stream_sibling_ref[...])
     for n in range(CORES):
-        put(1, n, chips - 1 - core * (chips - 2), beside_ref[rows[n]])
-        put(1, n, 1 + core * (chips - 2), both_ref[rows[n]])
-    put(1, core, 2, across_ref[...])
-    put(1, 1 - core, 2, across_sibling_ref[...])
+        put(1, n, SIDE - 1 - role * (SIDE - 2), beside_ref[rows[n]])
+        put(1, n, 1 + role * (SIDE - 2), both_ref[rows[n]])
+    put(1, role, 2, across_ref[...])
+    put(1, 1 - role, 2, both_ref[rows[4]])
 
 
 def add_kernel(a_ref, b_ref, c_ref, d_ref, out_ref):
@@ -177,9 +213,13 @@
     samples = CORES * half
     image_scale, back_scale, total_rows = scales
     own = lax.axis_index("samp")
-    core = lax.rem(own, CORES)
-    message[rows_at(core, half), :] = near_ref[...]
-    message[rows_at(1 - core, half), :] = far_ref[...]
+    height = half // SIDE
+    chip, _, role = whereabouts()
+    for n in range(SIDE):
+        owner = jnp.where(chip == n, role, 1 - role)
+        rows = slice(n * height, (n + 1) * height)
+        message[rows_at(owner * SIDE + n, height), :] = near_ref[rows]
+        message[rows_at((1 - owner) * SIDE + n, height), :] = far_ref[rows]
     turned = message[:, :columns].astype(F32).T
     left[...] = turned.astype(BF16)
     products = sum(
@@ -190,7 +230,6 @@
     bottom = jnp.where(first, products[half:], products[:half])
     bottom = jnp.concatenate([bottom[:, half:], bottom[:, :half]], axis=1)
     gram = jnp.concatenate([top, bottom], axis=0)
-    height = samples // lax.axis_size("samp")
     row, lane = [lax.broadcasted_iota(jnp.int32, gram.shape, axis) // height for axis in (0, 1)]
     chips = half // height
     moves = lax.rem(lane + 2 * chips - row - 2, chips) == 0
@@ -264,7 +303,7 @@
     temp_sibling = sibling(temp_slab)
     stream_sibling = sibling(stream_slab)
     (part,) = call(
-        part_kernel, "part", [stream_slab, probe], [((height, columns), F32)], work=2 * height * columns * local_rows
+        part_kernel, "part", [stream_slab, stream_sibling, probe], [((height, columns), F32)], work=2 * height * columns * local_rows
     )
     (before_copy,) = call(copy_kernel, "before", [before, part], [slab])
     before_sibling = sibling(before_copy)
@@ -281,25 +320,23 @@
         [stream_slab, stream_sibling, before, after, message],
         [((3 * height, local_rows), BF16)],
     )
-    beside = permute(beside, lambda n: (n - CORES if n % CORES == 0 else n + CORES) % groups)
-    (message,) = call(add_kernel, "add", around(message, 1), [((height, wide), F32)])
+    beside = beside_step(beside)
+    (message,) = call(add_kernel, "add", around(message, "y"), [((height, wide), F32)])
+    (across,) = call(relay_kernel, "relay", [beside, message], [slab])
+    across = beside_step(across)
     (message,) = call(
-        functools.partial(sum_kernel, columns), "total", around(message, 4), [((height, packed), BF16)]
-    )
-    (across,) = call(relay_kernel, "relay", [beside, message], [slab])
-    across = permute(across, lambda n: (n - CORES if n % CORES == 0 else n + CORES) % groups)
-    (both,) = call(both_kernel, "both", [beside, after, message], [((4 * height, local_rows), BF16)])
+        functools.partial(sum_kernel, columns), "total", around(message, "z"), [((height, packed), BF16)]
+    )
+    (both,) = call(both_kernel, "both", [beside, after, across, message], [((5 * height, local_rows), BF16)])
     both_sibling = sibling(both)
-    (message,) = call(collect_kernel, "collect", around(message, CORES, "samp"), [((half, packed), BF16)])
+    (message,) = call(collect_kernel, "collect", around(message, "x"), [((half, packed), BF16)])
     message_other = sibling(message)
-    (later,) = call(copy_kernel, "later", [across, message], [slab])
-    across_sibling = sibling(later)
     (slabs,) = call(
         order_kernel,
         "order",
         [
             temp_slab, temp_sibling, before, before_sibling, after, stream_slab, stream_sibling,
-            beside, both_sibling, across, across_sibling,
+            beside, both_sibling, across,
         ],
         [((2 * samples, local_rows), BF16)],
     )

time: 43.5 us -> 41.5 us (0.954)
  starting transfers between devices: 30 us -> 26.4 us
  waiting for transfers between devices: 7.34 us -> 8.88 us
    ppermute x19 -> x18, starting transfers between devices: 30 us -> 26.4 us  [move(): return lax.ppermute(value, ('rows', 'samp'), pairs)]
    ppermute x19 -> x18, waiting for transfers between devices: 7.34 us -> 8.88 us  [move(): return lax.ppermute(value, ('rows', 'samp'), pairs)]
    pallas_call x13 -> x12, Pallas kernels: 2.02 us -> 2.05 us  [call(): pl.pallas_call(kernel, out_shape=tuple(outs), in_specs=whole(len(operands...]
  transfers between devices with their start and end apart: 19 -> 18, of which waited for: 9 -> 10; matrix products, arithmetic and copies ran while one was open for 0% -> 0% of each run, Pallas kernels for 4% -> 3%
where the time goes in v3:
time: 41.5 us; the launch traced here: 41.4 us
  starting transfers between devices  26.4 us (64%)
  waiting for transfers between devices  8.88 us (21%)
  Pallas kernels  5.36 us (13%)
  between operations  0.75 us (2%)
    ppermute x18, starting transfers between devices, move(): return lax.ppermute(value, ('rows', 'samp'), pairs)  26.4 us
    ppermute x18, waiting for transfers between devices, move(): return lax.ppermute(value, ('rows', 'samp'), pairs)  8.88 us
    pallas_call x1, Pallas kernels, shards(): pl.pallas_call(functools.partial(output_kernel, columns, scales), out_sha...  3.31 us
    pallas_call x12, Pallas kernels, call(): pl.pallas_call(kernel, out_shape=tuple(outs), in_specs=whole(len(operands...  2.05 us
  transfers between devices with their start and end apart: 18, of which 10 were waited for; matrix products, arithmetic and copies ran while one was open for 0% of the time, Pallas kernels for 3%

profile of v3, /device:TPU:1, one launch (start us, length us, event | category | flops | bytes accessed | tf_op | source)
XLA Modules:
  0.0 41.4 jit_solution(7651499940298957220)
XLA Ops:
  0.6 0.0 copy-start.1
  0.6 0.0 copy-start.2
  0.6 0.0 copy-start
  0.7 2.1 %collective-permute-start.2 = (bf16[16,4096]{1,0:T(8,128)(2,1)}, bf16[16,4096]{1,0:T(8,128)(2,1)S(1)}, u32[]{:S(2)}, u32[]{:S(2)}) collective-permute-start(bf16[16,4096]{1,0:T(8,128)(2,1)} %temp_ref.1), channel_id=1, source_target_pairs={{6,0},{7,1},{0,2},{1,3},{2,4},{3,5},{4,6},{5,7},{14,9},{15,8},{8,1... | collective-permute-start | bytes 393224 | tf_op jit(solution)/shard_map/ppermute | solution.py:56
  2.8 1.0 %collective-permute-start.1 = (bf16[16,4096]{1,0:T(8,128)(2,1)}, bf16[16,4096]{1,0:T(8,128)(2,1)S(1)}, u32[]{:S(2)}, u32[]{:S(2)}) collective-permute-start(bf16[16,4096]{1,0:T(8,128)(2,1)} %temp_ref.1), channel_id=1, source_target_pairs={{1,0},{0,1},{3,2},{2,3},{5,4},{4,5},{7,6},{6,7},{8,9},{9,8},{10,11... | collective-permute-start | bytes 393224 | tf_op jit(solution)/shard_map/ppermute | solution.py:56
  3.7 0.0 collective-permute-start
  3.7 0.0 copy-done.1
  3.7 1.5 %collective-permute-start.4 = (bf16[16,4096]{1,0:T(8,128)(2,1)S(1)}, bf16[16,4096]{1,0:T(8,128)(2,1)S(1)}, u32[]{:S(2)}, u32[]{:S(2)}) collective-permute-start(bf16[16,4096]{1,0:T(8,128)(2,1)S(1)} %ahead.1), channel_id=1, source_target_pairs={{2,0},{3,1},{4,2},{5,3},{6,4},{7,5},{0,6},{1,7},{10,9},{11,8},{12,... | collective-permute-start | bytes 393224 | tf_op jit(solution)/shard_map/ppermute | solution.py:56
  5.2 0.1 collective-permute-done.sibling_ref.stream_sibling_ref
  5.3 0.0 copy-done.2
  5.3 0.0 copy-done
  5.3 1.2 %part.1._.part_ref = f32[16,512]{1,0:T(8,128)S(1)} custom-call(bf16[16,4096]{1,0:T(8,128)(2,1)S(1)} %copy-done.2, bf16[16,4096]{1,0:T(8,128)(2,1)S(1)} %collective-permute-done.sibling_ref.stream_sibling_ref, bf16[512,4096]{1,0:T(8,128)(2,1)S(1)} %copy-done), custom_call_target="tpu_custom_call" | custom-call | flops 67108864 | bytes 4489216 | tf_op jit(solution)/shard_map/part/pallas_call | solution.py:285
  6.5 0.6 %collective-permute-done.2.value_ref.before_ref = bf16[16,4096]{1,0:T(8,128)(2,1)S(1)} collective-permute-done((bf16[16,4096]{1,0:T(8,128)(2,1)}, bf16[16,4096]{1,0:T(8,128)(2,1)S(1)}, u32[]{:S(2)}, u32[]{:S(2)}) %collective-permute-start.2) | collective-permute-done | bytes 131104 | tf_op jit(solution)/shard_map/ppermute | solution.py:56
  7.0 1.8 %collective-permute-start.3 = (bf16[16,4096]{1,0:T(8,128)(2,1)S(1)}, bf16[16,4096]{1,0:T(8,128)(2,1)S(1)}, u32[]{:S(2)}, u32[]{:S(2)}) collective-permute-start(bf16[16,4096]{1,0:T(8,128)(2,1)S(1)} %before.1), channel_id=1, source_target_pairs={{1,0},{0,1},{3,2},{2,3},{5,4},{4,5},{7,6},{6,7},{8,9},{9,8},{10,11... | collective-permute-start | bytes 393224 | tf_op jit(solution)/shard_map/ppermute | solution.py:56
  8.8 0.0 collective-permute-done.4.after_ref
  8.8 0.0 collective-permute-done.1.sibling_ref.temp_sibling_ref
  8.8 1.0 %collective-permute-done.3.before_sibling_ref = bf16[16,4096]{1,0:T(8,128)(2,1)S(1)} collective-permute-done((bf16[16,4096]{1,0:T(8,128)(2,1)S(1)}, bf16[16,4096]{1,0:T(8,128)(2,1)S(1)}, u32[]{:S(2)}, u32[]{:S(2)}) %collective-permute-start.3) | collective-permute-done | bytes 131104 | tf_op jit(solution)/shard_map/ppermute | solution.py:56
  9.8 0.5 %gram.1.a_ref._ = f32[16,640]{1,0:T(8,128)S(1)} custom-call(f32[16,512]{1,0:T(8,128)S(1)} %part.1._.part_ref, bf16[16,4096]{1,0:T(8,128)(2,1)S(1)} %copy-done.1, bf16[16,4096]{1,0:T(8,128)(2,1)S(1)} %collective-permute-done.1.sibling_ref.temp_sibling_ref, bf16[16,4096]{1,0:T(8,128)(2,1)S(1)} %collective-permute-done.2.value_ref.before_ref, ...), custom_call_target="tpu_custom_call" | custom-call | flops 16777216 | bytes 729088 | tf_op jit(solution)/shard_map/gram/pallas_call | solution.py:285
  10.3 0.1 beside.1
  10.3 1.5 %collective-permute-start.15 = (bf16[48,4096]{1,0:T(8,128)(2,1)S(1)}, bf16[48,4096]{1,0:T(8,128)(2,1)S(1)}, u32[]{:S(2)}, u32[]{:S(2)}) collective-permute-start(bf16[48,4096]{1,0:T(8,128)(2,1)S(1)} %beside.1), channel_id=1, source_target_pairs={{6,0},{3,1},{0,2},{5,3},{2,4},{7,5},{4,6},{1,7},{15,9},{10,8},{9,1... | collective-permute-start | bytes 1179656 | tf_op jit(solution)/shard_map/ppermute | solution.py:56
  11.9 2.9 %collective-permute-start.7 = (f32[16,640]{1,0:T(8,128)S(1)}, f32[16,640]{1,0:T(8,128)S(1)}, u32[]{:S(2)}, u32[]{:S(2)}) collective-permute-start(f32[16,640]{1,0:T(8,128)S(1)} %gram.1.a_ref._), channel_id=1, source_target_pairs={{16,0},{17,1},{18,2},{19,3},{20,4},{21,5},{22,6},{23,7},{25,9},{24... | collective-permute-start | bytes 122888 | tf_op jit(solution)/shard_map/ppermute | solution.py:56
  14.8 1.8 %collective-permute-start.6 = (f32[16,640]{1,0:T(8,128)S(1)}, f32[16,640]{1,0:T(8,128)S(1)}, u32[]{:S(2)}, u32[]{:S(2)}) collective-permute-start(f32[16,640]{1,0:T(8,128)S(1)} %gram.1.a_ref._), channel_id=1, source_target_pairs={{25,0},{24,1},{27,2},{26,3},{29,4},{28,5},{31,6},{30,7},{0,9},{1,8... | collective-permute-start | bytes 122888 | tf_op jit(solution)/shard_map/ppermute | solution.py:56
  16.6 1.1 %collective-permute-start.5 = (f32[16,640]{1,0:T(8,128)S(1)}, f32[16,640]{1,0:T(8,128)S(1)}, u32[]{:S(2)}, u32[]{:S(2)}) collective-permute-start(f32[16,640]{1,0:T(8,128)S(1)} %gram.1.a_ref._), channel_id=1, source_target_pairs={{9,0},{8,1},{11,2},{10,3},{13,4},{12,5},{15,6},{14,7},{16,9},{17,8... | collective-permute-start | bytes 122888 | tf_op jit(solution)/shard_map/ppermute | solution.py:56
  17.8 0.0 collective-permute-done.7.d_ref
  17.8 1.7 %collective-permute-done.6.c_ref = f32[16,640]{1,0:T(8,128)S(1)} collective-permute-done((f32[16,640]{1,0:T(8,128)S(1)}, f32[16,640]{1,0:T(8,128)S(1)}, u32[]{:S(2)}, u32[]{:S(2)}) %collective-permute-start.6) | collective-permute-done | bytes 40992 | tf_op jit(solution)/shard_map/ppermute | solution.py:56
  19.5 0.6 %collective-permute-done.5.b_ref = f32[16,640]{1,0:T(8,128)S(1)} collective-permute-done((f32[16,640]{1,0:T(8,128)S(1)}, f32[16,640]{1,0:T(8,128)S(1)}, u32[]{:S(2)}, u32[]{:S(2)}) %collective-permute-start.5) | collective-permute-done | bytes 40992 | tf_op jit(solution)/shard_map/ppermute | solution.py:56
  20.1 0.0 collective-permute-done.15.beside_ref
  20.1 0.9 %collective-permute-start.16 = (bf16[16,4096]{1,0:T(8,128)(2,1)S(1)}, bf16[16,4096]{1,0:T(8,128)(2,1)S(1)}, u32[]{:S(2)}, u32[]{:S(2)}) collective-permute-start(bf16[16,4096]{1,0:T(8,128)(2,1)S(1)} %relay.1), channel_id=1, source_target_pairs={{6,0},{3,1},{0,2},{5,3},{2,4},{7,5},{4,6},{1,7},{15,9},{10,8},{9,1... | collective-permute-start | bytes 393224 | tf_op jit(solution)/shard_map/ppermute | solution.py:56
  21.1 3.6 %collective-permute-start.10 = (f32[16,640]{1,0:T(8,128)S(1)}, f32[16,640]{1,0:T(8,128)S(1)}, u32[]{:S(2)}, u32[]{:S(2)}) collective-permute-start(f32[16,640]{1,0:T(8,128)S(1)} %add.1.a_ref._), channel_id=1, source_target_pairs={{64,0},{65,1},{66,2},{67,3},{68,4},{69,5},{70,6},{71,7},{73,9},{72... | collective-permute-start | bytes 122888 | tf_op jit(solution)/shard_map/ppermute | solution.py:56
  24.7 2.0 %collective-permute-start.9 = (f32[16,640]{1,0:T(8,128)S(1)}, f32[16,640]{1,0:T(8,128)S(1)}, u32[]{:S(2)}, u32[]{:S(2)}) collective-permute-start(f32[16,640]{1,0:T(8,128)S(1)} %add.1.a_ref._), channel_id=1, source_target_pairs={{97,0},{96,1},{99,2},{98,3},{101,4},{100,5},{103,6},{102,7},{104,9... | collective-permute-start | bytes 122888 | tf_op jit(solution)/shard_map/ppermute | solution.py:56
  26.7 0.9 %collective-permute-start.8 = (f32[16,640]{1,0:T(8,128)S(1)}, f32[16,640]{1,0:T(8,128)S(1)}, u32[]{:S(2)}, u32[]{:S(2)}) collective-permute-start(f32[16,640]{1,0:T(8,128)S(1)} %add.1.a_ref._), channel_id=1, source_target_pairs={{33,0},{32,1},{35,2},{34,3},{37,4},{36,5},{39,6},{38,7},{40,9},{41... | collective-permute-start | bytes 122888 | tf_op jit(solution)/shard_map/ppermute | solution.py:56
  27.6 0.0 collective-permute-done.10.d_ref
  27.6 1.9 %collective-permute-done.9.c_ref = f32[16,640]{1,0:T(8,128)S(1)} collective-permute-done((f32[16,640]{1,0:T(8,128)S(1)}, f32[16,640]{1,0:T(8,128)S(1)}, u32[]{:S(2)}, u32[]{:S(2)}) %collective-permute-start.9) | collective-permute-done | bytes 40992 | tf_op jit(solution)/shard_map/ppermute | solution.py:56
  29.5 0.6 %collective-permute-done.8.b_ref = f32[16,640]{1,0:T(8,128)S(1)} collective-permute-done((f32[16,640]{1,0:T(8,128)S(1)}, f32[16,640]{1,0:T(8,128)S(1)}, u32[]{:S(2)}, u32[]{:S(2)}) %collective-permute-start.8) | collective-permute-done | bytes 40992 | tf_op jit(solution)/shard_map/ppermute | solution.py:56
  30.2 0.0 collective-permute-done.16.across_ref
  30.2 0.1 collective-permute-start.17
  30.3 1.7 %collective-permute-start.13 = (bf16[16,896]{1,0:T(8,128)(2,1)S(1)}, bf16[16,896]{1,0:T(8,128)(2,1)S(1)}, u32[]{:S(2)}, u32[]{:S(2)}) collective-permute-start(bf16[16,896]{1,0:T(8,128)(2,1)S(1)} %total.1.refs_0_._), channel_id=1, source_target_pairs={{5,0},{4,1},{7,2},{6,3},{1,4},{0,5},{3,6},{2,7},{12,9},{13,8},{14,... | collective-permute-start | bytes 86024 | tf_op jit(solution)/shard_map/ppermute | solution.py:56
  32.0 0.5 %collective-permute-start.12 = (bf16[16,896]{1,0:T(8,128)(2,1)S(1)}, bf16[16,896]{1,0:T(8,128)(2,1)S(1)}, u32[]{:S(2)}, u32[]{:S(2)}) collective-permute-start(bf16[16,896]{1,0:T(8,128)(2,1)S(1)} %total.1.refs_0_._), channel_id=1, source_target_pairs={{7,0},{6,1},{1,2},{0,3},{3,4},{2,5},{5,6},{4,7},{14,9},{15,8},{8,1... | collective-permute-start | bytes 86024 | tf_op jit(solution)/shard_map/ppermute | solution.py:56
  32.6 2.4 %collective-permute-start.11 = (bf16[16,896]{1,0:T(8,128)(2,1)S(1)}, bf16[16,896]{1,0:T(8,128)(2,1)S(1)}, u32[]{:S(2)}, u32[]{:S(2)}) collective-permute-start(bf16[16,896]{1,0:T(8,128)(2,1)S(1)} %total.1.refs_0_._), channel_id=1, source_target_pairs={{3,0},{2,1},{5,2},{4,3},{7,4},{6,5},{1,6},{0,7},{10,9},{11,8},{12,... | collective-permute-start | bytes 86024 | tf_op jit(solution)/shard_map/ppermute | solution.py:56
  35.0 0.2 collective-permute-done.13.refs_3_
  35.3 1.4 %collective-permute-done.12.refs_2_ = bf16[16,896]{1,0:T(8,128)(2,1)S(1)} collective-permute-done((bf16[16,896]{1,0:T(8,128)(2,1)S(1)}, bf16[16,896]{1,0:T(8,128)(2,1)S(1)}, u32[]{:S(2)}, u32[]{:S(2)}) %collective-permute-start.12) | collective-permute-done | bytes 28704 | tf_op jit(solution)/shard_map/ppermute | solution.py:56
  36.6 0.0 collective-permute-done.11.refs_1_
  36.7 0.5 %collective-permute-start.14 = (bf16[64,896]{1,0:T(8,128)(2,1)S(1)}, bf16[64,896]{1,0:T(8,128)(2,1)S(1)}, u32[]{:S(2)}, u32[]{:S(2)}) collective-permute-start(bf16[64,896]{1,0:T(8,128)(2,1)S(1)} %collect.1.refs_0_), channel_id=1, source_target_pairs={{1,0},{0,1},{3,2},{2,3},{5,4},{4,5},{7,6},{6,7},{8,9},{9,8},{10,11... | collective-permute-start | bytes 344072 | tf_op jit(solution)/shard_map/ppermute | solution.py:56
  37.1 0.0 collective-permute-done.17.both_ref
  37.1 0.2 order.1.refs_2_
  37.3 0.8 %collective-permute-done.14.refs_1_ = bf16[64,896]{1,0:T(8,128)(2,1)S(1)} collective-permute-done((bf16[64,896]{1,0:T(8,128)(2,1)S(1)}, bf16[64,896]{1,0:T(8,128)(2,1)S(1)}, u32[]{:S(2)}, u32[]{:S(2)}) %collective-permute-start.14) | collective-permute-done | bytes 114720 | tf_op jit(solution)/shard_map/ppermute | solution.py:56
  38.1 3.3 %outputs.1 = (bf16[512,4096]{1,0:T(8,128)(2,1)}, f32[64,4096]{1,0:T(8,128)}) custom-call(bf16[64,896]{1,0:T(8,128)(2,1)S(1)} %collect.1.refs_0_, bf16[64,896]{1,0:T(8,128)(2,1)S(1)} %collective-permute-done.14.refs_1_, bf16[256,4096]{1,0:T(8,128)(2,1)S(1)} %order.1.refs_2_), custom_call_target="tpu_custom_call" | custom-call | flops 603979776 | bytes 7340032 | tf_op jit(solution)/shard_map/outputs/pallas_call | solution.py:352
  (8 shorter events, 0.2 us)
Async XLA Ops:
  0.6 3.1 %copy-start.1 = (bf16[16,4096]{1,0:T(8,128)(2,1)S(1)}, bf16[16,4096]{1,0:T(8,128)(2,1)}, u32[]{:S(2)}) copy-start(bf16[16,4096]{1,0:T(8,128)(2,1)} %temp_ref.1) | copy-start | bytes 393220
  0.6 4.6 %copy-start.2 = (bf16[16,4096]{1,0:T(8,128)(2,1)S(1)}, bf16[16,4096]{1,0:T(8,128)(2,1)}, u32[]{:S(2)}) copy-start(bf16[16,4096]{1,0:T(8,128)(2,1)} %stream_ref.3) | copy-start | bytes 393220
  0.6 4.6 %copy-start = (bf16[512,4096]{1,0:T(8,128)(2,1)S(1)}, bf16[512,4096]{1,0:T(8,128)(2,1)}, u32[]{:S(2)}) copy-start(bf16[512,4096]{1,0:T(8,128)(2,1)} %probe_ref.1) | copy-start | bytes 12582916
  0.7 6.4 %collective-permute-start.2 = (bf16[16,4096]{1,0:T(8,128)(2,1)}, bf16[16,4096]{1,0:T(8,128)(2,1)S(1)}, u32[]{:S(2)}, u32[]{:S(2)}) collective-permute-start(bf16[16,4096]{1,0:T(8,128)(2,1)} %temp_ref.1), channel_id=1, source_target_pairs={{6,0},{7,1},{0,2},{1,3},{2,4},{3,5},{4,6},{5,7},{14,9},{15,8},{8,1... | collective-permute-start | bytes 393224 | tf_op jit(solution)/shard_map/ppermute | solution.py:56
  2.8 6.0 %collective-permute-start.1 = (bf16[16,4096]{1,0:T(8,128)(2,1)}, bf16[16,4096]{1,0:T(8,128)(2,1)S(1)}, u32[]{:S(2)}, u32[]{:S(2)}) collective-permute-start(bf16[16,4096]{1,0:T(8,128)(2,1)} %temp_ref.1), channel_id=1, source_target_pairs={{1,0},{0,1},{3,2},{2,3},{5,4},{4,5},{7,6},{6,7},{8,9},{9,8},{10,11... | collective-permute-start | bytes 393224 | tf_op jit(solution)/shard_map/ppermute | solution.py:56
  3.7 1.6 %collective-permute-start = (bf16[16,4096]{1,0:T(8,128)(2,1)}, bf16[16,4096]{1,0:T(8,128)(2,1)S(1)}, u32[]{:S(2)}, u32[]{:S(2)}) collective-permute-start(bf16[16,4096]{1,0:T(8,128)(2,1)} %stream_ref.3), channel_id=1, source_target_pairs={{1,0},{0,1},{3,2},{2,3},{5,4},{4,5},{7,6},{6,7},{8,9},{9,8},{10,11... | collective-permute-start | bytes 393224 | tf_op jit(solution)/shard_map/ppermute | solution.py:56
  3.7 5.0 %collective-permute-start.4 = (bf16[16,4096]{1,0:T(8,128)(2,1)S(1)}, bf16[16,4096]{1,0:T(8,128)(2,1)S(1)}, u32[]{:S(2)}, u32[]{:S(2)}) collective-permute-start(bf16[16,4096]{1,0:T(8,128)(2,1)S(1)} %ahead.1), channel_id=1, source_target_pairs={{2,0},{3,1},{4,2},{5,3},{6,4},{7,5},{0,6},{1,7},{10,9},{11,8},{12,... | collective-permute-start | bytes 393224 | tf_op jit(solution)/shard_map/ppermute | solution.py:56
  7.0 2.7 %collective-permute-start.3 = (bf16[16,4096]{1,0:T(8,128)(2,1)S(1)}, bf16[16,4096]{1,0:T(8,128)(2,1)S(1)}, u32[]{:S(2)}, u32[]{:S(2)}) collective-permute-start(bf16[16,4096]{1,0:T(8,128)(2,1)S(1)} %before.1), channel_id=1, source_target_pairs={{1,0},{0,1},{3,2},{2,3},{5,4},{4,5},{7,6},{6,7},{8,9},{9,8},{10,11... | collective-permute-start | bytes 393224 | tf_op jit(solution)/shard_map/ppermute | solution.py:56
  10.3 9.7 %collective-permute-start.15 = (bf16[48,4096]{1,0:T(8,128)(2,1)S(1)}, bf16[48,4096]{1,0:T(8,128)(2,1)S(1)}, u32[]{:S(2)}, u32[]{:S(2)}) collective-permute-start(bf16[48,4096]{1,0:T(8,128)(2,1)S(1)} %beside.1), channel_id=1, source_target_pairs={{6,0},{3,1},{0,2},{5,3},{2,4},{7,5},{4,6},{1,7},{15,9},{10,8},{9,1... | collective-permute-start | bytes 1179656 | tf_op jit(solution)/shard_map/ppermute | solution.py:56
  11.9 5.9 %collective-permute-start.7 = (f32[16,640]{1,0:T(8,128)S(1)}, f32[16,640]{1,0:T(8,128)S(1)}, u32[]{:S(2)}, u32[]{:S(2)}) collective-permute-start(f32[16,640]{1,0:T(8,128)S(1)} %gram.1.a_ref._), channel_id=1, source_target_pairs={{16,0},{17,1},{18,2},{19,3},{20,4},{21,5},{22,6},{23,7},{25,9},{24... | collective-permute-start | bytes 122888 | tf_op jit(solution)/shard_map/ppermute | solution.py:56
  14.8 4.7 %collective-permute-start.6 = (f32[16,640]{1,0:T(8,128)S(1)}, f32[16,640]{1,0:T(8,128)S(1)}, u32[]{:S(2)}, u32[]{:S(2)}) collective-permute-start(f32[16,640]{1,0:T(8,128)S(1)} %gram.1.a_ref._), channel_id=1, source_target_pairs={{25,0},{24,1},{27,2},{26,3},{29,4},{28,5},{31,6},{30,7},{0,9},{1,8... | collective-permute-start | bytes 122888 | tf_op jit(solution)/shard_map/ppermute | solution.py:56
  16.6 3.4 %collective-permute-start.5 = (f32[16,640]{1,0:T(8,128)S(1)}, f32[16,640]{1,0:T(8,128)S(1)}, u32[]{:S(2)}, u32[]{:S(2)}) collective-permute-start(f32[16,640]{1,0:T(8,128)S(1)} %gram.1.a_ref._), channel_id=1, source_target_pairs={{9,0},{8,1},{11,2},{10,3},{13,4},{12,5},{15,6},{14,7},{16,9},{17,8... | collective-permute-start | bytes 122888 | tf_op jit(solution)/shard_map/ppermute | solution.py:56
  20.1 10.0 %collective-permute-start.16 = (bf16[16,4096]{1,0:T(8,128)(2,1)S(1)}, bf16[16,4096]{1,0:T(8,128)(2,1)S(1)}, u32[]{:S(2)}, u32[]{:S(2)}) collective-permute-start(bf16[16,4096]{1,0:T(8,128)(2,1)S(1)} %relay.1), channel_id=1, source_target_pairs={{6,0},{3,1},{0,2},{5,3},{2,4},{7,5},{4,6},{1,7},{15,9},{10,8},{9,1... | collective-permute-start | bytes 393224 | tf_op jit(solution)/shard_map/ppermute | solution.py:56
  21.1 6.6 %collective-permute-start.10 = (f32[16,640]{1,0:T(8,128)S(1)}, f32[16,640]{1,0:T(8,128)S(1)}, u32[]{:S(2)}, u32[]{:S(2)}) collective-permute-start(f32[16,640]{1,0:T(8,128)S(1)} %add.1.a_ref._), channel_id=1, source_target_pairs={{64,0},{65,1},{66,2},{67,3},{68,4},{69,5},{70,6},{71,7},{73,9},{72... | collective-permute-start | bytes 122888 | tf_op jit(solution)/shard_map/ppermute | solution.py:56
  24.7 4.8 %collective-permute-start.9 = (f32[16,640]{1,0:T(8,128)S(1)}, f32[16,640]{1,0:T(8,128)S(1)}, u32[]{:S(2)}, u32[]{:S(2)}) collective-permute-start(f32[16,640]{1,0:T(8,128)S(1)} %add.1.a_ref._), channel_id=1, source_target_pairs={{97,0},{96,1},{99,2},{98,3},{101,4},{100,5},{103,6},{102,7},{104,9... | collective-permute-start | bytes 122888 | tf_op jit(solution)/shard_map/ppermute | solution.py:56
  26.7 3.4 %collective-permute-start.8 = (f32[16,640]{1,0:T(8,128)S(1)}, f32[16,640]{1,0:T(8,128)S(1)}, u32[]{:S(2)}, u32[]{:S(2)}) collective-permute-start(f32[16,640]{1,0:T(8,128)S(1)} %add.1.a_ref._), channel_id=1, source_target_pairs={{33,0},{32,1},{35,2},{34,3},{37,4},{36,5},{39,6},{38,7},{40,9},{41... | collective-permute-start | bytes 122888 | tf_op jit(solution)/shard_map/ppermute | solution.py:56
  30.2 6.9 %collective-permute-start.17 = (bf16[80,4096]{1,0:T(8,128)(2,1)S(1)}, bf16[80,4096]{1,0:T(8,128)(2,1)S(1)}, u32[]{:S(2)}, u32[]{:S(2)}) collective-permute-start(bf16[80,4096]{1,0:T(8,128)(2,1)S(1)} %both.1), channel_id=1, source_target_pairs={{1,0},{0,1},{3,2},{2,3},{5,4},{4,5},{7,6},{6,7},{8,9},{9,8},{10,11... | collective-permute-start | bytes 1966088 | tf_op jit(solution)/shard_map/ppermute | solution.py:56
  30.3 4.9 %collective-permute-start.13 = (bf16[16,896]{1,0:T(8,128)(2,1)S(1)}, bf16[16,896]{1,0:T(8,128)(2,1)S(1)}, u32[]{:S(2)}, u32[]{:S(2)}) collective-permute-start(bf16[16,896]{1,0:T(8,128)(2,1)S(1)} %total.1.refs_0_._), channel_id=1, source_target_pairs={{5,0},{4,1},{7,2},{6,3},{1,4},{0,5},{3,6},{2,7},{12,9},{13,8},{14,... | collective-permute-start | bytes 86024 | tf_op jit(solution)/shard_map/ppermute | solution.py:56
  32.0 4.6 %collective-permute-start.12 = (bf16[16,896]{1,0:T(8,128)(2,1)S(1)}, bf16[16,896]{1,0:T(8,128)(2,1)S(1)}, u32[]{:S(2)}, u32[]{:S(2)}) collective-permute-start(bf16[16,896]{1,0:T(8,128)(2,1)S(1)} %total.1.refs_0_._), channel_id=1, source_target_pairs={{7,0},{6,1},{1,2},{0,3},{3,4},{2,5},{5,6},{4,7},{14,9},{15,8},{8,1... | collective-permute-start | bytes 86024 | tf_op jit(solution)/shard_map/ppermute | solution.py:56
  32.6 4.1 %collective-permute-start.11 = (bf16[16,896]{1,0:T(8,128)(2,1)S(1)}, bf16[16,896]{1,0:T(8,128)(2,1)S(1)}, u32[]{:S(2)}, u32[]{:S(2)}) collective-permute-start(bf16[16,896]{1,0:T(8,128)(2,1)S(1)} %total.1.refs_0_._), channel_id=1, source_target_pairs={{3,0},{2,1},{5,2},{4,3},{7,4},{6,5},{1,6},{0,7},{10,9},{11,8},{12,... | collective-permute-start | bytes 86024 | tf_op jit(solution)/shard_map/ppermute | solution.py:56
  36.7 1.4 %collective-permute-start.14 = (bf16[64,896]{1,0:T(8,128)(2,1)S(1)}, bf16[64,896]{1,0:T(8,128)(2,1)S(1)}, u32[]{:S(2)}, u32[]{:S(2)}) collective-permute-start(bf16[64,896]{1,0:T(8,128)(2,1)S(1)} %collect.1.refs_0_), channel_id=1, source_target_pairs={{1,0},{0,1},{3,2},{2,3},{5,4},{4,5},{7,6},{6,7},{8,9},{9,8},{10,11... | collective-permute-start | bytes 344072 | tf_op jit(solution)/shard_map/ppermute | solution.py:56

commit v4 on v3

v4 whole, which is shorter than its diff:
```python
import functools

import jax
import jax.numpy as jnp
from jax import lax
from jax.experimental import pallas as pl
from jax.experimental.pallas import tpu as pltpu
from jax.sharding import PartitionSpec as P

F32 = jnp.float32
BF16 = jnp.bfloat16
CORES = 2
SIDE = 4
LEAD_WORK = 1 << 33


def dot(left, right, dims):
    return lax.dot_general(left, right, (dims, ((), ())), preferred_element_type=F32)


def split3(value):
    high = value.astype(BF16)
    rest = value - high.astype(F32)
    mid = rest.astype(BF16)
    return high, mid, (rest - mid.astype(F32)).astype(BF16)


def params(mebibytes):
    return pltpu.CompilerParams(vmem_limit_bytes=mebibytes << 20)


def whole(count):
    return [pl.BlockSpec(memory_space=pltpu.VMEM)] * count


def cost(flops, traffic):
    return pl.CostEstimate(flops=flops, bytes_accessed=traffic, transcendentals=0)


def parity(row):
    return (row // SIDE + row % SIDE) % 2


def place(row, chip, role):
    return (row * SIDE + chip) * CORES + (role ^ parity(row))


def move(value, source):
    everyone = [
        (row, chip, role)
        for row in range(lax.axis_size("rows"))
        for chip in range(SIDE)
        for role in range(CORES)
    ]
    pairs = [(place(*source(*one)), place(*one)) for one in everyone]
    return lax.ppermute(value, ("rows", "samp"), pairs)


def chip_step(value, step):
    return move(value, lambda row, chip, role: (row, chip ^ step, role ^ parity(row)))


def sibling(value):
    return move(value, lambda row, chip, role: (row, chip, 1 - role))


def beside_step(value, flip):
    return move(value, lambda row, chip, role: (row, chip ^ (3 if role else 1), role ^ flip))


def around(value, axis):
    def source(step):
        def of(row, chip, role):
            z, y = divmod(row, SIDE)
            if axis == "y":
                return z * SIDE + (y ^ step), chip, role
            if axis == "z":
                return (z ^ step) * SIDE + y, chip, role
            return row, chip ^ step, 1 - role

        return of

    return [value] + [move(value, source(step)) for step in (1, 3, 2)]


def whereabouts():
    own, row = lax.axis_index("samp"), lax.axis_index("rows")
    chip, core = own // CORES, lax.rem(own, CORES)
    return chip, core, lax.rem(core + row // SIDE + lax.rem(row, SIDE), 2)


def rows_at(place, height):
    return pl.ds(pl.multiple_of(place * height, height), height)


def by_role(own_ref, sibling_ref):
    _, core, role = whereabouts()
    own, other = own_ref[...], sibling_ref[...]
    return jnp.where(core == role, own, other), jnp.where(core == role, other, own)


def gram_kernel(
    part_ref, own_ref, sibling_ref, other_ref, near_ref, near_sibling_ref, message_ref
):
    height, columns = part_ref.shape
    chip, _, _ = whereabouts()
    mine, other = by_role(own_ref, sibling_ref)
    both = jnp.concatenate([mine, other], axis=0)
    centre = 0.5 * dot(both, mine, ((1,), (1,)))
    span = own_ref.shape[1] // 2

    def half(number, *refs):
        rows = rows_at(number, span)
        blocks = [ref[:, rows] for ref in refs]
        return blocks[0] if len(blocks) == 1 else jnp.concatenate(blocks, axis=0)

    odd = lax.rem(chip, 2)
    core_first = whereabouts()[1] == whereabouts()[2]
    rows = half(odd, own_ref, sibling_ref)
    rows = jnp.where(core_first, rows, jnp.concatenate([rows[height:], rows[:height]], axis=0))
    sides = dot(rows, half(odd, near_ref, other_ref), ((1,), (1,)))
    across = dot(half(chip // 2, near_ref, near_sibling_ref), half(chip // 2, other_ref), ((1,), (1,)))
    pieces = []
    for n in range(SIDE):
        side = jnp.where(n == chip ^ 1, sides[:, :height], sides[:, height:])
        pieces.append(jnp.where(n == chip, centre, jnp.where(n == chip ^ 2, across, side)))
    gram = jnp.concatenate(pieces, axis=1)
    message_ref[:, :columns] = part_ref[...]
    message_ref[:, columns:] = jnp.concatenate([gram[:height], gram[height:]], axis=1)


def collect_kernel(*refs):
    *blocks, out_ref = refs
    height = blocks[0].shape[0]
    chip, _, _ = whereabouts()
    for step, block in zip((0, 1, 3, 2), blocks):
        out_ref[rows_at(chip ^ step, height), :] = block[...]


def lead_kernel(out_ref):
    out_ref[...] = jnp.zeros(out_ref.shape, F32)


def copy_kernel(value_ref, _, out_ref):
    out_ref[...] = value_ref[...]


def part_kernel(stream_ref, sibling_ref, probe_ref, part_ref):
    stream, _ = by_role(stream_ref, sibling_ref)
    part_ref[...] = dot(stream, probe_ref[...], ((1,), (1,)))


def beside_kernel(own_ref, sibling_ref, _, out_ref):
    height = own_ref.shape[0]
    _, core, _ = whereabouts()
    out_ref[rows_at(core, height), :] = own_ref[...]
    out_ref[rows_at(1 - core, height), :] = sibling_ref[...]


def relay_kernel(beside_ref, near_ref, other_ref, _, out_ref):
    height = near_ref.shape[0]
    _, _, role = whereabouts()
    out_ref[:height] = beside_ref[rows_at(1 - role, height), :]

    @pl.when(role == 0)
    def _():
        out_ref[height:] = near_ref[...]

    @pl.when(role == 1)
    def _():
        out_ref[height:] = other_ref[...]


def both_kernel(beside_ref, other_ref, across_ref, _, out_ref):
    height = other_ref.shape[0]
    out_ref[: 2 * height] = beside_ref[...]
    out_ref[2 * height : 3 * height] = other_ref[...]
    out_ref[3 * height :] = across_ref[...]


def order_kernel(
    temp_ref, temp_sibling_ref, near_ref, near_sibling_ref, other_ref, stream_ref, stream_sibling_ref,
    beside_ref, both_ref, across_ref, out_ref,
):
    chip, core, role = whereabouts()
    height = temp_ref.shape[0]

    def put(base, owner, place, value):
        place = (base * CORES + owner) * SIDE + place
        out_ref[rows_at(place, height), :] = value

    rows = [slice(n * height, (n + 1) * height) for n in range(5)]
    put(0, core, chip, temp_ref[...])
    put(0, 1 - core, chip, temp_sibling_ref[...])
    put(0, role, chip ^ 1, near_ref[...])
    put(0, 1 - role, chip ^ 1, near_sibling_ref[...])
    put(0, role, chip ^ 3, other_ref[...])
    put(0, 1 - role, chip ^ 3, both_ref[rows[2]])
    put(0, 1 - role, chip ^ 2, across_ref[rows[1]])
    put(0, role, chip ^ 2, both_ref[rows[4]])
    put(1, core, chip, stream_ref[...])
    put(1, 1 - core, chip, stream_sibling_ref[...])
    for n in range(CORES):
        put(1, n, chip ^ (1 + 2 * role), beside_ref[rows[n]])
        put(1, n, chip ^ (3 - 2 * role), both_ref[rows[n]])
    put(1, role, chip ^ 2, across_ref[rows[0]])
    put(1, 1 - role, chip ^ 2, both_ref[rows[3]])


def add_kernel(a_ref, b_ref, c_ref, d_ref, out_ref):
    out_ref[...] = (a_ref[...] + b_ref[...]) + (c_ref[...] + d_ref[...])


def sum_kernel(columns, a_ref, b_ref, c_ref, d_ref, message_ref):
    total = (a_ref[...] + b_ref[...]) + (c_ref[...] + d_ref[...])
    pieces = [total[:, :columns].astype(BF16), *split3(total[:, columns:])]
    pieces = jnp.concatenate(pieces, axis=1)
    message_ref[...] = pieces


def output_kernel(columns, scales, *refs):
    near_ref, far_ref, slabs_ref, basis_ref, back_ref, weights, message, basis, back, done = refs
    half = near_ref.shape[0]
    samples = CORES * half
    image_scale, back_scale, total_rows = scales
    own = lax.axis_index("samp")
    height = half // SIDE
    chip, _, role = whereabouts()
    for n in range(SIDE):
        owner = jnp.where(chip == n, role, 1 - role)
        rows = slice(n * height, (n + 1) * height)
        message[rows_at(owner * SIDE + n, height), :] = near_ref[rows]
        message[rows_at((1 - owner) * SIDE + n, height), :] = far_ref[rows]
    products = sum(
        message[:, columns + n * samples : columns + (n + 1) * samples].astype(F32) for n in range(3)
    )
    first = lax.broadcasted_iota(jnp.int32, (half, samples), 1) < half
    top = jnp.where(first, products[:half], products[half:])
    bottom = jnp.where(first, products[half:], products[:half])
    bottom = jnp.concatenate([bottom[:, half:], bottom[:, :half]], axis=1)
    gram = jnp.concatenate([top, bottom], axis=0)
    row, lane = [lax.broadcasted_iota(jnp.int32, gram.shape, axis) // height for axis in (0, 1)]
    moves = lax.rem(lane, SIDE) == lax.rem(row, SIDE) ^ 2
    moved = jnp.where(moves, gram, 0.0)
    moved = jnp.concatenate([moved[(n ^ 1) * height : ((n ^ 1) + 1) * height] for n in range(samples // height)], axis=0)
    ahead = jnp.concatenate([moved[:, height:], moved[:, :height]], axis=1)
    behind = jnp.concatenate([moved[:, -height:], moved[:, :-height]], axis=1)
    moved = jnp.where(lax.rem(lane, 2) == 0, ahead, behind)
    gram = jnp.where(moves, 0.0, gram) + moved
    pieces = split3(gram + gram.T)
    chunks = done.shape[0] - 1
    size = columns // chunks
    copies = []
    for n in range(chunks):
        here = pl.ds(n * size, size)
        turned = message[:, n * size : (n + 1) * size].astype(F32).T
        left = turned.astype(BF16)
        product = sum(dot(left, piece, ((1,), (0,))) for piece in pieces)
        power = jnp.maximum(jnp.sum(product * turned, axis=1, keepdims=True), 0.0)
        power = power * (image_scale * image_scale)
        gain = jnp.broadcast_to(image_scale * lax.rsqrt(power / total_rows + 1e-06), product.shape)
        weights[here, :] = product * gain
        image = dot(left, slabs_ref[:samples, :], ((1,), (0,)))
        basis[here, :] = (image * jnp.concatenate([gain] * (image.shape[1] // samples), axis=1)).astype(BF16)
        copies.append(pltpu.make_async_copy(basis.at[here], basis_ref.at[here], done.at[n]))
        copies[-1].start()
    chosen = weights[rows_at(own, back.shape[0]), :].astype(BF16)
    back[...] = dot(chosen, slabs_ref[samples:, :], ((1,), (0,))) * back_scale
    copies.append(pltpu.make_async_copy(back, back_ref, done.at[chunks]))
    copies[-1].start()
    for copy in copies:
        copy.wait()


def shards(temp_slab, stream_slab, probe):
    height, local_rows = temp_slab.shape
    columns = probe.shape[0]
    groups = lax.axis_size("samp")
    row_groups = lax.axis_size("rows")
    total_rows = local_rows * row_groups
    samples = height * groups
    half = samples // CORES
    wide = columns + samples
    shape = jax.ShapeDtypeStruct

    def call(kernel, name, operands, outs, scratch=(), work=0):
        outs = [shape(*out) for out in outs]
        traffic = sum(value.size * value.dtype.itemsize for value in [*operands, *outs])
        return pl.pallas_call(
            kernel,
            out_shape=tuple(outs),
            in_specs=whole(len(operands)),
            out_specs=tuple(whole(len(outs))),
            scratch_shapes=[pltpu.VMEM(*one) for one in scratch],
            compiler_params=params(16),
            cost_estimate=cost(work, traffic),
            name=name,
        )(*operands)

    slab = ((height, local_rows), BF16)
    packed = columns + 3 * samples

    (lead,) = call(lead_kernel, "lead", [], [((8, 128), F32)], work=LEAD_WORK)
    (temp_copy,) = call(copy_kernel, "ahead", [temp_slab, lead], [slab])
    near = chip_step(temp_slab, 1)
    other = chip_step(temp_slab, 3)
    temp_sibling = sibling(temp_copy)
    stream_sibling = sibling(stream_slab)
    (part,) = call(
        part_kernel, "part", [stream_slab, stream_sibling, probe], [((height, columns), F32)], work=2 * height * columns * local_rows
    )
    (near,) = call(copy_kernel, "near", [near, part], [slab], work=LEAD_WORK)
    (other,) = call(copy_kernel, "other", [other, part], [slab], work=LEAD_WORK)
    near_sibling = sibling(near)
    (message,) = call(
        gram_kernel,
        "gram",
        [part, temp_slab, temp_sibling, other, near, near_sibling],
        [((height, wide), F32)],
        work=4 * height * half * local_rows,
    )
    (beside,) = call(
        beside_kernel,
        "beside",
        [stream_slab, stream_sibling, temp_sibling],
        [((2 * height, local_rows), BF16)],
    )
    beside = beside_step(beside, 0)
    (message,) = call(add_kernel, "add", around(message, "y"), [((height, wide), F32)])
    (across,) = call(relay_kernel, "relay", [beside, near, other, message], [((2 * height, local_rows), BF16)])
    across = beside_step(across, 1)
    (message,) = call(
        functools.partial(sum_kernel, columns), "total", around(message, "z"), [((height, packed), BF16)]
    )
    (both,) = call(both_kernel, "both", [beside, other, across, message], [((5 * height, local_rows), BF16)])
    both_sibling = sibling(both)
    (message,) = call(collect_kernel, "collect", around(message, "x"), [((half, packed), BF16)])
    message_other = sibling(message)
    (slabs,) = call(
        order_kernel,
        "order",
        [
            temp_slab, temp_sibling, near, near_sibling, other, stream_slab, stream_sibling,
            beside, both_sibling, across,
        ],
        [((2 * samples, local_rows), BF16)],
    )

    scales = (
        1.0 / (samples - 1.0),
        1.0 / ((samples - 1.0) * float(total_rows) ** 0.5),
        float(total_rows),
    )
    mine = columns // groups
    chunks = 4
    outs = (shape((columns, local_rows), BF16), shape((mine, local_rows), F32))
    basis, back_image = pl.pallas_call(
        functools.partial(output_kernel, columns, scales),
        out_shape=outs,
        in_specs=whole(3),
        out_specs=tuple([pl.BlockSpec(memory_space=pl.ANY)] * 2),
        scratch_shapes=[
            pltpu.VMEM((columns, samples), F32),
            pltpu.VMEM((samples, packed), BF16),
            *[pltpu.VMEM(out.shape, out.dtype) for out in outs],
            pltpu.SemaphoreType.DMA((chunks + 1,)),
        ],
        compiler_params=params(40),
        cost_estimate=cost(2 * (columns + mine) * samples * local_rows, 7 << 20),
        name="outputs",
    )(message, message_other, slabs)
    return (basis, back_image)


def solution(mesh):
    return jax.shard_map(
        shards,
        mesh=mesh,
        in_specs=(P("samp", "rows"), P("samp", "rows"), P(None, "rows")),
        out_specs=(P(None, "rows"), P("samp", "rows")),
        check_vma=False,
    )
```

time: 41.5 us -> 40.2 us (0.969)
  starting transfers between devices: 26.4 us -> 22.1 us
  waiting for transfers between devices: 8.88 us -> 12 us
    ppermute x18, starting transfers between devices: 26.4 us -> 22.1 us  [move(): return lax.ppermute(value, ('rows', 'samp'), pairs)]
    ppermute x18, waiting for transfers between devices: 8.88 us -> 12 us  [move(): return lax.ppermute(value, ('rows', 'samp'), pairs)]
    pallas_call x12 -> x13, Pallas kernels: 2.05 us -> 1.98 us  [call(): pl.pallas_call(kernel, out_shape=tuple(outs), in_specs=whole(len(operands...]
  transfers between devices with their start and end apart: 18 -> 18, of which waited for: 10 -> 10; matrix products, arithmetic and copies ran while one was open for 0% -> 0% of each run, Pallas kernels for 3% -> 5%
where the time goes in v4:
time: 40.2 us; the launch traced here: 40.1 us
  starting transfers between devices  22.1 us (55%)
  waiting for transfers between devices  12 us (30%)
  Pallas kernels  5.19 us (13%)
  between operations  0.76 us (2%)
    ppermute x18, starting transfers between devices, move(): return lax.ppermute(value, ('rows', 'samp'), pairs)  22.1 us
    ppermute x18, waiting for transfers between devices, move(): return lax.ppermute(value, ('rows', 'samp'), pairs)  12 us
    pallas_call x1, Pallas kernels, shards(): pl.pallas_call(functools.partial(output_kernel, columns, scales), out_sha...  3.21 us
    pallas_call x13, Pallas kernels, call(): pl.pallas_call(kernel, out_shape=tuple(outs), in_specs=whole(len(operands...  1.98 us
  transfers between devices with their start and end apart: 18, of which 10 were waited for; matrix products, arithmetic and copies ran while one was open for 0% of the time, Pallas kernels for 5%

profile of v4, /device:TPU:1, one launch (start us, length us, event | category | flops | bytes accessed | tf_op | source)
XLA Modules:
  0.0 40.1 jit_solution(14377568161033538432)
XLA Ops:
  0.6 0.0 copy-start.2
  0.6 0.0 copy-start.1
  0.6 0.0 copy-start
  0.7 2.1 %collective-permute-start.3 = (bf16[16,4096]{1,0:T(8,128)(2,1)}, bf16[16,4096]{1,0:T(8,128)(2,1)S(1)}, u32[]{:S(2)}, u32[]{:S(2)}) collective-permute-start(bf16[16,4096]{1,0:T(8,128)(2,1)} %temp_ref.1), channel_id=1, source_target_pairs={{2,0},{3,1},{0,2},{1,3},{6,4},{7,5},{4,6},{5,7},{10,9},{11,8},{8,1... | collective-permute-start | bytes 393224 | tf_op jit(solution)/shard_map/ppermute | solution.py:56
  2.8 1.8 %collective-permute-start.2 = (bf16[16,4096]{1,0:T(8,128)(2,1)}, bf16[16,4096]{1,0:T(8,128)(2,1)S(1)}, u32[]{:S(2)}, u32[]{:S(2)}) collective-permute-start(bf16[16,4096]{1,0:T(8,128)(2,1)} %temp_ref.1), channel_id=1, source_target_pairs={{6,0},{7,1},{4,2},{5,3},{2,4},{3,5},{0,6},{1,7},{14,9},{15,8},{12,... | collective-permute-start | bytes 393224 | tf_op jit(solution)/shard_map/ppermute | solution.py:56
  4.6 1.2 %collective-permute-start = (bf16[16,4096]{1,0:T(8,128)(2,1)}, bf16[16,4096]{1,0:T(8,128)(2,1)S(1)}, u32[]{:S(2)}, u32[]{:S(2)}) collective-permute-start(bf16[16,4096]{1,0:T(8,128)(2,1)} %stream_ref.3), channel_id=1, source_target_pairs={{1,0},{0,1},{3,2},{2,3},{5,4},{4,5},{7,6},{6,7},{8,9},{9,8},{10,11... | collective-permute-start | bytes 393224 | tf_op jit(solution)/shard_map/ppermute | solution.py:56
  5.8 0.0 copy-done.2
  5.8 0.1 collective-permute-start.1
  5.9 1.1 %collective-permute-done.sibling_ref.stream_sibling_ref = bf16[16,4096]{1,0:T(8,128)(2,1)S(1)} collective-permute-done((bf16[16,4096]{1,0:T(8,128)(2,1)}, bf16[16,4096]{1,0:T(8,128)(2,1)S(1)}, u32[]{:S(2)}, u32[]{:S(2)}) %collective-permute-start) | collective-permute-done | bytes 131104 | tf_op jit(solution)/shard_map/ppermute | solution.py:56
  7.0 0.0 copy-done.1
  7.0 0.0 copy-done
  7.0 1.2 %part.1._.part_ref = f32[16,512]{1,0:T(8,128)S(1)} custom-call(bf16[16,4096]{1,0:T(8,128)(2,1)S(1)} %copy-done.1, bf16[16,4096]{1,0:T(8,128)(2,1)S(1)} %collective-permute-done.sibling_ref.stream_sibling_ref, bf16[512,4096]{1,0:T(8,128)(2,1)S(1)} %copy-done), custom_call_target="tpu_custom_call" | custom-call | flops 67108864 | bytes 4489216 | tf_op jit(solution)/shard_map/part/pallas_call | solution.py:289
  8.2 0.0 collective-permute-done.3.value_ref
  8.2 0.4 %collective-permute-start.4 = (bf16[16,4096]{1,0:T(8,128)(2,1)S(1)}, bf16[16,4096]{1,0:T(8,128)(2,1)S(1)}, u32[]{:S(2)}, u32[]{:S(2)}) collective-permute-start(bf16[16,4096]{1,0:T(8,128)(2,1)S(1)} %near.1.near_ref), channel_id=1, source_target_pairs={{1,0},{0,1},{3,2},{2,3},{5,4},{4,5},{7,6},{6,7},{8,9},{9,8},{10,11... | collective-permute-start | bytes 393224 | tf_op jit(solution)/shard_map/ppermute | solution.py:56
  8.7 0.0 collective-permute-done.1.sibling_ref._.temp_sibling_ref
  8.7 1.7 %collective-permute-start.15 = (bf16[32,4096]{1,0:T(8,128)(2,1)S(1)}, bf16[32,4096]{1,0:T(8,128)(2,1)S(1)}, u32[]{:S(2)}, u32[]{:S(2)}) collective-permute-start(bf16[32,4096]{1,0:T(8,128)(2,1)S(1)} %beside.1), channel_id=1, source_target_pairs={{2,0},{7,1},{0,2},{5,3},{6,4},{3,5},{4,6},{1,7},{11,9},{14,8},{9,1... | collective-permute-start | bytes 786440 | tf_op jit(solution)/shard_map/ppermute | solution.py:56
  10.4 0.0 collective-permute-done.2.value_ref
  10.4 0.0 collective-permute-done.4.near_sibling_ref
  10.4 0.4 %gram.1.a_ref = f32[16,640]{1,0:T(8,128)S(1)} custom-call(f32[16,512]{1,0:T(8,128)S(1)} %part.1._.part_ref, bf16[16,4096]{1,0:T(8,128)(2,1)S(1)} %copy-done.2, bf16[16,4096]{1,0:T(8,128)(2,1)S(1)} %collective-permute-done.1.sibling_ref._.temp_sibling_ref, bf16[16,4096]{1,0:T(8,128)(2,1)S(1)} %other.1.other_ref, bf16[16,4096]{1,0:T(8,128)(2,1)S(1)} %near.1.near_ref, ...), custom_call_target="tpu_custom_call" | custom-call | flops 16777216 | bytes 729088 | tf_op jit(solution)/shard_map/gram/pallas_call | solution.py:289
  10.9 2.9 %collective-permute-start.7 = (f32[16,640]{1,0:T(8,128)S(1)}, f32[16,640]{1,0:T(8,128)S(1)}, u32[]{:S(2)}, u32[]{:S(2)}) collective-permute-start(f32[16,640]{1,0:T(8,128)S(1)} %gram.1.a_ref), channel_id=1, source_target_pairs={{16,0},{17,1},{18,2},{19,3},{20,4},{21,5},{22,6},{23,7},{25,9},{24... | collective-permute-start | bytes 122888 | tf_op jit(solution)/shard_map/ppermute | solution.py:56
  13.8 1.9 %collective-permute-start.6 = (f32[16,640]{1,0:T(8,128)S(1)}, f32[16,640]{1,0:T(8,128)S(1)}, u32[]{:S(2)}, u32[]{:S(2)}) collective-permute-start(f32[16,640]{1,0:T(8,128)S(1)} %gram.1.a_ref), channel_id=1, source_target_pairs={{25,0},{24,1},{27,2},{26,3},{29,4},{28,5},{31,6},{30,7},{16,9},{17... | collective-permute-start | bytes 122888 | tf_op jit(solution)/shard_map/ppermute | solution.py:56
  15.7 0.0 collective-permute-start.5
  15.7 0.1 collective-permute-done.7.d_ref
  15.8 2.7 %collective-permute-done.6.c_ref = f32[16,640]{1,0:T(8,128)S(1)} collective-permute-done((f32[16,640]{1,0:T(8,128)S(1)}, f32[16,640]{1,0:T(8,128)S(1)}, u32[]{:S(2)}, u32[]{:S(2)}) %collective-permute-start.6) | collective-permute-done | bytes 40992 | tf_op jit(solution)/shard_map/ppermute | solution.py:56
  18.4 0.7 %collective-permute-done.5.b_ref = f32[16,640]{1,0:T(8,128)S(1)} collective-permute-done((f32[16,640]{1,0:T(8,128)S(1)}, f32[16,640]{1,0:T(8,128)S(1)}, u32[]{:S(2)}, u32[]{:S(2)}) %collective-permute-start.5) | collective-permute-done | bytes 40992 | tf_op jit(solution)/shard_map/ppermute | solution.py:56
  19.1 0.0 collective-permute-done.15.beside_ref
  19.2 0.3 collective-permute-start.16
  19.5 3.6 %collective-permute-start.10 = (f32[16,640]{1,0:T(8,128)S(1)}, f32[16,640]{1,0:T(8,128)S(1)}, u32[]{:S(2)}, u32[]{:S(2)}) collective-permute-start(f32[16,640]{1,0:T(8,128)S(1)} %add.1.a_ref._), channel_id=1, source_target_pairs={{64,0},{65,1},{66,2},{67,3},{68,4},{69,5},{70,6},{71,7},{73,9},{72... | collective-permute-start | bytes 122888 | tf_op jit(solution)/shard_map/ppermute | solution.py:56
  23.1 1.0 %collective-permute-start.9 = (f32[16,640]{1,0:T(8,128)S(1)}, f32[16,640]{1,0:T(8,128)S(1)}, u32[]{:S(2)}, u32[]{:S(2)}) collective-permute-start(f32[16,640]{1,0:T(8,128)S(1)} %add.1.a_ref._), channel_id=1, source_target_pairs={{97,0},{96,1},{99,2},{98,3},{101,4},{100,5},{103,6},{102,7},{104,9... | collective-permute-start | bytes 122888 | tf_op jit(solution)/shard_map/ppermute | solution.py:56
  24.1 0.3 collective-permute-start.8
  24.4 0.1 collective-permute-done.10.d_ref
  24.5 3.2 %collective-permute-done.9.c_ref = f32[16,640]{1,0:T(8,128)S(1)} collective-permute-done((f32[16,640]{1,0:T(8,128)S(1)}, f32[16,640]{1,0:T(8,128)S(1)}, u32[]{:S(2)}, u32[]{:S(2)}) %collective-permute-start.9) | collective-permute-done | bytes 40992 | tf_op jit(solution)/shard_map/ppermute | solution.py:56
  27.7 0.0 collective-permute-done.8.b_ref
  27.7 0.0 collective-permute-done.16.across_ref
  27.8 1.7 %collective-permute-start.17 = (bf16[80,4096]{1,0:T(8,128)(2,1)S(1)}, bf16[80,4096]{1,0:T(8,128)(2,1)S(1)}, u32[]{:S(2)}, u32[]{:S(2)}) collective-permute-start(bf16[80,4096]{1,0:T(8,128)(2,1)S(1)} %both.1), channel_id=1, source_target_pairs={{1,0},{0,1},{3,2},{2,3},{5,4},{4,5},{7,6},{6,7},{8,9},{9,8},{10,11... | collective-permute-start | bytes 1966088 | tf_op jit(solution)/shard_map/ppermute | solution.py:56
  29.5 1.2 %collective-permute-start.13 = (bf16[16,896]{1,0:T(8,128)(2,1)S(1)}, bf16[16,896]{1,0:T(8,128)(2,1)S(1)}, u32[]{:S(2)}, u32[]{:S(2)}) collective-permute-start(bf16[16,896]{1,0:T(8,128)(2,1)S(1)} %total.1.refs_0_._), channel_id=1, source_target_pairs={{5,0},{4,1},{7,2},{6,3},{1,4},{0,5},{3,6},{2,7},{12,9},{13,8},{14,... | collective-permute-start | bytes 86024 | tf_op jit(solution)/shard_map/ppermute | solution.py:56
  30.7 1.5 %collective-permute-start.12 = (bf16[16,896]{1,0:T(8,128)(2,1)S(1)}, bf16[16,896]{1,0:T(8,128)(2,1)S(1)}, u32[]{:S(2)}, u32[]{:S(2)}) collective-permute-start(bf16[16,896]{1,0:T(8,128)(2,1)S(1)} %total.1.refs_0_._), channel_id=1, source_target_pairs={{7,0},{6,1},{5,2},{4,3},{3,4},{2,5},{1,6},{0,7},{14,9},{15,8},{12,... | collective-permute-start | bytes 86024 | tf_op jit(solution)/shard_map/ppermute | solution.py:56
  32.2 0.2 collective-permute-start.11
  32.4 1.9 %collective-permute-done.13.refs_3_ = bf16[16,896]{1,0:T(8,128)(2,1)S(1)} collective-permute-done((bf16[16,896]{1,0:T(8,128)(2,1)S(1)}, bf16[16,896]{1,0:T(8,128)(2,1)S(1)}, u32[]{:S(2)}, u32[]{:S(2)}) %collective-permute-start.13) | collective-permute-done | bytes 28704 | tf_op jit(solution)/shard_map/ppermute | solution.py:56
  34.3 0.9 %collective-permute-done.12.refs_2_ = bf16[16,896]{1,0:T(8,128)(2,1)S(1)} collective-permute-done((bf16[16,896]{1,0:T(8,128)(2,1)S(1)}, bf16[16,896]{1,0:T(8,128)(2,1)S(1)}, u32[]{:S(2)}, u32[]{:S(2)}) %collective-permute-start.12) | collective-permute-done | bytes 28704 | tf_op jit(solution)/shard_map/ppermute | solution.py:56
  35.2 0.3 collective-permute-done.11.refs_1_
  35.5 0.1 collective-permute-start.14
  35.6 0.0 collective-permute-done.17.both_ref
  35.6 0.2 order.1.refs_2_
  35.8 1.1 %collective-permute-done.14.refs_1_ = bf16[64,896]{1,0:T(8,128)(2,1)S(1)} collective-permute-done((bf16[64,896]{1,0:T(8,128)(2,1)S(1)}, bf16[64,896]{1,0:T(8,128)(2,1)S(1)}, u32[]{:S(2)}, u32[]{:S(2)}) %collective-permute-start.14) | collective-permute-done | bytes 114720 | tf_op jit(solution)/shard_map/ppermute | solution.py:56
  36.9 3.2 %outputs.1 = (bf16[512,4096]{1,0:T(8,128)(2,1)}, f32[64,4096]{1,0:T(8,128)}) custom-call(bf16[64,896]{1,0:T(8,128)(2,1)S(1)} %collect.1.refs_0_, bf16[64,896]{1,0:T(8,128)(2,1)S(1)} %collective-permute-done.14.refs_1_, bf16[256,4096]{1,0:T(8,128)(2,1)S(1)} %order.1.refs_2_), custom_call_target="tpu_custom_call" | custom-call | flops 603979776 | bytes 7340032 | tf_op jit(solution)/shard_map/outputs/pallas_call | solution.py:357
  (10 shorter events, 0.2 us)
Async XLA Ops:
  0.6 5.2 %copy-start.2 = (bf16[16,4096]{1,0:T(8,128)(2,1)S(1)}, bf16[16,4096]{1,0:T(8,128)(2,1)}, u32[]{:S(2)}) copy-start(bf16[16,4096]{1,0:T(8,128)(2,1)} %temp_ref.1) | copy-start | bytes 393220
  0.6 6.4 %copy-start.1 = (bf16[16,4096]{1,0:T(8,128)(2,1)S(1)}, bf16[16,4096]{1,0:T(8,128)(2,1)}, u32[]{:S(2)}) copy-start(bf16[16,4096]{1,0:T(8,128)(2,1)} %stream_ref.3) | copy-start | bytes 393220
  0.6 6.4 %copy-start = (bf16[512,4096]{1,0:T(8,128)(2,1)S(1)}, bf16[512,4096]{1,0:T(8,128)(2,1)}, u32[]{:S(2)}) copy-start(bf16[512,4096]{1,0:T(8,128)(2,1)} %probe_ref.1) | copy-start | bytes 12582916
  0.7 7.6 %collective-permute-start.3 = (bf16[16,4096]{1,0:T(8,128)(2,1)}, bf16[16,4096]{1,0:T(8,128)(2,1)S(1)}, u32[]{:S(2)}, u32[]{:S(2)}) collective-permute-start(bf16[16,4096]{1,0:T(8,128)(2,1)} %temp_ref.1), channel_id=1, source_target_pairs={{2,0},{3,1},{0,2},{1,3},{6,4},{7,5},{4,6},{5,7},{10,9},{11,8},{8,1... | collective-permute-start | bytes 393224 | tf_op jit(solution)/shard_map/ppermute | solution.py:56
  2.8 7.6 %collective-permute-start.2 = (bf16[16,4096]{1,0:T(8,128)(2,1)}, bf16[16,4096]{1,0:T(8,128)(2,1)S(1)}, u32[]{:S(2)}, u32[]{:S(2)}) collective-permute-start(bf16[16,4096]{1,0:T(8,128)(2,1)} %temp_ref.1), channel_id=1, source_target_pairs={{6,0},{7,1},{4,2},{5,3},{2,4},{3,5},{0,6},{1,7},{14,9},{15,8},{12,... | collective-permute-start | bytes 393224 | tf_op jit(solution)/shard_map/ppermute | solution.py:56
  4.6 2.4 %collective-permute-start = (bf16[16,4096]{1,0:T(8,128)(2,1)}, bf16[16,4096]{1,0:T(8,128)(2,1)S(1)}, u32[]{:S(2)}, u32[]{:S(2)}) collective-permute-start(bf16[16,4096]{1,0:T(8,128)(2,1)} %stream_ref.3), channel_id=1, source_target_pairs={{1,0},{0,1},{3,2},{2,3},{5,4},{4,5},{7,6},{6,7},{8,9},{9,8},{10,11... | collective-permute-start | bytes 393224 | tf_op jit(solution)/shard_map/ppermute | solution.py:56
  5.8 2.8 %collective-permute-start.1 = (bf16[16,4096]{1,0:T(8,128)(2,1)S(1)}, bf16[16,4096]{1,0:T(8,128)(2,1)S(1)}, u32[]{:S(2)}, u32[]{:S(2)}) collective-permute-start(bf16[16,4096]{1,0:T(8,128)(2,1)S(1)} %ahead.1), channel_id=1, source_target_pairs={{1,0},{0,1},{3,2},{2,3},{5,4},{4,5},{7,6},{6,7},{8,9},{9,8},{10,11... | collective-permute-start | bytes 393224 | tf_op jit(solution)/shard_map/ppermute | solution.py:56
  8.2 2.1 %collective-permute-start.4 = (bf16[16,4096]{1,0:T(8,128)(2,1)S(1)}, bf16[16,4096]{1,0:T(8,128)(2,1)S(1)}, u32[]{:S(2)}, u32[]{:S(2)}) collective-permute-start(bf16[16,4096]{1,0:T(8,128)(2,1)S(1)} %near.1.near_ref), channel_id=1, source_target_pairs={{1,0},{0,1},{3,2},{2,3},{5,4},{4,5},{7,6},{6,7},{8,9},{9,8},{10,11... | collective-permute-start | bytes 393224 | tf_op jit(solution)/shard_map/ppermute | solution.py:56
  8.7 10.4 %collective-permute-start.15 = (bf16[32,4096]{1,0:T(8,128)(2,1)S(1)}, bf16[32,4096]{1,0:T(8,128)(2,1)S(1)}, u32[]{:S(2)}, u32[]{:S(2)}) collective-permute-start(bf16[32,4096]{1,0:T(8,128)(2,1)S(1)} %beside.1), channel_id=1, source_target_pairs={{2,0},{7,1},{0,2},{5,3},{6,4},{3,5},{4,6},{1,7},{11,9},{14,8},{9,1... | collective-permute-start | bytes 786440 | tf_op jit(solution)/shard_map/ppermute | solution.py:56
  10.9 4.9 %collective-permute-start.7 = (f32[16,640]{1,0:T(8,128)S(1)}, f32[16,640]{1,0:T(8,128)S(1)}, u32[]{:S(2)}, u32[]{:S(2)}) collective-permute-start(f32[16,640]{1,0:T(8,128)S(1)} %gram.1.a_ref), channel_id=1, source_target_pairs={{16,0},{17,1},{18,2},{19,3},{20,4},{21,5},{22,6},{23,7},{25,9},{24... | collective-permute-start | bytes 122888 | tf_op jit(solution)/shard_map/ppermute | solution.py:56
  13.8 4.6 %collective-permute-start.6 = (f32[16,640]{1,0:T(8,128)S(1)}, f32[16,640]{1,0:T(8,128)S(1)}, u32[]{:S(2)}, u32[]{:S(2)}) collective-permute-start(f32[16,640]{1,0:T(8,128)S(1)} %gram.1.a_ref), channel_id=1, source_target_pairs={{25,0},{24,1},{27,2},{26,3},{29,4},{28,5},{31,6},{30,7},{16,9},{17... | collective-permute-start | bytes 122888 | tf_op jit(solution)/shard_map/ppermute | solution.py:56
  15.7 3.4 %collective-permute-start.5 = (f32[16,640]{1,0:T(8,128)S(1)}, f32[16,640]{1,0:T(8,128)S(1)}, u32[]{:S(2)}, u32[]{:S(2)}) collective-permute-start(f32[16,640]{1,0:T(8,128)S(1)} %gram.1.a_ref), channel_id=1, source_target_pairs={{9,0},{8,1},{11,2},{10,3},{13,4},{12,5},{15,6},{14,7},{0,9},{1,8},... | collective-permute-start | bytes 122888 | tf_op jit(solution)/shard_map/ppermute | solution.py:56
  19.2 8.5 %collective-permute-start.16 = (bf16[32,4096]{1,0:T(8,128)(2,1)S(1)}, bf16[32,4096]{1,0:T(8,128)(2,1)S(1)}, u32[]{:S(2)}, u32[]{:S(2)}) collective-permute-start(bf16[32,4096]{1,0:T(8,128)(2,1)S(1)} %relay.1), channel_id=1, source_target_pairs={{3,0},{6,1},{1,2},{4,3},{7,4},{2,5},{5,6},{0,7},{10,9},{15,8},{8,1... | collective-permute-start | bytes 786440 | tf_op jit(solution)/shard_map/ppermute | solution.py:56
  19.5 5.0 %collective-permute-start.10 = (f32[16,640]{1,0:T(8,128)S(1)}, f32[16,640]{1,0:T(8,128)S(1)}, u32[]{:S(2)}, u32[]{:S(2)}) collective-permute-start(f32[16,640]{1,0:T(8,128)S(1)} %add.1.a_ref._), channel_id=1, source_target_pairs={{64,0},{65,1},{66,2},{67,3},{68,4},{69,5},{70,6},{71,7},{73,9},{72... | collective-permute-start | bytes 122888 | tf_op jit(solution)/shard_map/ppermute | solution.py:56
  23.1 4.6 %collective-permute-start.9 = (f32[16,640]{1,0:T(8,128)S(1)}, f32[16,640]{1,0:T(8,128)S(1)}, u32[]{:S(2)}, u32[]{:S(2)}) collective-permute-start(f32[16,640]{1,0:T(8,128)S(1)} %add.1.a_ref._), channel_id=1, source_target_pairs={{97,0},{96,1},{99,2},{98,3},{101,4},{100,5},{103,6},{102,7},{104,9... | collective-permute-start | bytes 122888 | tf_op jit(solution)/shard_map/ppermute | solution.py:56
  24.1 3.6 %collective-permute-start.8 = (f32[16,640]{1,0:T(8,128)S(1)}, f32[16,640]{1,0:T(8,128)S(1)}, u32[]{:S(2)}, u32[]{:S(2)}) collective-permute-start(f32[16,640]{1,0:T(8,128)S(1)} %add.1.a_ref._), channel_id=1, source_target_pairs={{33,0},{32,1},{35,2},{34,3},{37,4},{36,5},{39,6},{38,7},{40,9},{41... | collective-permute-start | bytes 122888 | tf_op jit(solution)/shard_map/ppermute | solution.py:56
  27.8 7.8 %collective-permute-start.17 = (bf16[80,4096]{1,0:T(8,128)(2,1)S(1)}, bf16[80,4096]{1,0:T(8,128)(2,1)S(1)}, u32[]{:S(2)}, u32[]{:S(2)}) collective-permute-start(bf16[80,4096]{1,0:T(8,128)(2,1)S(1)} %both.1), channel_id=1, source_target_pairs={{1,0},{0,1},{3,2},{2,3},{5,4},{4,5},{7,6},{6,7},{8,9},{9,8},{10,11... | collective-permute-start | bytes 1966088 | tf_op jit(solution)/shard_map/ppermute | solution.py:56
  29.5 4.8 %collective-permute-start.13 = (bf16[16,896]{1,0:T(8,128)(2,1)S(1)}, bf16[16,896]{1,0:T(8,128)(2,1)S(1)}, u32[]{:S(2)}, u32[]{:S(2)}) collective-permute-start(bf16[16,896]{1,0:T(8,128)(2,1)S(1)} %total.1.refs_0_._), channel_id=1, source_target_pairs={{5,0},{4,1},{7,2},{6,3},{1,4},{0,5},{3,6},{2,7},{12,9},{13,8},{14,... | collective-permute-start | bytes 86024 | tf_op jit(solution)/shard_map/ppermute | solution.py:56
  30.7 4.5 %collective-permute-start.12 = (bf16[16,896]{1,0:T(8,128)(2,1)S(1)}, bf16[16,896]{1,0:T(8,128)(2,1)S(1)}, u32[]{:S(2)}, u32[]{:S(2)}) collective-permute-start(bf16[16,896]{1,0:T(8,128)(2,1)S(1)} %total.1.refs_0_._), channel_id=1, source_target_pairs={{7,0},{6,1},{5,2},{4,3},{3,4},{2,5},{1,6},{0,7},{14,9},{15,8},{12,... | collective-permute-start | bytes 86024 | tf_op jit(solution)/shard_map/ppermute | solution.py:56
  32.2 3.3 %collective-permute-start.11 = (bf16[16,896]{1,0:T(8,128)(2,1)S(1)}, bf16[16,896]{1,0:T(8,128)(2,1)S(1)}, u32[]{:S(2)}, u32[]{:S(2)}) collective-permute-start(bf16[16,896]{1,0:T(8,128)(2,1)S(1)} %total.1.refs_0_._), channel_id=1, source_target_pairs={{3,0},{2,1},{1,2},{0,3},{7,4},{6,5},{5,6},{4,7},{10,9},{11,8},{8,1... | collective-permute-start | bytes 86024 | tf_op jit(solution)/shard_map/ppermute | solution.py:56
  35.5 1.4 %collective-permute-start.14 = (bf16[64,896]{1,0:T(8,128)(2,1)S(1)}, bf16[64,896]{1,0:T(8,128)(2,1)S(1)}, u32[]{:S(2)}, u32[]{:S(2)}) collective-permute-start(bf16[64,896]{1,0:T(8,128)(2,1)S(1)} %collect.1.refs_0_), channel_id=1, source_target_pairs={{1,0},{0,1},{3,2},{2,3},{5,4},{4,5},{7,6},{6,7},{8,9},{9,8},{10,11... | collective-permute-start | bytes 344072 | tf_op jit(solution)/shard_map/ppermute | solution.py:56

commit v5 on v4

--- a/solution.py
+++ b/solution.py
@@ -248,7 +248,7 @@
     moved = jnp.where(lax.rem(lane, 2) == 0, ahead, behind)
     gram = jnp.where(moves, 0.0, gram) + moved
     pieces = split3(gram + gram.T)
-    chunks = done.shape[0] - 1
+    chunks = done.shape[0] - 2
     size = columns // chunks
     copies = []
     for n in range(chunks):
@@ -260,13 +260,18 @@
         power = power * (image_scale * image_scale)
         gain = jnp.broadcast_to(image_scale * lax.rsqrt(power / total_rows + 1e-06), product.shape)
         weights[here, :] = product * gain
-        image = dot(left, slabs_ref[:samples, :], ((1,), (0,)))
-        basis[here, :] = (image * jnp.concatenate([gain] * (image.shape[1] // samples), axis=1)).astype(BF16)
-        copies.append(pltpu.make_async_copy(basis.at[here], basis_ref.at[here], done.at[n]))
-        copies[-1].start()
+        step = size if n else size // 2
+        for start in range(0, size, step):
+            rows = slice(start, start + step)
+            here = pl.ds(n * size + start, step)
+            image = dot(left[rows], slabs_ref[:samples, :], ((1,), (0,)))
+            scale = jnp.concatenate([gain[rows]] * (image.shape[1] // samples), axis=1)
+            basis[here, :] = (image * scale).astype(BF16)
+            copies.append(pltpu.make_async_copy(basis.at[here], basis_ref.at[here], done.at[len(copies)]))
+            copies[-1].start()
     chosen = weights[rows_at(own, back.shape[0]), :].astype(BF16)
     back[...] = dot(chosen, slabs_ref[samples:, :], ((1,), (0,))) * back_scale
-    copies.append(pltpu.make_async_copy(back, back_ref, done.at[chunks]))
+    copies.append(pltpu.make_async_copy(back, back_ref, done.at[len(copies)]))
     copies[-1].start()
     for copy in copies:
         copy.wait()
@@ -325,7 +330,7 @@
         [stream_slab, stream_sibling, temp_sibling],
         [((2 * height, local_rows), BF16)],
     )
-    beside = beside_step(beside, 0)
+    beside = beside_step(beside, 1)
     (message,) = call(add_kernel, "add", around(message, "y"), [((height, wide), F32)])
     (across,) = call(relay_kernel, "relay", [beside, near, other, message], [((2 * height, local_rows), BF16)])
     across = beside_step(across, 1)
@@ -363,7 +368,7 @@
             pltpu.VMEM((columns, samples), F32),
             pltpu.VMEM((samples, packed), BF16),
             *[pltpu.VMEM(out.shape, out.dtype) for out in outs],
-            pltpu.SemaphoreType.DMA((chunks + 1,)),
+            pltpu.SemaphoreType.DMA((chunks + 2,)),
         ],
         compiler_params=params(40),
         cost_estimate=cost(2 * (columns + mine) * samples * local_rows, 7 << 20),

time: 40.2 us -> 39.9 us (level)
  starting transfers between devices: 22.1 us -> 20.8 us
  waiting for transfers between devices: 12 us -> 13.1 us
    ppermute x18, starting transfers between devices: 22.1 us -> 20.8 us  [move(): return lax.ppermute(value, ('rows', 'samp'), pairs)]
    ppermute x18, waiting for transfers between devices: 12 us -> 13.1 us  [move(): return lax.ppermute(value, ('rows', 'samp'), pairs)]
  transfers between devices with their start and end apart: 18 -> 18, of which waited for: 10 -> 11; matrix products, arithmetic and copies ran while one was open for 0% -> 0% of each run, Pallas kernels for 5% -> 5%
where the time goes in v5:
time: 39.9 us; the launch traced here: 39.8 us
  starting transfers between devices  20.8 us (52%)
  waiting for transfers between devices  13.1 us (33%)
  Pallas kernels  5.18 us (13%)
  between operations  0.75 us (2%)
    ppermute x18, starting transfers between devices, move(): return lax.ppermute(value, ('rows', 'samp'), pairs)  20.8 us
    ppermute x18, waiting for transfers between devices, move(): return lax.ppermute(value, ('rows', 'samp'), pairs)  13.1 us
    pallas_call x1, Pallas kernels, shards(): pl.pallas_call(functools.partial(output_kernel, columns, scales), out_sha...  3.22 us
    pallas_call x13, Pallas kernels, call(): pl.pallas_call(kernel, out_shape=tuple(outs), in_specs=whole(len(operands...  1.96 us
  transfers between devices with their start and end apart: 18, of which 11 were waited for; matrix products, arithmetic and copies ran while one was open for 0% of the time, Pallas kernels for 5%

profile of v5, /device:TPU:1, one launch (start us, length us, event | category | flops | bytes accessed | tf_op | source)
XLA Modules:
  0.0 39.8 jit_solution(14396798605765561782)
XLA Ops:
  0.6 0.0 copy-start.2
  0.6 0.0 copy-start.1
  0.6 0.0 copy-start
  0.7 2.1 %collective-permute-start.3 = (bf16[16,4096]{1,0:T(8,128)(2,1)}, bf16[16,4096]{1,0:T(8,128)(2,1)S(1)}, u32[]{:S(2)}, u32[]{:S(2)}) collective-permute-start(bf16[16,4096]{1,0:T(8,128)(2,1)} %temp_ref.1), channel_id=1, source_target_pairs={{2,0},{3,1},{0,2},{1,3},{6,4},{7,5},{4,6},{5,7},{10,9},{11,8},{8,1... | collective-permute-start | bytes 393224 | tf_op jit(solution)/shard_map/ppermute | solution.py:56
  2.8 1.8 %collective-permute-start.2 = (bf16[16,4096]{1,0:T(8,128)(2,1)}, bf16[16,4096]{1,0:T(8,128)(2,1)S(1)}, u32[]{:S(2)}, u32[]{:S(2)}) collective-permute-start(bf16[16,4096]{1,0:T(8,128)(2,1)} %temp_ref.1), channel_id=1, source_target_pairs={{6,0},{7,1},{4,2},{5,3},{2,4},{3,5},{0,6},{1,7},{14,9},{15,8},{12,... | collective-permute-start | bytes 393224 | tf_op jit(solution)/shard_map/ppermute | solution.py:56
  4.6 1.2 %collective-permute-start = (bf16[16,4096]{1,0:T(8,128)(2,1)}, bf16[16,4096]{1,0:T(8,128)(2,1)S(1)}, u32[]{:S(2)}, u32[]{:S(2)}) collective-permute-start(bf16[16,4096]{1,0:T(8,128)(2,1)} %stream_ref.3), channel_id=1, source_target_pairs={{1,0},{0,1},{3,2},{2,3},{5,4},{4,5},{7,6},{6,7},{8,9},{9,8},{10,11... | collective-permute-start | bytes 393224 | tf_op jit(solution)/shard_map/ppermute | solution.py:56
  5.8 0.0 copy-done.2
  5.8 0.1 collective-permute-start.1
  5.9 1.1 %collective-permute-done.sibling_ref.stream_sibling_ref = bf16[16,4096]{1,0:T(8,128)(2,1)S(1)} collective-permute-done((bf16[16,4096]{1,0:T(8,128)(2,1)}, bf16[16,4096]{1,0:T(8,128)(2,1)S(1)}, u32[]{:S(2)}, u32[]{:S(2)}) %collective-permute-start) | collective-permute-done | bytes 131104 | tf_op jit(solution)/shard_map/ppermute | solution.py:56
  7.0 0.0 copy-done.1
  7.0 0.0 copy-done
  7.0 1.2 %part.1._.part_ref = f32[16,512]{1,0:T(8,128)S(1)} custom-call(bf16[16,4096]{1,0:T(8,128)(2,1)S(1)} %copy-done.1, bf16[16,4096]{1,0:T(8,128)(2,1)S(1)} %collective-permute-done.sibling_ref.stream_sibling_ref, bf16[512,4096]{1,0:T(8,128)(2,1)S(1)} %copy-done), custom_call_target="tpu_custom_call" | custom-call | flops 67108864 | bytes 4489216 | tf_op jit(solution)/shard_map/part/pallas_call | solution.py:294
  8.2 0.0 collective-permute-done.3.value_ref
  8.2 0.4 %collective-permute-start.4 = (bf16[16,4096]{1,0:T(8,128)(2,1)S(1)}, bf16[16,4096]{1,0:T(8,128)(2,1)S(1)}, u32[]{:S(2)}, u32[]{:S(2)}) collective-permute-start(bf16[16,4096]{1,0:T(8,128)(2,1)S(1)} %near.1.near_ref), channel_id=1, source_target_pairs={{1,0},{0,1},{3,2},{2,3},{5,4},{4,5},{7,6},{6,7},{8,9},{9,8},{10,11... | collective-permute-start | bytes 393224 | tf_op jit(solution)/shard_map/ppermute | solution.py:56
  8.7 0.0 collective-permute-done.1.sibling_ref._.temp_sibling_ref
  8.7 0.4 %collective-permute-start.15 = (bf16[32,4096]{1,0:T(8,128)(2,1)S(1)}, bf16[32,4096]{1,0:T(8,128)(2,1)S(1)}, u32[]{:S(2)}, u32[]{:S(2)}) collective-permute-start(bf16[32,4096]{1,0:T(8,128)(2,1)S(1)} %beside.1), channel_id=1, source_target_pairs={{3,0},{6,1},{1,2},{4,3},{7,4},{2,5},{5,6},{0,7},{10,9},{15,8},{8,1... | collective-permute-start | bytes 786440 | tf_op jit(solution)/shard_map/ppermute | solution.py:56
  9.1 0.0 collective-permute-done.2.value_ref
  9.2 0.5 %collective-permute-done.4.near_sibling_ref = bf16[16,4096]{1,0:T(8,128)(2,1)S(1)} collective-permute-done((bf16[16,4096]{1,0:T(8,128)(2,1)S(1)}, bf16[16,4096]{1,0:T(8,128)(2,1)S(1)}, u32[]{:S(2)}, u32[]{:S(2)}) %collective-permute-start.4) | collective-permute-done | bytes 131104 | tf_op jit(solution)/shard_map/ppermute | solution.py:56
  9.7 0.4 %gram.1.a_ref = f32[16,640]{1,0:T(8,128)S(1)} custom-call(f32[16,512]{1,0:T(8,128)S(1)} %part.1._.part_ref, bf16[16,4096]{1,0:T(8,128)(2,1)S(1)} %copy-done.2, bf16[16,4096]{1,0:T(8,128)(2,1)S(1)} %collective-permute-done.1.sibling_ref._.temp_sibling_ref, bf16[16,4096]{1,0:T(8,128)(2,1)S(1)} %other.1.other_ref, bf16[16,4096]{1,0:T(8,128)(2,1)S(1)} %near.1.near_ref, ...), custom_call_target="tpu_custom_call" | custom-call | flops 16777216 | bytes 729088 | tf_op jit(solution)/shard_map/gram/pallas_call | solution.py:294
  10.1 2.9 %collective-permute-start.7 = (f32[16,640]{1,0:T(8,128)S(1)}, f32[16,640]{1,0:T(8,128)S(1)}, u32[]{:S(2)}, u32[]{:S(2)}) collective-permute-start(f32[16,640]{1,0:T(8,128)S(1)} %gram.1.a_ref), channel_id=1, source_target_pairs={{16,0},{17,1},{18,2},{19,3},{20,4},{21,5},{22,6},{23,7},{25,9},{24... | collective-permute-start | bytes 122888 | tf_op jit(solution)/shard_map/ppermute | solution.py:56
  13.1 1.4 %collective-permute-start.6 = (f32[16,640]{1,0:T(8,128)S(1)}, f32[16,640]{1,0:T(8,128)S(1)}, u32[]{:S(2)}, u32[]{:S(2)}) collective-permute-start(f32[16,640]{1,0:T(8,128)S(1)} %gram.1.a_ref), channel_id=1, source_target_pairs={{25,0},{24,1},{27,2},{26,3},{29,4},{28,5},{31,6},{30,7},{16,9},{17... | collective-permute-start | bytes 122888 | tf_op jit(solution)/shard_map/ppermute | solution.py:56
  14.4 0.0 collective-permute-start.5
  14.4 0.1 collective-permute-done.7.d_ref
  14.5 3.2 %collective-permute-done.6.c_ref = f32[16,640]{1,0:T(8,128)S(1)} collective-permute-done((f32[16,640]{1,0:T(8,128)S(1)}, f32[16,640]{1,0:T(8,128)S(1)}, u32[]{:S(2)}, u32[]{:S(2)}) %collective-permute-start.6) | collective-permute-done | bytes 40992 | tf_op jit(solution)/shard_map/ppermute | solution.py:56
  17.7 0.5 %collective-permute-done.5.b_ref = f32[16,640]{1,0:T(8,128)S(1)} collective-permute-done((f32[16,640]{1,0:T(8,128)S(1)}, f32[16,640]{1,0:T(8,128)S(1)}, u32[]{:S(2)}, u32[]{:S(2)}) %collective-permute-start.5) | collective-permute-done | bytes 40992 | tf_op jit(solution)/shard_map/ppermute | solution.py:56
  18.2 0.0 collective-permute-done.15.beside_ref
  18.3 1.2 %collective-permute-start.16 = (bf16[32,4096]{1,0:T(8,128)(2,1)S(1)}, bf16[32,4096]{1,0:T(8,128)(2,1)S(1)}, u32[]{:S(2)}, u32[]{:S(2)}) collective-permute-start(bf16[32,4096]{1,0:T(8,128)(2,1)S(1)} %relay.1), channel_id=1, source_target_pairs={{3,0},{6,1},{1,2},{4,3},{7,4},{2,5},{5,6},{0,7},{10,9},{15,8},{8,1... | collective-permute-start | bytes 786440 | tf_op jit(solution)/shard_map/ppermute | solution.py:56
  19.5 3.6 %collective-permute-start.10 = (f32[16,640]{1,0:T(8,128)S(1)}, f32[16,640]{1,0:T(8,128)S(1)}, u32[]{:S(2)}, u32[]{:S(2)}) collective-permute-start(f32[16,640]{1,0:T(8,128)S(1)} %add.1.a_ref._), channel_id=1, source_target_pairs={{64,0},{65,1},{66,2},{67,3},{68,4},{69,5},{70,6},{71,7},{73,9},{72... | collective-permute-start | bytes 122888 | tf_op jit(solution)/shard_map/ppermute | solution.py:56
  23.1 0.6 %collective-permute-start.9 = (f32[16,640]{1,0:T(8,128)S(1)}, f32[16,640]{1,0:T(8,128)S(1)}, u32[]{:S(2)}, u32[]{:S(2)}) collective-permute-start(f32[16,640]{1,0:T(8,128)S(1)} %add.1.a_ref._), channel_id=1, source_target_pairs={{97,0},{96,1},{99,2},{98,3},{101,4},{100,5},{103,6},{102,7},{104,9... | collective-permute-start | bytes 122888 | tf_op jit(solution)/shard_map/ppermute | solution.py:56
  23.7 0.3 collective-permute-start.8
  24.0 0.5 %collective-permute-done.10.d_ref = f32[16,640]{1,0:T(8,128)S(1)} collective-permute-done((f32[16,640]{1,0:T(8,128)S(1)}, f32[16,640]{1,0:T(8,128)S(1)}, u32[]{:S(2)}, u32[]{:S(2)}) %collective-permute-start.10) | collective-permute-done | bytes 40992 | tf_op jit(solution)/shard_map/ppermute | solution.py:56
  24.5 3.2 %collective-permute-done.9.c_ref = f32[16,640]{1,0:T(8,128)S(1)} collective-permute-done((f32[16,640]{1,0:T(8,128)S(1)}, f32[16,640]{1,0:T(8,128)S(1)}, u32[]{:S(2)}, u32[]{:S(2)}) %collective-permute-start.9) | collective-permute-done | bytes 40992 | tf_op jit(solution)/shard_map/ppermute | solution.py:56
  27.8 0.0 collective-permute-done.8.b_ref
  27.8 0.0 collective-permute-done.16.across_ref
  27.8 1.4 %collective-permute-start.17 = (bf16[80,4096]{1,0:T(8,128)(2,1)S(1)}, bf16[80,4096]{1,0:T(8,128)(2,1)S(1)}, u32[]{:S(2)}, u32[]{:S(2)}) collective-permute-start(bf16[80,4096]{1,0:T(8,128)(2,1)S(1)} %both.1), channel_id=1, source_target_pairs={{1,0},{0,1},{3,2},{2,3},{5,4},{4,5},{7,6},{6,7},{8,9},{9,8},{10,11... | collective-permute-start | bytes 1966088 | tf_op jit(solution)/shard_map/ppermute | solution.py:56
  29.2 1.2 %collective-permute-start.13 = (bf16[16,896]{1,0:T(8,128)(2,1)S(1)}, bf16[16,896]{1,0:T(8,128)(2,1)S(1)}, u32[]{:S(2)}, u32[]{:S(2)}) collective-permute-start(bf16[16,896]{1,0:T(8,128)(2,1)S(1)} %total.1.refs_0_._), channel_id=1, source_target_pairs={{5,0},{4,1},{7,2},{6,3},{1,4},{0,5},{3,6},{2,7},{12,9},{13,8},{14,... | collective-permute-start | bytes 86024 | tf_op jit(solution)/shard_map/ppermute | solution.py:56
  30.4 1.4 %collective-permute-start.12 = (bf16[16,896]{1,0:T(8,128)(2,1)S(1)}, bf16[16,896]{1,0:T(8,128)(2,1)S(1)}, u32[]{:S(2)}, u32[]{:S(2)}) collective-permute-start(bf16[16,896]{1,0:T(8,128)(2,1)S(1)} %total.1.refs_0_._), channel_id=1, source_target_pairs={{7,0},{6,1},{5,2},{4,3},{3,4},{2,5},{1,6},{0,7},{14,9},{15,8},{12,... | collective-permute-start | bytes 86024 | tf_op jit(solution)/shard_map/ppermute | solution.py:56
  31.9 0.3 collective-permute-start.11
  32.1 1.9 %collective-permute-done.13.refs_3_ = bf16[16,896]{1,0:T(8,128)(2,1)S(1)} collective-permute-done((bf16[16,896]{1,0:T(8,128)(2,1)S(1)}, bf16[16,896]{1,0:T(8,128)(2,1)S(1)}, u32[]{:S(2)}, u32[]{:S(2)}) %collective-permute-start.13) | collective-permute-done | bytes 28704 | tf_op jit(solution)/shard_map/ppermute | solution.py:56
  34.0 0.9 %collective-permute-done.12.refs_2_ = bf16[16,896]{1,0:T(8,128)(2,1)S(1)} collective-permute-done((bf16[16,896]{1,0:T(8,128)(2,1)S(1)}, bf16[16,896]{1,0:T(8,128)(2,1)S(1)}, u32[]{:S(2)}, u32[]{:S(2)}) %collective-permute-start.12) | collective-permute-done | bytes 28704 | tf_op jit(solution)/shard_map/ppermute | solution.py:56
  34.9 0.2 collective-permute-done.11.refs_1_
  35.2 0.4 %collective-permute-start.14 = (bf16[64,896]{1,0:T(8,128)(2,1)S(1)}, bf16[64,896]{1,0:T(8,128)(2,1)S(1)}, u32[]{:S(2)}, u32[]{:S(2)}) collective-permute-start(bf16[64,896]{1,0:T(8,128)(2,1)S(1)} %collect.1.refs_0_), channel_id=1, source_target_pairs={{1,0},{0,1},{3,2},{2,3},{5,4},{4,5},{7,6},{6,7},{8,9},{9,8},{10,11... | collective-permute-start | bytes 344072 | tf_op jit(solution)/shard_map/ppermute | solution.py:56
  35.6 0.0 collective-permute-done.17.both_ref
  35.6 0.2 order.1.refs_2_
  35.7 0.8 %collective-permute-done.14.refs_1_ = bf16[64,896]{1,0:T(8,128)(2,1)S(1)} collective-permute-done((bf16[64,896]{1,0:T(8,128)(2,1)S(1)}, bf16[64,896]{1,0:T(8,128)(2,1)S(1)}, u32[]{:S(2)}, u32[]{:S(2)}) %collective-permute-start.14) | collective-permute-done | bytes 114720 | tf_op jit(solution)/shard_map/ppermute | solution.py:56
  36.6 3.2 %outputs.1 = (bf16[512,4096]{1,0:T(8,128)(2,1)}, f32[64,4096]{1,0:T(8,128)}) custom-call(bf16[64,896]{1,0:T(8,128)(2,1)S(1)} %collect.1.refs_0_, bf16[64,896]{1,0:T(8,128)(2,1)S(1)} %collective-permute-done.14.refs_1_, bf16[256,4096]{1,0:T(8,128)(2,1)S(1)} %order.1.refs_2_), custom_call_target="tpu_custom_call" | custom-call | flops 603979776 | bytes 7340032 | tf_op jit(solution)/shard_map/outputs/pallas_call | solution.py:362
  (10 shorter events, 0.2 us)
Async XLA Ops:
  0.6 5.2 %copy-start.2 = (bf16[16,4096]{1,0:T(8,128)(2,1)S(1)}, bf16[16,4096]{1,0:T(8,128)(2,1)}, u32[]{:S(2)}) copy-start(bf16[16,4096]{1,0:T(8,128)(2,1)} %temp_ref.1) | copy-start | bytes 393220
  0.6 6.4 %copy-start.1 = (bf16[16,4096]{1,0:T(8,128)(2,1)S(1)}, bf16[16,4096]{1,0:T(8,128)(2,1)}, u32[]{:S(2)}) copy-start(bf16[16,4096]{1,0:T(8,128)(2,1)} %stream_ref.3) | copy-start | bytes 393220
  0.6 6.4 %copy-start = (bf16[512,4096]{1,0:T(8,128)(2,1)S(1)}, bf16[512,4096]{1,0:T(8,128)(2,1)}, u32[]{:S(2)}) copy-start(bf16[512,4096]{1,0:T(8,128)(2,1)} %probe_ref.1) | copy-start | bytes 12582916
  0.7 7.6 %collective-permute-start.3 = (bf16[16,4096]{1,0:T(8,128)(2,1)}, bf16[16,4096]{1,0:T(8,128)(2,1)S(1)}, u32[]{:S(2)}, u32[]{:S(2)}) collective-permute-start(bf16[16,4096]{1,0:T(8,128)(2,1)} %temp_ref.1), channel_id=1, source_target_pairs={{2,0},{3,1},{0,2},{1,3},{6,4},{7,5},{4,6},{5,7},{10,9},{11,8},{8,1... | collective-permute-start | bytes 393224 | tf_op jit(solution)/shard_map/ppermute | solution.py:56
  2.8 6.4 %collective-permute-start.2 = (bf16[16,4096]{1,0:T(8,128)(2,1)}, bf16[16,4096]{1,0:T(8,128)(2,1)S(1)}, u32[]{:S(2)}, u32[]{:S(2)}) collective-permute-start(bf16[16,4096]{1,0:T(8,128)(2,1)} %temp_ref.1), channel_id=1, source_target_pairs={{6,0},{7,1},{4,2},{5,3},{2,4},{3,5},{0,6},{1,7},{14,9},{15,8},{12,... | collective-permute-start | bytes 393224 | tf_op jit(solution)/shard_map/ppermute | solution.py:56
  4.6 2.4 %collective-permute-start = (bf16[16,4096]{1,0:T(8,128)(2,1)}, bf16[16,4096]{1,0:T(8,128)(2,1)S(1)}, u32[]{:S(2)}, u32[]{:S(2)}) collective-permute-start(bf16[16,4096]{1,0:T(8,128)(2,1)} %stream_ref.3), channel_id=1, source_target_pairs={{1,0},{0,1},{3,2},{2,3},{5,4},{4,5},{7,6},{6,7},{8,9},{9,8},{10,11... | collective-permute-start | bytes 393224 | tf_op jit(solution)/shard_map/ppermute | solution.py:56
  5.8 2.8 %collective-permute-start.1 = (bf16[16,4096]{1,0:T(8,128)(2,1)S(1)}, bf16[16,4096]{1,0:T(8,128)(2,1)S(1)}, u32[]{:S(2)}, u32[]{:S(2)}) collective-permute-start(bf16[16,4096]{1,0:T(8,128)(2,1)S(1)} %ahead.1), channel_id=1, source_target_pairs={{1,0},{0,1},{3,2},{2,3},{5,4},{4,5},{7,6},{6,7},{8,9},{9,8},{10,11... | collective-permute-start | bytes 393224 | tf_op jit(solution)/shard_map/ppermute | solution.py:56
  8.2 1.4 %collective-permute-start.4 = (bf16[16,4096]{1,0:T(8,128)(2,1)S(1)}, bf16[16,4096]{1,0:T(8,128)(2,1)S(1)}, u32[]{:S(2)}, u32[]{:S(2)}) collective-permute-start(bf16[16,4096]{1,0:T(8,128)(2,1)S(1)} %near.1.near_ref), channel_id=1, source_target_pairs={{1,0},{0,1},{3,2},{2,3},{5,4},{4,5},{7,6},{6,7},{8,9},{9,8},{10,11... | collective-permute-start | bytes 393224 | tf_op jit(solution)/shard_map/ppermute | solution.py:56
  8.7 9.5 %collective-permute-start.15 = (bf16[32,4096]{1,0:T(8,128)(2,1)S(1)}, bf16[32,4096]{1,0:T(8,128)(2,1)S(1)}, u32[]{:S(2)}, u32[]{:S(2)}) collective-permute-start(bf16[32,4096]{1,0:T(8,128)(2,1)S(1)} %beside.1), channel_id=1, source_target_pairs={{3,0},{6,1},{1,2},{4,3},{7,4},{2,5},{5,6},{0,7},{10,9},{15,8},{8,1... | collective-permute-start | bytes 786440 | tf_op jit(solution)/shard_map/ppermute | solution.py:56
  10.1 4.4 %collective-permute-start.7 = (f32[16,640]{1,0:T(8,128)S(1)}, f32[16,640]{1,0:T(8,128)S(1)}, u32[]{:S(2)}, u32[]{:S(2)}) collective-permute-start(f32[16,640]{1,0:T(8,128)S(1)} %gram.1.a_ref), channel_id=1, source_target_pairs={{16,0},{17,1},{18,2},{19,3},{20,4},{21,5},{22,6},{23,7},{25,9},{24... | collective-permute-start | bytes 122888 | tf_op jit(solution)/shard_map/ppermute | solution.py:56
  13.1 4.6 %collective-permute-start.6 = (f32[16,640]{1,0:T(8,128)S(1)}, f32[16,640]{1,0:T(8,128)S(1)}, u32[]{:S(2)}, u32[]{:S(2)}) collective-permute-start(f32[16,640]{1,0:T(8,128)S(1)} %gram.1.a_ref), channel_id=1, source_target_pairs={{25,0},{24,1},{27,2},{26,3},{29,4},{28,5},{31,6},{30,7},{16,9},{17... | collective-permute-start | bytes 122888 | tf_op jit(solution)/shard_map/ppermute | solution.py:56
  14.4 3.8 %collective-permute-start.5 = (f32[16,640]{1,0:T(8,128)S(1)}, f32[16,640]{1,0:T(8,128)S(1)}, u32[]{:S(2)}, u32[]{:S(2)}) collective-permute-start(f32[16,640]{1,0:T(8,128)S(1)} %gram.1.a_ref), channel_id=1, source_target_pairs={{9,0},{8,1},{11,2},{10,3},{13,4},{12,5},{15,6},{14,7},{0,9},{1,8},... | collective-permute-start | bytes 122888 | tf_op jit(solution)/shard_map/ppermute | solution.py:56
  18.3 9.5 %collective-permute-start.16 = (bf16[32,4096]{1,0:T(8,128)(2,1)S(1)}, bf16[32,4096]{1,0:T(8,128)(2,1)S(1)}, u32[]{:S(2)}, u32[]{:S(2)}) collective-permute-start(bf16[32,4096]{1,0:T(8,128)(2,1)S(1)} %relay.1), channel_id=1, source_target_pairs={{3,0},{6,1},{1,2},{4,3},{7,4},{2,5},{5,6},{0,7},{10,9},{15,8},{8,1... | collective-permute-start | bytes 786440 | tf_op jit(solution)/shard_map/ppermute | solution.py:56
  19.5 5.0 %collective-permute-start.10 = (f32[16,640]{1,0:T(8,128)S(1)}, f32[16,640]{1,0:T(8,128)S(1)}, u32[]{:S(2)}, u32[]{:S(2)}) collective-permute-start(f32[16,640]{1,0:T(8,128)S(1)} %add.1.a_ref._), channel_id=1, source_target_pairs={{64,0},{65,1},{66,2},{67,3},{68,4},{69,5},{70,6},{71,7},{73,9},{72... | collective-permute-start | bytes 122888 | tf_op jit(solution)/shard_map/ppermute | solution.py:56
  23.1 4.6 %collective-permute-start.9 = (f32[16,640]{1,0:T(8,128)S(1)}, f32[16,640]{1,0:T(8,128)S(1)}, u32[]{:S(2)}, u32[]{:S(2)}) collective-permute-start(f32[16,640]{1,0:T(8,128)S(1)} %add.1.a_ref._), channel_id=1, source_target_pairs={{97,0},{96,1},{99,2},{98,3},{101,4},{100,5},{103,6},{102,7},{104,9... | collective-permute-start | bytes 122888 | tf_op jit(solution)/shard_map/ppermute | solution.py:56
  23.7 4.1 %collective-permute-start.8 = (f32[16,640]{1,0:T(8,128)S(1)}, f32[16,640]{1,0:T(8,128)S(1)}, u32[]{:S(2)}, u32[]{:S(2)}) collective-permute-start(f32[16,640]{1,0:T(8,128)S(1)} %add.1.a_ref._), channel_id=1, source_target_pairs={{33,0},{32,1},{35,2},{34,3},{37,4},{36,5},{39,6},{38,7},{40,9},{41... | collective-permute-start | bytes 122888 | tf_op jit(solution)/shard_map/ppermute | solution.py:56
  27.8 7.7 %collective-permute-start.17 = (bf16[80,4096]{1,0:T(8,128)(2,1)S(1)}, bf16[80,4096]{1,0:T(8,128)(2,1)S(1)}, u32[]{:S(2)}, u32[]{:S(2)}) collective-permute-start(bf16[80,4096]{1,0:T(8,128)(2,1)S(1)} %both.1), channel_id=1, source_target_pairs={{1,0},{0,1},{3,2},{2,3},{5,4},{4,5},{7,6},{6,7},{8,9},{9,8},{10,11... | collective-permute-start | bytes 1966088 | tf_op jit(solution)/shard_map/ppermute | solution.py:56
  29.2 4.8 %collective-permute-start.13 = (bf16[16,896]{1,0:T(8,128)(2,1)S(1)}, bf16[16,896]{1,0:T(8,128)(2,1)S(1)}, u32[]{:S(2)}, u32[]{:S(2)}) collective-permute-start(bf16[16,896]{1,0:T(8,128)(2,1)S(1)} %total.1.refs_0_._), channel_id=1, source_target_pairs={{5,0},{4,1},{7,2},{6,3},{1,4},{0,5},{3,6},{2,7},{12,9},{13,8},{14,... | collective-permute-start | bytes 86024 | tf_op jit(solution)/shard_map/ppermute | solution.py:56
  30.4 4.5 %collective-permute-start.12 = (bf16[16,896]{1,0:T(8,128)(2,1)S(1)}, bf16[16,896]{1,0:T(8,128)(2,1)S(1)}, u32[]{:S(2)}, u32[]{:S(2)}) collective-permute-start(bf16[16,896]{1,0:T(8,128)(2,1)S(1)} %total.1.refs_0_._), channel_id=1, source_target_pairs={{7,0},{6,1},{5,2},{4,3},{3,4},{2,5},{1,6},{0,7},{14,9},{15,8},{12,... | collective-permute-start | bytes 86024 | tf_op jit(solution)/shard_map/ppermute | solution.py:56
  31.9 3.3 %collective-permute-start.11 = (bf16[16,896]{1,0:T(8,128)(2,1)S(1)}, bf16[16,896]{1,0:T(8,128)(2,1)S(1)}, u32[]{:S(2)}, u32[]{:S(2)}) collective-permute-start(bf16[16,896]{1,0:T(8,128)(2,1)S(1)} %total.1.refs_0_._), channel_id=1, source_target_pairs={{3,0},{2,1},{1,2},{0,3},{7,4},{6,5},{5,6},{4,7},{10,9},{11,8},{8,1... | collective-permute-start | bytes 86024 | tf_op jit(solution)/shard_map/ppermute | solution.py:56
  35.2 1.4 %collective-permute-start.14 = (bf16[64,896]{1,0:T(8,128)(2,1)S(1)}, bf16[64,896]{1,0:T(8,128)(2,1)S(1)}, u32[]{:S(2)}, u32[]{:S(2)}) collective-permute-start(bf16[64,896]{1,0:T(8,128)(2,1)S(1)} %collect.1.refs_0_), channel_id=1, source_target_pairs={{1,0},{0,1},{3,2},{2,3},{5,4},{4,5},{7,6},{6,7},{8,9},{9,8},{10,11... | collective-permute-start | bytes 344072 | tf_op jit(solution)/shard_map/ppermute | solution.py:56

commit v6 on v5

--- a/solution.py
+++ b/solution.py
@@ -315,7 +315,7 @@
         part_kernel, "part", [stream_slab, stream_sibling, probe], [((height, columns), F32)], work=2 * height * columns * local_rows
     )
     (near,) = call(copy_kernel, "near", [near, part], [slab], work=LEAD_WORK)
-    (other,) = call(copy_kernel, "other", [other, part], [slab], work=LEAD_WORK)
+    (other,) = call(copy_kernel, "other", [other, near], [slab], work=LEAD_WORK)
     near_sibling = sibling(near)
     (message,) = call(
         gram_kernel,
@@ -331,11 +331,11 @@
         [((2 * height, local_rows), BF16)],
     )
     beside = beside_step(beside, 1)
-    (message,) = call(add_kernel, "add", around(message, "y"), [((height, wide), F32)])
+    (message,) = call(add_kernel, "add", around(message, "z"), [((height, wide), F32)])
     (across,) = call(relay_kernel, "relay", [beside, near, other, message], [((2 * height, local_rows), BF16)])
     across = beside_step(across, 1)
     (message,) = call(
-        functools.partial(sum_kernel, columns), "total", around(message, "z"), [((height, packed), BF16)]
+        functools.partial(sum_kernel, columns), "total", around(message, "y"), [((height, packed), BF16)]
     )
     (both,) = call(both_kernel, "both", [beside, other, across, message], [((5 * height, local_rows), BF16)])
     both_sibling = sibling(both)

time: 39.9 us -> 40 us (level)
  transfers between devices with their start and end apart: 18 -> 18, of which waited for: 11 -> 10; matrix products, arithmetic and copies ran while one was open for 0% -> 0% of each run, Pallas kernels for 5% -> 5%
where the time goes in v6:
time: 40 us; the launch traced here: 39.9 us
  starting transfers between devices  21.2 us (53%)
  waiting for transfers between devices  12.8 us (32%)
  Pallas kernels  5.17 us (13%)
  between operations  0.75 us (2%)
    ppermute x18, starting transfers between devices, move(): return lax.ppermute(value, ('rows', 'samp'), pairs)  21.2 us
    ppermute x18, waiting for transfers between devices, move(): return lax.ppermute(value, ('rows', 'samp'), pairs)  12.8 us
    pallas_call x1, Pallas kernels, shards(): pl.pallas_call(functools.partial(output_kernel, columns, scales), out_sha...  3.21 us
    pallas_call x13, Pallas kernels, call(): pl.pallas_call(kernel, out_shape=tuple(outs), in_specs=whole(len(operands...  1.96 us
  transfers between devices with their start and end apart: 18, of which 10 were waited for; matrix products, arithmetic and copies ran while one was open for 0% of the time, Pallas kernels for 5%

profile of v6, /device:TPU:1, one launch (start us, length us, event | category | flops | bytes accessed | tf_op | source)
XLA Modules:
  0.0 39.9 jit_solution(10463645293337116319)
XLA Ops:
  0.6 0.0 copy-start.2
  0.6 0.0 copy-start.1
  0.6 0.0 copy-start
  0.7 2.1 %collective-permute-start.3 = (bf16[16,4096]{1,0:T(8,128)(2,1)}, bf16[16,4096]{1,0:T(8,128)(2,1)S(1)}, u32[]{:S(2)}, u32[]{:S(2)}) collective-permute-start(bf16[16,4096]{1,0:T(8,128)(2,1)} %temp_ref.1), channel_id=1, source_target_pairs={{2,0},{3,1},{0,2},{1,3},{6,4},{7,5},{4,6},{5,7},{10,9},{11,8},{8,1... | collective-permute-start | bytes 393224 | tf_op jit(solution)/shard_map/ppermute | solution.py:56
  2.8 1.8 %collective-permute-start.2 = (bf16[16,4096]{1,0:T(8,128)(2,1)}, bf16[16,4096]{1,0:T(8,128)(2,1)S(1)}, u32[]{:S(2)}, u32[]{:S(2)}) collective-permute-start(bf16[16,4096]{1,0:T(8,128)(2,1)} %temp_ref.1), channel_id=1, source_target_pairs={{6,0},{7,1},{4,2},{5,3},{2,4},{3,5},{0,6},{1,7},{14,9},{15,8},{12,... | collective-permute-start | bytes 393224 | tf_op jit(solution)/shard_map/ppermute | solution.py:56
  4.6 1.2 %collective-permute-start = (bf16[16,4096]{1,0:T(8,128)(2,1)}, bf16[16,4096]{1,0:T(8,128)(2,1)S(1)}, u32[]{:S(2)}, u32[]{:S(2)}) collective-permute-start(bf16[16,4096]{1,0:T(8,128)(2,1)} %stream_ref.3), channel_id=1, source_target_pairs={{1,0},{0,1},{3,2},{2,3},{5,4},{4,5},{7,6},{6,7},{8,9},{9,8},{10,11... | collective-permute-start | bytes 393224 | tf_op jit(solution)/shard_map/ppermute | solution.py:56
  5.8 0.0 copy-done.2
  5.8 0.1 collective-permute-start.1
  5.9 1.1 %collective-permute-done.sibling_ref.stream_sibling_ref = bf16[16,4096]{1,0:T(8,128)(2,1)S(1)} collective-permute-done((bf16[16,4096]{1,0:T(8,128)(2,1)}, bf16[16,4096]{1,0:T(8,128)(2,1)S(1)}, u32[]{:S(2)}, u32[]{:S(2)}) %collective-permute-start) | collective-permute-done | bytes 131104 | tf_op jit(solution)/shard_map/ppermute | solution.py:56
  7.0 0.0 copy-done.1
  7.0 0.0 copy-done
  7.0 1.2 %part.1._.part_ref = f32[16,512]{1,0:T(8,128)S(1)} custom-call(bf16[16,4096]{1,0:T(8,128)(2,1)S(1)} %copy-done.1, bf16[16,4096]{1,0:T(8,128)(2,1)S(1)} %collective-permute-done.sibling_ref.stream_sibling_ref, bf16[512,4096]{1,0:T(8,128)(2,1)S(1)} %copy-done), custom_call_target="tpu_custom_call" | custom-call | flops 67108864 | bytes 4489216 | tf_op jit(solution)/shard_map/part/pallas_call | solution.py:294
  8.2 0.0 collective-permute-done.3.value_ref
  8.2 0.4 %collective-permute-start.4 = (bf16[16,4096]{1,0:T(8,128)(2,1)S(1)}, bf16[16,4096]{1,0:T(8,128)(2,1)S(1)}, u32[]{:S(2)}, u32[]{:S(2)}) collective-permute-start(bf16[16,4096]{1,0:T(8,128)(2,1)S(1)} %near.1._.near_ref), channel_id=1, source_target_pairs={{1,0},{0,1},{3,2},{2,3},{5,4},{4,5},{7,6},{6,7},{8,9},{9,8},{10,11... | collective-permute-start | bytes 393224 | tf_op jit(solution)/shard_map/ppermute | solution.py:56
  8.7 0.0 collective-permute-done.1.sibling_ref._.temp_sibling_ref
  8.7 0.4 %collective-permute-start.15 = (bf16[32,4096]{1,0:T(8,128)(2,1)S(1)}, bf16[32,4096]{1,0:T(8,128)(2,1)S(1)}, u32[]{:S(2)}, u32[]{:S(2)}) collective-permute-start(bf16[32,4096]{1,0:T(8,128)(2,1)S(1)} %beside.1), channel_id=1, source_target_pairs={{3,0},{6,1},{1,2},{4,3},{7,4},{2,5},{5,6},{0,7},{10,9},{15,8},{8,1... | collective-permute-start | bytes 786440 | tf_op jit(solution)/shard_map/ppermute | solution.py:56
  9.1 0.0 collective-permute-done.2.value_ref
  9.2 0.5 %collective-permute-done.4.near_sibling_ref = bf16[16,4096]{1,0:T(8,128)(2,1)S(1)} collective-permute-done((bf16[16,4096]{1,0:T(8,128)(2,1)S(1)}, bf16[16,4096]{1,0:T(8,128)(2,1)S(1)}, u32[]{:S(2)}, u32[]{:S(2)}) %collective-permute-start.4) | collective-permute-done | bytes 131104 | tf_op jit(solution)/shard_map/ppermute | solution.py:56
  9.7 0.4 %gram.1.a_ref = f32[16,640]{1,0:T(8,128)S(1)} custom-call(f32[16,512]{1,0:T(8,128)S(1)} %part.1._.part_ref, bf16[16,4096]{1,0:T(8,128)(2,1)S(1)} %copy-done.2, bf16[16,4096]{1,0:T(8,128)(2,1)S(1)} %collective-permute-done.1.sibling_ref._.temp_sibling_ref, bf16[16,4096]{1,0:T(8,128)(2,1)S(1)} %other.1.other_ref, bf16[16,4096]{1,0:T(8,128)(2,1)S(1)} %near.1._.near_ref, ...), custom_call_target="tpu_custom_call" | custom-call | flops 16777216 | bytes 729088 | tf_op jit(solution)/shard_map/gram/pallas_call | solution.py:294
  10.1 3.6 %collective-permute-start.7 = (f32[16,640]{1,0:T(8,128)S(1)}, f32[16,640]{1,0:T(8,128)S(1)}, u32[]{:S(2)}, u32[]{:S(2)}) collective-permute-start(f32[16,640]{1,0:T(8,128)S(1)} %gram.1.a_ref), channel_id=1, source_target_pairs={{64,0},{65,1},{66,2},{67,3},{68,4},{69,5},{70,6},{71,7},{73,9},{72... | collective-permute-start | bytes 122888 | tf_op jit(solution)/shard_map/ppermute | solution.py:56
  13.7 1.0 %collective-permute-start.6 = (f32[16,640]{1,0:T(8,128)S(1)}, f32[16,640]{1,0:T(8,128)S(1)}, u32[]{:S(2)}, u32[]{:S(2)}) collective-permute-start(f32[16,640]{1,0:T(8,128)S(1)} %gram.1.a_ref), channel_id=1, source_target_pairs={{97,0},{96,1},{99,2},{98,3},{101,4},{100,5},{103,6},{102,7},{104,9... | collective-permute-start | bytes 122888 | tf_op jit(solution)/shard_map/ppermute | solution.py:56
  14.7 0.3 collective-permute-start.5
  15.0 0.1 collective-permute-done.7.d_ref
  15.1 3.2 %collective-permute-done.6.c_ref = f32[16,640]{1,0:T(8,128)S(1)} collective-permute-done((f32[16,640]{1,0:T(8,128)S(1)}, f32[16,640]{1,0:T(8,128)S(1)}, u32[]{:S(2)}, u32[]{:S(2)}) %collective-permute-start.6) | collective-permute-done | bytes 40992 | tf_op jit(solution)/shard_map/ppermute | solution.py:56
  18.4 0.2 collective-permute-done.5.b_ref
  18.6 0.0 collective-permute-done.15.beside_ref
  18.6 1.6 %collective-permute-start.16 = (bf16[32,4096]{1,0:T(8,128)(2,1)S(1)}, bf16[32,4096]{1,0:T(8,128)(2,1)S(1)}, u32[]{:S(2)}, u32[]{:S(2)}) collective-permute-start(bf16[32,4096]{1,0:T(8,128)(2,1)S(1)} %relay.1), channel_id=1, source_target_pairs={{3,0},{6,1},{1,2},{4,3},{7,4},{2,5},{5,6},{0,7},{10,9},{15,8},{8,1... | collective-permute-start | bytes 786440 | tf_op jit(solution)/shard_map/ppermute | solution.py:56
  20.2 2.9 %collective-permute-start.10 = (f32[16,640]{1,0:T(8,128)S(1)}, f32[16,640]{1,0:T(8,128)S(1)}, u32[]{:S(2)}, u32[]{:S(2)}) collective-permute-start(f32[16,640]{1,0:T(8,128)S(1)} %add.1.a_ref._), channel_id=1, source_target_pairs={{16,0},{17,1},{18,2},{19,3},{20,4},{21,5},{22,6},{23,7},{25,9},{24... | collective-permute-start | bytes 122888 | tf_op jit(solution)/shard_map/ppermute | solution.py:56
  23.1 0.9 %collective-permute-start.9 = (f32[16,640]{1,0:T(8,128)S(1)}, f32[16,640]{1,0:T(8,128)S(1)}, u32[]{:S(2)}, u32[]{:S(2)}) collective-permute-start(f32[16,640]{1,0:T(8,128)S(1)} %add.1.a_ref._), channel_id=1, source_target_pairs={{25,0},{24,1},{27,2},{26,3},{29,4},{28,5},{31,6},{30,7},{16,9},{17... | collective-permute-start | bytes 122888 | tf_op jit(solution)/shard_map/ppermute | solution.py:56
  24.0 0.0 collective-permute-start.8
  24.0 0.5 %collective-permute-done.10.d_ref = f32[16,640]{1,0:T(8,128)S(1)} collective-permute-done((f32[16,640]{1,0:T(8,128)S(1)}, f32[16,640]{1,0:T(8,128)S(1)}, u32[]{:S(2)}, u32[]{:S(2)}) %collective-permute-start.10) | collective-permute-done | bytes 40992 | tf_op jit(solution)/shard_map/ppermute | solution.py:56
  24.6 3.2 %collective-permute-done.9.c_ref = f32[16,640]{1,0:T(8,128)S(1)} collective-permute-done((f32[16,640]{1,0:T(8,128)S(1)}, f32[16,640]{1,0:T(8,128)S(1)}, u32[]{:S(2)}, u32[]{:S(2)}) %collective-permute-start.9) | collective-permute-done | bytes 40992 | tf_op jit(solution)/shard_map/ppermute | solution.py:56
  27.8 0.0 collective-permute-done.8.b_ref
  27.8 0.0 collective-permute-done.16.across_ref
  27.8 1.4 %collective-permute-start.17 = (bf16[80,4096]{1,0:T(8,128)(2,1)S(1)}, bf16[80,4096]{1,0:T(8,128)(2,1)S(1)}, u32[]{:S(2)}, u32[]{:S(2)}) collective-permute-start(bf16[80,4096]{1,0:T(8,128)(2,1)S(1)} %both.1), channel_id=1, source_target_pairs={{1,0},{0,1},{3,2},{2,3},{5,4},{4,5},{7,6},{6,7},{8,9},{9,8},{10,11... | collective-permute-start | bytes 1966088 | tf_op jit(solution)/shard_map/ppermute | solution.py:56
  29.2 1.5 %collective-permute-start.13 = (bf16[16,896]{1,0:T(8,128)(2,1)S(1)}, bf16[16,896]{1,0:T(8,128)(2,1)S(1)}, u32[]{:S(2)}, u32[]{:S(2)}) collective-permute-start(bf16[16,896]{1,0:T(8,128)(2,1)S(1)} %total.1.refs_0_._), channel_id=1, source_target_pairs={{5,0},{4,1},{7,2},{6,3},{1,4},{0,5},{3,6},{2,7},{12,9},{13,8},{14,... | collective-permute-start | bytes 86024 | tf_op jit(solution)/shard_map/ppermute | solution.py:56
  30.7 1.3 %collective-permute-start.12 = (bf16[16,896]{1,0:T(8,128)(2,1)S(1)}, bf16[16,896]{1,0:T(8,128)(2,1)S(1)}, u32[]{:S(2)}, u32[]{:S(2)}) collective-permute-start(bf16[16,896]{1,0:T(8,128)(2,1)S(1)} %total.1.refs_0_._), channel_id=1, source_target_pairs={{7,0},{6,1},{5,2},{4,3},{3,4},{2,5},{1,6},{0,7},{14,9},{15,8},{12,... | collective-permute-start | bytes 86024 | tf_op jit(solution)/shard_map/ppermute | solution.py:56
  32.0 0.2 collective-permute-start.11
  32.1 1.9 %collective-permute-done.13.refs_3_ = bf16[16,896]{1,0:T(8,128)(2,1)S(1)} collective-permute-done((bf16[16,896]{1,0:T(8,128)(2,1)S(1)}, bf16[16,896]{1,0:T(8,128)(2,1)S(1)}, u32[]{:S(2)}, u32[]{:S(2)}) %collective-permute-start.13) | collective-permute-done | bytes 28704 | tf_op jit(solution)/shard_map/ppermute | solution.py:56
  34.0 1.2 %collective-permute-done.12.refs_2_ = bf16[16,896]{1,0:T(8,128)(2,1)S(1)} collective-permute-done((bf16[16,896]{1,0:T(8,128)(2,1)S(1)}, bf16[16,896]{1,0:T(8,128)(2,1)S(1)}, u32[]{:S(2)}, u32[]{:S(2)}) %collective-permute-start.12) | collective-permute-done | bytes 28704 | tf_op jit(solution)/shard_map/ppermute | solution.py:56
  35.2 0.0 collective-permute-done.11.refs_1_
  35.3 0.4 %collective-permute-start.14 = (bf16[64,896]{1,0:T(8,128)(2,1)S(1)}, bf16[64,896]{1,0:T(8,128)(2,1)S(1)}, u32[]{:S(2)}, u32[]{:S(2)}) collective-permute-start(bf16[64,896]{1,0:T(8,128)(2,1)S(1)} %collect.1.refs_0_), channel_id=1, source_target_pairs={{1,0},{0,1},{3,2},{2,3},{5,4},{4,5},{7,6},{6,7},{8,9},{9,8},{10,11... | collective-permute-start | bytes 344072 | tf_op jit(solution)/shard_map/ppermute | solution.py:56
  35.7 0.0 collective-permute-done.17.both_ref
  35.7 0.2 order.1.refs_2_
  35.9 0.8 %collective-permute-done.14.refs_1_ = bf16[64,896]{1,0:T(8,128)(2,1)S(1)} collective-permute-done((bf16[64,896]{1,0:T(8,128)(2,1)S(1)}, bf16[64,896]{1,0:T(8,128)(2,1)S(1)}, u32[]{:S(2)}, u32[]{:S(2)}) %collective-permute-start.14) | collective-permute-done | bytes 114720 | tf_op jit(solution)/shard_map/ppermute | solution.py:56
  36.7 3.2 %outputs.1 = (bf16[512,4096]{1,0:T(8,128)(2,1)}, f32[64,4096]{1,0:T(8,128)}) custom-call(bf16[64,896]{1,0:T(8,128)(2,1)S(1)} %collect.1.refs_0_, bf16[64,896]{1,0:T(8,128)(2,1)S(1)} %collective-permute-done.14.refs_1_, bf16[256,4096]{1,0:T(8,128)(2,1)S(1)} %order.1.refs_2_), custom_call_target="tpu_custom_call" | custom-call | flops 603979776 | bytes 7340032 | tf_op jit(solution)/shard_map/outputs/pallas_call | solution.py:362
  (10 shorter events, 0.2 us)
Async XLA Ops:
  0.6 5.2 %copy-start.2 = (bf16[16,4096]{1,0:T(8,128)(2,1)S(1)}, bf16[16,4096]{1,0:T(8,128)(2,1)}, u32[]{:S(2)}) copy-start(bf16[16,4096]{1,0:T(8,128)(2,1)} %temp_ref.1) | copy-start | bytes 393220
  0.6 6.4 %copy-start.1 = (bf16[16,4096]{1,0:T(8,128)(2,1)S(1)}, bf16[16,4096]{1,0:T(8,128)(2,1)}, u32[]{:S(2)}) copy-start(bf16[16,4096]{1,0:T(8,128)(2,1)} %stream_ref.3) | copy-start | bytes 393220
  0.6 6.4 %copy-start = (bf16[512,4096]{1,0:T(8,128)(2,1)S(1)}, bf16[512,4096]{1,0:T(8,128)(2,1)}, u32[]{:S(2)}) copy-start(bf16[512,4096]{1,0:T(8,128)(2,1)} %probe_ref.1) | copy-start | bytes 12582916
  0.7 7.6 %collective-permute-start.3 = (bf16[16,4096]{1,0:T(8,128)(2,1)}, bf16[16,4096]{1,0:T(8,128)(2,1)S(1)}, u32[]{:S(2)}, u32[]{:S(2)}) collective-permute-start(bf16[16,4096]{1,0:T(8,128)(2,1)} %temp_ref.1), channel_id=1, source_target_pairs={{2,0},{3,1},{0,2},{1,3},{6,4},{7,5},{4,6},{5,7},{10,9},{11,8},{8,1... | collective-permute-start | bytes 393224 | tf_op jit(solution)/shard_map/ppermute | solution.py:56
  2.8 6.4 %collective-permute-start.2 = (bf16[16,4096]{1,0:T(8,128)(2,1)}, bf16[16,4096]{1,0:T(8,128)(2,1)S(1)}, u32[]{:S(2)}, u32[]{:S(2)}) collective-permute-start(bf16[16,4096]{1,0:T(8,128)(2,1)} %temp_ref.1), channel_id=1, source_target_pairs={{6,0},{7,1},{4,2},{5,3},{2,4},{3,5},{0,6},{1,7},{14,9},{15,8},{12,... | collective-permute-start | bytes 393224 | tf_op jit(solution)/shard_map/ppermute | solution.py:56
  4.6 2.4 %collective-permute-start = (bf16[16,4096]{1,0:T(8,128)(2,1)}, bf16[16,4096]{1,0:T(8,128)(2,1)S(1)}, u32[]{:S(2)}, u32[]{:S(2)}) collective-permute-start(bf16[16,4096]{1,0:T(8,128)(2,1)} %stream_ref.3), channel_id=1, source_target_pairs={{1,0},{0,1},{3,2},{2,3},{5,4},{4,5},{7,6},{6,7},{8,9},{9,8},{10,11... | collective-permute-start | bytes 393224 | tf_op jit(solution)/shard_map/ppermute | solution.py:56
  5.8 2.8 %collective-permute-start.1 = (bf16[16,4096]{1,0:T(8,128)(2,1)S(1)}, bf16[16,4096]{1,0:T(8,128)(2,1)S(1)}, u32[]{:S(2)}, u32[]{:S(2)}) collective-permute-start(bf16[16,4096]{1,0:T(8,128)(2,1)S(1)} %ahead.1), channel_id=1, source_target_pairs={{1,0},{0,1},{3,2},{2,3},{5,4},{4,5},{7,6},{6,7},{8,9},{9,8},{10,11... | collective-permute-start | bytes 393224 | tf_op jit(solution)/shard_map/ppermute | solution.py:56
  8.2 1.4 %collective-permute-start.4 = (bf16[16,4096]{1,0:T(8,128)(2,1)S(1)}, bf16[16,4096]{1,0:T(8,128)(2,1)S(1)}, u32[]{:S(2)}, u32[]{:S(2)}) collective-permute-start(bf16[16,4096]{1,0:T(8,128)(2,1)S(1)} %near.1._.near_ref), channel_id=1, source_target_pairs={{1,0},{0,1},{3,2},{2,3},{5,4},{4,5},{7,6},{6,7},{8,9},{9,8},{10,11... | collective-permute-start | bytes 393224 | tf_op jit(solution)/shard_map/ppermute | solution.py:56
  8.7 9.8 %collective-permute-start.15 = (bf16[32,4096]{1,0:T(8,128)(2,1)S(1)}, bf16[32,4096]{1,0:T(8,128)(2,1)S(1)}, u32[]{:S(2)}, u32[]{:S(2)}) collective-permute-start(bf16[32,4096]{1,0:T(8,128)(2,1)S(1)} %beside.1), channel_id=1, source_target_pairs={{3,0},{6,1},{1,2},{4,3},{7,4},{2,5},{5,6},{0,7},{10,9},{15,8},{8,1... | collective-permute-start | bytes 786440 | tf_op jit(solution)/shard_map/ppermute | solution.py:56
  10.1 5.0 %collective-permute-start.7 = (f32[16,640]{1,0:T(8,128)S(1)}, f32[16,640]{1,0:T(8,128)S(1)}, u32[]{:S(2)}, u32[]{:S(2)}) collective-permute-start(f32[16,640]{1,0:T(8,128)S(1)} %gram.1.a_ref), channel_id=1, source_target_pairs={{64,0},{65,1},{66,2},{67,3},{68,4},{69,5},{70,6},{71,7},{73,9},{72... | collective-permute-start | bytes 122888 | tf_op jit(solution)/shard_map/ppermute | solution.py:56
  13.7 4.6 %collective-permute-start.6 = (f32[16,640]{1,0:T(8,128)S(1)}, f32[16,640]{1,0:T(8,128)S(1)}, u32[]{:S(2)}, u32[]{:S(2)}) collective-permute-start(f32[16,640]{1,0:T(8,128)S(1)} %gram.1.a_ref), channel_id=1, source_target_pairs={{97,0},{96,1},{99,2},{98,3},{101,4},{100,5},{103,6},{102,7},{104,9... | collective-permute-start | bytes 122888 | tf_op jit(solution)/shard_map/ppermute | solution.py:56
  14.7 3.8 %collective-permute-start.5 = (f32[16,640]{1,0:T(8,128)S(1)}, f32[16,640]{1,0:T(8,128)S(1)}, u32[]{:S(2)}, u32[]{:S(2)}) collective-permute-start(f32[16,640]{1,0:T(8,128)S(1)} %gram.1.a_ref), channel_id=1, source_target_pairs={{33,0},{32,1},{35,2},{34,3},{37,4},{36,5},{39,6},{38,7},{40,9},{41... | collective-permute-start | bytes 122888 | tf_op jit(solution)/shard_map/ppermute | solution.py:56
  18.6 9.2 %collective-permute-start.16 = (bf16[32,4096]{1,0:T(8,128)(2,1)S(1)}, bf16[32,4096]{1,0:T(8,128)(2,1)S(1)}, u32[]{:S(2)}, u32[]{:S(2)}) collective-permute-start(bf16[32,4096]{1,0:T(8,128)(2,1)S(1)} %relay.1), channel_id=1, source_target_pairs={{3,0},{6,1},{1,2},{4,3},{7,4},{2,5},{5,6},{0,7},{10,9},{15,8},{8,1... | collective-permute-start | bytes 786440 | tf_op jit(solution)/shard_map/ppermute | solution.py:56
  20.2 4.4 %collective-permute-start.10 = (f32[16,640]{1,0:T(8,128)S(1)}, f32[16,640]{1,0:T(8,128)S(1)}, u32[]{:S(2)}, u32[]{:S(2)}) collective-permute-start(f32[16,640]{1,0:T(8,128)S(1)} %add.1.a_ref._), channel_id=1, source_target_pairs={{16,0},{17,1},{18,2},{19,3},{20,4},{21,5},{22,6},{23,7},{25,9},{24... | collective-permute-start | bytes 122888 | tf_op jit(solution)/shard_map/ppermute | solution.py:56
  23.1 4.6 %collective-permute-start.9 = (f32[16,640]{1,0:T(8,128)S(1)}, f32[16,640]{1,0:T(8,128)S(1)}, u32[]{:S(2)}, u32[]{:S(2)}) collective-permute-start(f32[16,640]{1,0:T(8,128)S(1)} %add.1.a_ref._), channel_id=1, source_target_pairs={{25,0},{24,1},{27,2},{26,3},{29,4},{28,5},{31,6},{30,7},{16,9},{17... | collective-permute-start | bytes 122888 | tf_op jit(solution)/shard_map/ppermute | solution.py:56
  24.0 3.7 %collective-permute-start.8 = (f32[16,640]{1,0:T(8,128)S(1)}, f32[16,640]{1,0:T(8,128)S(1)}, u32[]{:S(2)}, u32[]{:S(2)}) collective-permute-start(f32[16,640]{1,0:T(8,128)S(1)} %add.1.a_ref._), channel_id=1, source_target_pairs={{9,0},{8,1},{11,2},{10,3},{13,4},{12,5},{15,6},{14,7},{0,9},{1,8},... | collective-permute-start | bytes 122888 | tf_op jit(solution)/shard_map/ppermute | solution.py:56
  27.8 7.9 %collective-permute-start.17 = (bf16[80,4096]{1,0:T(8,128)(2,1)S(1)}, bf16[80,4096]{1,0:T(8,128)(2,1)S(1)}, u32[]{:S(2)}, u32[]{:S(2)}) collective-permute-start(bf16[80,4096]{1,0:T(8,128)(2,1)S(1)} %both.1), channel_id=1, source_target_pairs={{1,0},{0,1},{3,2},{2,3},{5,4},{4,5},{7,6},{6,7},{8,9},{9,8},{10,11... | collective-permute-start | bytes 1966088 | tf_op jit(solution)/shard_map/ppermute | solution.py:56
  29.2 4.8 %collective-permute-start.13 = (bf16[16,896]{1,0:T(8,128)(2,1)S(1)}, bf16[16,896]{1,0:T(8,128)(2,1)S(1)}, u32[]{:S(2)}, u32[]{:S(2)}) collective-permute-start(bf16[16,896]{1,0:T(8,128)(2,1)S(1)} %total.1.refs_0_._), channel_id=1, source_target_pairs={{5,0},{4,1},{7,2},{6,3},{1,4},{0,5},{3,6},{2,7},{12,9},{13,8},{14,... | collective-permute-start | bytes 86024 | tf_op jit(solution)/shard_map/ppermute | solution.py:56
  30.7 4.5 %collective-permute-start.12 = (bf16[16,896]{1,0:T(8,128)(2,1)S(1)}, bf16[16,896]{1,0:T(8,128)(2,1)S(1)}, u32[]{:S(2)}, u32[]{:S(2)}) collective-permute-start(bf16[16,896]{1,0:T(8,128)(2,1)S(1)} %total.1.refs_0_._), channel_id=1, source_target_pairs={{7,0},{6,1},{5,2},{4,3},{3,4},{2,5},{1,6},{0,7},{14,9},{15,8},{12,... | collective-permute-start | bytes 86024 | tf_op jit(solution)/shard_map/ppermute | solution.py:56
  32.0 3.3 %collective-permute-start.11 = (bf16[16,896]{1,0:T(8,128)(2,1)S(1)}, bf16[16,896]{1,0:T(8,128)(2,1)S(1)}, u32[]{:S(2)}, u32[]{:S(2)}) collective-permute-start(bf16[16,896]{1,0:T(8,128)(2,1)S(1)} %total.1.refs_0_._), channel_id=1, source_target_pairs={{3,0},{2,1},{1,2},{0,3},{7,4},{6,5},{5,6},{4,7},{10,9},{11,8},{8,1... | collective-permute-start | bytes 86024 | tf_op jit(solution)/shard_map/ppermute | solution.py:56
  35.3 1.4 %collective-permute-start.14 = (bf16[64,896]{1,0:T(8,128)(2,1)S(1)}, bf16[64,896]{1,0:T(8,128)(2,1)S(1)}, u32[]{:S(2)}, u32[]{:S(2)}) collective-permute-start(bf16[64,896]{1,0:T(8,128)(2,1)S(1)} %collect.1.refs_0_), channel_id=1, source_target_pairs={{1,0},{0,1},{3,2},{2,3},{5,4},{4,5},{7,6},{6,7},{8,9},{9,8},{10,11... | collective-permute-start | bytes 344072 | tf_op jit(solution)/shard_map/ppermute | solution.py:56
